TPU v7x, 32 devices: a whole 2x2x4 slice. The times are simulated.
32 devices in a mesh: fsdp: 8 (over z, y), rep: 4 (over x, core).
Axes of the slice: x: 2, y: 2, z: 4, core: 2. Of those that a mesh axis runs over, the one named last changes fastest.
Arguments:
- tokens_in: bfloat16 [4096, 2048], P(('fsdp', 'rep')), may hold values from -6 to 6
- segment_ids: int32 [64, 64], P(('fsdp', 'rep')), may hold values from 0 to 2, never falling along the last dimension, each value on 1 to 48 neighbouring positions
- w_query: bfloat16 [2048, 2048], P('fsdp'), may hold values from -0.125 to 0.125
- w_key: bfloat16 [2048, 512], P('fsdp'), may hold values from -0.125 to 0.125
- w_value: bfloat16 [2048, 512], P('fsdp'), may hold values from -0.125 to 0.125
- w_out: bfloat16 [2048, 2048], P('fsdp'), may hold values from -0.375 to 0.375
- w_gate: bfloat16 [2048, 8192], P('fsdp'), may hold values from -0.125 to 0.125
- w_up: bfloat16 [2048, 8192], P('fsdp'), may hold values from -0.125 to 0.125
- w_down: bfloat16 [8192, 2048], P('fsdp'), may hold values from -0.09375 to 0.09375
- gain_attn: bfloat16 [2048], P('fsdp'), may hold values from 0.5 to 1.5
- gain_ffn: bfloat16 [2048], P('fsdp'), may hold values from 0.5 to 1.5
- gain_query: bfloat16 [64], replicated, may hold values from 0.25 to 1.75
- gain_key: bfloat16 [64], replicated, may hold values from 0.25 to 1.75
- d_out: bfloat16 [4096, 2048], P(('fsdp', 'rep')), may hold values from -6 to 6
Outputs:
- block_out: bfloat16 [4096, 2048], P(('fsdp', 'rep'))
- d_tokens: bfloat16 [4096, 2048], P(('fsdp', 'rep'))
- grad_w_query: float32 [2048, 2048], P('fsdp')
- grad_w_key: float32 [2048, 512], P('fsdp')
- grad_w_value: float32 [2048, 512], P('fsdp')
- grad_w_out: float32 [2048, 2048], P('fsdp')
- grad_w_gate: float32 [2048, 8192], P('fsdp')
- grad_w_up: float32 [2048, 8192], P('fsdp')
- grad_w_down: float32 [8192, 2048], P('fsdp')
- grad_gain_attn: float32 [2048], P('fsdp')
- grad_gain_ffn: float32 [2048], P('fsdp')
- grad_gain_query: float32 [64], replicated
- grad_gain_key: float32 [64], replicated
- rms_stats: float32 [5], replicated
All inputs are finite; a program needn't handle non-finite values.
Results may differ from a plain program's by a relative error of at most 0.02.
Values may be sent and summed in bfloat16 or wider, within the bound.
No kernel may reach another device: no remote copies, remote signals or barrier semaphores. Data moves between devices by JAX's collectives and lax.ppermute only.
A program may use at most 448 MiB of HBM per device.

v0:
```python
import math

import jax
import jax.numpy as jnp
from jax import lax
from jax.sharding import PartitionSpec as P

D = 2048
HD = 64
MICRO = 2


EPS = 1e-05
THETA = 1000000.0
NEG = -1e30


def norm_rows(values, gain):
    return values * lax.rsqrt(jnp.mean(values * values, axis=-1, keepdims=True) + EPS) * gain


def rotate(values, cosine, sine):
    half_dim = values.shape[-1] // 2
    first_half = values[..., :half_dim]
    second_half = values[..., half_dim:]
    return jnp.concatenate(
        [first_half * cosine - second_half * sine, second_half * cosine + first_half * sine],
        axis=-1,
    )


def angles(seg_row):
    token_index = jnp.arange(seg_row.shape[0])
    earlier = (seg_row[:, None] == seg_row[None, :]) & (token_index[None, :] < token_index[:, None])
    position = jnp.sum(earlier.astype(jnp.int32), axis=1)
    half_dim = HD // 2
    frequency = jnp.exp(jnp.arange(half_dim).astype(jnp.float32) * (-2.0 * math.log(THETA) / HD))
    phase = position.astype(jnp.float32)[:, None] * frequency[None, :]
    return (jnp.cos(phase)[:, None, :], jnp.sin(phase)[:, None, :])


def allowed_pairs(seg_row):
    token_index = jnp.arange(seg_row.shape[0])
    return (seg_row[:, None] == seg_row[None, :]) & (token_index[None, :] <= token_index[:, None])


def softmax_rows(scores, allowed):
    masked = jnp.where(allowed, scores, NEG)
    row_max = jnp.max(masked, axis=-1, keepdims=True)
    exponent = jnp.exp(masked - row_max)
    return exponent / jnp.sum(exponent, axis=-1, keepdims=True)


def swiglu(gate_in, up_in):
    return gate_in * jax.nn.sigmoid(gate_in) * up_in


def matmul(left, right):
    return jnp.dot(left, right, preferred_element_type=jnp.float32)


def left_tmul(left, right):
    return jnp.einsum("tc,tq->cq", left, right, preferred_element_type=jnp.float32)


def right_tmul(left, right):
    return jnp.einsum("tq,cq->tc", left, right, preferred_element_type=jnp.float32)


def local(
    tokens_in,
    segment_ids,
    w_query,
    w_key,
    w_value,
    w_out,
    w_gate,
    w_up,
    w_down,
    gain_attn,
    gain_ffn,
    gain_query,
    gain_key,
    d_out,
):
    row_count = tokens_in.shape[0] // MICRO
    head_count = w_query.shape[1] // HD
    kv_count = w_key.shape[1] // HD
    group_size = head_count // kv_count
    score_scale = HD ** (-0.5)
    query_gain_f = gain_query.astype(jnp.float32)
    key_gain_f = gain_key.astype(jnp.float32)
    acc_glu = tuple((jnp.zeros(item.shape, jnp.float32) for item in (w_gate, w_up, gain_ffn)))
    acc_attn = tuple(
        (jnp.zeros(item.shape, jnp.float32) for item in (w_query, w_key, w_value, w_out, gain_attn))
    )
    ffn_gain_local = jnp.zeros((gain_ffn.shape[0] * lax.axis_size("fsdp"),), jnp.float32)
    attn_gain_local = jnp.zeros((gain_attn.shape[0] * lax.axis_size("fsdp"),), jnp.float32)
    kept_rows = []
    squares = jnp.zeros((5,), jnp.float32)
    query_gain_sum = jnp.zeros((HD,), jnp.float32)
    key_gain_sum = jnp.zeros((HD,), jnp.float32)
    out_parts = []
    grad_parts = []
    for micro_step in range(MICRO):
        first_row = micro_step * row_count
        tokens_f = tokens_in[first_row : first_row + row_count].astype(jnp.float32)
        upstream = d_out[first_row : first_row + row_count].astype(jnp.float32)
        seg_row = segment_ids[micro_step]
        cosine, sine = angles(seg_row)
        allowed = allowed_pairs(seg_row)
        full_query, full_key, full_value, full_out, full_gain_attn = (
            lax.all_gather(w_query, "fsdp", axis=0, tiled=True),
            lax.all_gather(w_key, "fsdp", axis=0, tiled=True),
            lax.all_gather(w_value, "fsdp", axis=0, tiled=True),
            lax.all_gather(w_out, "fsdp", axis=0, tiled=True),
            lax.all_gather(gain_attn, "fsdp", axis=0, tiled=True),
        )
        full_gate, full_up, full_down, full_gain_ffn = (
            lax.all_gather(w_gate, "fsdp", axis=0, tiled=True),
            lax.all_gather(w_up, "fsdp", axis=0, tiled=True),
            lax.all_gather(w_down, "fsdp", axis=0, tiled=True),
            lax.all_gather(gain_ffn, "fsdp", axis=0, tiled=True),
        )
        attn_norm, attn_norm_pull = jax.vjp(norm_rows, tokens_f, full_gain_attn.astype(jnp.float32))
        attn_in = attn_norm.astype(jnp.bfloat16)
        query_raw = matmul(attn_in, full_query)
        key_raw = matmul(attn_in, full_key)
        value_low = matmul(attn_in, full_value).astype(jnp.bfloat16)
        value_heads = value_low.reshape(row_count, kv_count, HD)

        def prep_query(raw, gain):
            return rotate(norm_rows(raw.reshape(row_count, head_count, HD), gain), cosine, sine)

        def prep_key(raw, gain):
            return rotate(norm_rows(raw.reshape(row_count, kv_count, HD), gain), cosine, sine)

        query_f, query_pull = jax.vjp(prep_query, query_raw, query_gain_f)
        key_f, key_pull = jax.vjp(prep_key, key_raw, key_gain_f)
        query_heads = query_f.astype(jnp.bfloat16).reshape(row_count, kv_count, group_size, HD)
        key_heads = key_f.astype(jnp.bfloat16)
        scores = (
            jnp.einsum("ikgd,jkd->kgij", query_heads, key_heads, preferred_element_type=jnp.float32)
            * score_scale
        )
        attn_probs, soft_pull = jax.vjp(lambda values: softmax_rows(values, allowed), scores)
        probs_low = attn_probs.astype(jnp.bfloat16)
        mixed_f = jnp.einsum(
            "kgij,jkd->ikgd", probs_low, value_heads, preferred_element_type=jnp.float32
        )
        mixed = mixed_f.reshape(row_count, head_count * HD).astype(jnp.bfloat16)
        attn_branch = matmul(mixed, full_out)
        middle = tokens_f + attn_branch
        ffn_norm, ffn_norm_pull = jax.vjp(norm_rows, middle, full_gain_ffn.astype(jnp.float32))
        ffn_in = ffn_norm.astype(jnp.bfloat16)
        gate_all = matmul(ffn_in, full_gate)
        up_all = matmul(ffn_in, full_up)
        hidden_f, glu_pull = jax.vjp(swiglu, gate_all, up_all)
        hidden = hidden_f.astype(jnp.bfloat16)
        ffn_branch = matmul(hidden, full_down)
        block_f = middle + ffn_branch
        back_gate, back_up, back_down = (
            lax.all_gather(w_gate, "fsdp", axis=0, tiled=True),
            lax.all_gather(w_up, "fsdp", axis=0, tiled=True),
            lax.all_gather(w_down, "fsdp", axis=0, tiled=True),
        )
        g_ffn = upstream.astype(jnp.bfloat16)
        g_hidden = right_tmul(g_ffn, back_down).astype(jnp.bfloat16)
        g_gate_f, g_up_f = glu_pull(g_hidden.astype(jnp.float32))
        g_gate = g_gate_f.astype(jnp.bfloat16)
        g_up = g_up_f.astype(jnp.bfloat16)
        g_ffn_in = right_tmul(g_gate, back_gate) + right_tmul(g_up, back_up)
        g_middle_norm, grad_gain_ffn_local = ffn_norm_pull(g_ffn_in)
        ffn_gain_local = ffn_gain_local + grad_gain_ffn_local
        g_middle = upstream + g_middle_norm
        back_query, back_key, back_value, back_out = (
            lax.all_gather(w_query, "fsdp", axis=0, tiled=True),
            lax.all_gather(w_key, "fsdp", axis=0, tiled=True),
            lax.all_gather(w_value, "fsdp", axis=0, tiled=True),
            lax.all_gather(w_out, "fsdp", axis=0, tiled=True),
        )
        g_attn = g_middle.astype(jnp.bfloat16)
        g_mixed = (
            right_tmul(g_attn, back_out)
            .astype(jnp.bfloat16)
            .reshape(row_count, kv_count, group_size, HD)
        )
        g_probs = jnp.einsum(
            "ikgd,jkd->kgij", g_mixed, value_heads, preferred_element_type=jnp.float32
        )
        g_value = jnp.einsum(
            "kgij,ikgd->jkd", probs_low, g_mixed, preferred_element_type=jnp.float32
        )
        g_value = g_value.reshape(row_count, kv_count * HD).astype(jnp.bfloat16)
        g_scores = soft_pull(g_probs)[0].astype(jnp.bfloat16)
        g_query = (
            jnp.einsum("kgij,jkd->ikgd", g_scores, key_heads, preferred_element_type=jnp.float32)
            * score_scale
        )
        g_key = (
            jnp.einsum("kgij,ikgd->jkd", g_scores, query_heads, preferred_element_type=jnp.float32)
            * score_scale
        )
        g_query_raw_f, grad_gain_query_local = query_pull(
            g_query.reshape(row_count, head_count, HD)
        )
        g_key_raw_f, grad_gain_key_local = key_pull(g_key)
        g_query_raw = g_query_raw_f.astype(jnp.bfloat16)
        g_key_raw = g_key_raw_f.astype(jnp.bfloat16)
        g_attn_in = (
            right_tmul(g_query_raw, back_query)
            + right_tmul(g_key_raw, back_key)
            + right_tmul(g_value, back_value)
        )
        g_tokens_norm, grad_gain_attn_local = attn_norm_pull(g_attn_in)
        attn_gain_local = attn_gain_local + grad_gain_attn_local
        kept_rows.append(
            (
                hidden,
                g_ffn,
                ffn_in,
                g_gate,
                g_up,
                attn_in,
                g_query_raw,
                g_key_raw,
                g_value,
                mixed,
                g_attn,
            )
        )
        d_tokens_f = g_middle + g_tokens_norm
        query_gain_sum = query_gain_sum + grad_gain_query_local
        key_gain_sum = key_gain_sum + grad_gain_key_local
        squares = squares + jnp.stack(
            [
                jnp.sum(middle * middle),
                jnp.sum(attn_branch * attn_branch),
                jnp.sum(ffn_branch * ffn_branch),
                jnp.sum(block_f * block_f),
                jnp.sum(d_tokens_f * d_tokens_f),
            ]
        )
        out_parts.append(block_f.astype(jnp.bfloat16))
        grad_parts.append(d_tokens_f.astype(jnp.bfloat16))
    joined = [jnp.concatenate([kept[index] for kept in kept_rows], axis=0) for index in range(11)]
    (
        hidden_all,
        g_ffn_all,
        ffn_in_all,
        g_gate_all,
        g_up_all,
        attn_in_all,
        g_query_all,
        g_key_all,
        g_value_all,
        mixed_all,
        g_attn_all,
    ) = joined
    acc_down = lax.psum_scatter(
        left_tmul(hidden_all, g_ffn_all).astype(jnp.bfloat16),
        "fsdp",
        scatter_dimension=0,
        tiled=True,
    )
    acc_glu = (
        lax.psum_scatter(
            left_tmul(ffn_in_all, g_gate_all).astype(jnp.bfloat16),
            "fsdp",
            scatter_dimension=0,
            tiled=True,
        ).astype(jnp.float32),
        lax.psum_scatter(
            left_tmul(ffn_in_all, g_up_all).astype(jnp.bfloat16),
            "fsdp",
            scatter_dimension=0,
            tiled=True,
        ).astype(jnp.float32),
        lax.psum_scatter(
            ffn_gain_local.astype(jnp.bfloat16), "fsdp", scatter_dimension=0, tiled=True
        ).astype(jnp.float32),
    )
    acc_attn = (
        lax.psum_scatter(
            left_tmul(attn_in_all, g_query_all).astype(jnp.bfloat16),
            "fsdp",
            scatter_dimension=0,
            tiled=True,
        ).astype(jnp.float32),
        lax.psum_scatter(
            left_tmul(attn_in_all, g_key_all).astype(jnp.bfloat16),
            "fsdp",
            scatter_dimension=0,
            tiled=True,
        ).astype(jnp.float32),
        lax.psum_scatter(
            left_tmul(attn_in_all, g_value_all).astype(jnp.bfloat16),
            "fsdp",
            scatter_dimension=0,
            tiled=True,
        ).astype(jnp.float32),
        lax.psum_scatter(
            left_tmul(mixed_all, g_attn_all).astype(jnp.bfloat16),
            "fsdp",
            scatter_dimension=0,
            tiled=True,
        ).astype(jnp.float32),
        lax.psum_scatter(
            attn_gain_local.astype(jnp.bfloat16), "fsdp", scatter_dimension=0, tiled=True
        ).astype(jnp.float32),
    )
    summed = (
        lax.psum(acc_attn[0].astype(jnp.bfloat16), "rep").astype(jnp.float32),
        lax.psum(acc_attn[1].astype(jnp.bfloat16), "rep").astype(jnp.float32),
        lax.psum(acc_attn[2].astype(jnp.bfloat16), "rep").astype(jnp.float32),
        lax.psum(acc_attn[3].astype(jnp.bfloat16), "rep").astype(jnp.float32),
        lax.psum(acc_glu[0].astype(jnp.bfloat16), "rep").astype(jnp.float32),
        lax.psum(acc_glu[1].astype(jnp.bfloat16), "rep").astype(jnp.float32),
        lax.psum(acc_down, "rep").astype(jnp.float32),
        lax.psum(acc_attn[4].astype(jnp.bfloat16), "rep").astype(jnp.float32),
        lax.psum(acc_glu[2].astype(jnp.bfloat16), "rep").astype(jnp.float32),
    )
    totals = lax.psum((squares, query_gain_sum, key_gain_sum), ("fsdp", "rep"))
    entry_total = row_count * MICRO * lax.axis_size("fsdp") * lax.axis_size("rep") * D
    stats = jnp.sqrt(totals[0] / entry_total)
    block_out = jnp.concatenate(out_parts, axis=0)
    d_tokens = jnp.concatenate(grad_parts, axis=0)
    return (
        block_out,
        d_tokens,
        summed[0],
        summed[1],
        summed[2],
        summed[3],
        summed[4],
        summed[5],
        summed[6],
        summed[7],
        summed[8],
        totals[1],
        totals[2],
        stats,
    )


def solution(mesh):
    placed = (
        P(("fsdp", "rep"), None),
        P(("fsdp", "rep"), None),
        P("fsdp", None),
        P("fsdp", None),
        P("fsdp", None),
        P("fsdp", None),
        P("fsdp", None),
        P("fsdp", None),
        P("fsdp", None),
        P("fsdp"),
        P("fsdp"),
        P(),
        P(),
        P(("fsdp", "rep"), None),
    )
    return jax.shard_map(
        local,
        mesh=mesh,
        in_specs=placed,
        out_specs=(
            P(("fsdp", "rep"), None),
            P(("fsdp", "rep"), None),
            P("fsdp", None),
            P("fsdp", None),
            P("fsdp", None),
            P("fsdp", None),
            P("fsdp", None),
            P("fsdp", None),
            P("fsdp", None),
            P("fsdp"),
            P("fsdp"),
            P(),
            P(),
            P(),
        ),
        check_vma=False,
    )
```

profile of v0, /device:TPU:0, one launch (start us, length us, event | category | flops | bytes accessed | tf_op | source)
XLA Modules:
  0.0 4819.3 jit_solution(16328634590431689538)
XLA Ops:
  12.0 22.4 all-gather
  35.3 16.4 all-gather.1
  67.1 45.1 all-gather.10.cloned.1.call-done
  117.7 120.1 %all-gather.14.cloned.1.call-done = bf16[2048,2048]{1,0:T(8,128)(2,1)} async-done(((bf16[256,2048]{1,0:T(8,128)(2,1)}), bf16[2048,2048]{1,0:T(8,128)(2,1)}) %all-gather.14.cloned.1.call-update) | async-done | bytes 8388624 | tf_op jit(solution)/shard_map/all_gather | solution.py:113
  261.8 101.1 %all-gather.16.cloned.1.call-done = bf16[2048,2048]{1,0:T(8,128)(2,1)} async-done(((bf16[256,2048]{1,0:T(8,128)(2,1)}), bf16[2048,2048]{1,0:T(8,128)(2,1)}) %all-gather.16.cloned.1.call-update) | async-done | bytes 8388624 | tf_op jit(solution)/shard_map/all_gather | solution.py:116
  372.0 628.2 %all-gather.18.cloned.1.call-done = bf16[2048,8192]{1,0:T(8,128)(2,1)} async-done(((bf16[256,8192]{1,0:T(8,128)(2,1)}), bf16[2048,8192]{1,0:T(8,128)(2,1)}) %all-gather.18.cloned.1.call-update) | async-done | bytes 33554448 | tf_op jit(solution)/shard_map/all_gather | solution.py:120
  1000.2 15.9 fusion.111
  1016.1 623.2 %all-gather.20.cloned.1.call-done = bf16[2048,8192]{1,0:T(8,128)(2,1)} async-done(((bf16[256,8192]{1,0:T(8,128)(2,1)}), bf16[2048,8192]{1,0:T(8,128)(2,1)}) %all-gather.20.cloned.1.call-update) | async-done | bytes 33554448 | tf_op jit(solution)/shard_map/all_gather | solution.py:121
  1639.4 16.1 fusion.112
  1685.2 593.4 %all-gather.22.cloned.1.call-done = bf16[8192,2048]{1,0:T(8,128)(2,1)} async-done(((bf16[1024,2048]{1,0:T(8,128)(2,1)}), bf16[8192,2048]{1,0:T(8,128)(2,1)}) %all-gather.22.cloned.1.call-update) | async-done | bytes 33554448 | tf_op jit(solution)/shard_map/all_gather | solution.py:122
  2278.6 17.1 multiply_convert_fusion
  2296.7 16.2 fusion.115
  2312.9 17.7 multiply_convert_fusion.1
  2375.7 16.1 convolution_add_fusion.5
  2391.8 18.5 multiply_reduce_fusion.9
  2530.2 47.8 reduce-scatter.12.cloned.1.call-done
  2578.0 152.1 %reduce-scatter.8.cloned.1.call-done = bf16[256,2048]{1,0:T(8,128)(2,1)} async-done(((bf16[2048,2048]{1,0:T(8,128)(2,1)}), bf16[256,2048]{1,0:T(8,128)(2,1)}) %reduce-scatter.8.cloned.1.call-update) | async-done | bytes 1048592 | tf_op jit(solution)/shard_map/reduce_scatter | solution.py:284
  2730.2 152.7 %reduce-scatter.14.cloned.1.call-done = bf16[256,2048]{1,0:T(8,128)(2,1)} async-done(((bf16[2048,2048]{1,0:T(8,128)(2,1)}), bf16[256,2048]{1,0:T(8,128)(2,1)}) %reduce-scatter.14.cloned.1.call-update) | async-done | bytes 1048592 | tf_op jit(solution)/shard_map/reduce_scatter | solution.py:302
  2882.8 546.0 %reduce-scatter.16.cloned.1.call-done = bf16[256,8192]{1,0:T(8,128)(2,1)} async-done(((bf16[2048,8192]{1,0:T(8,128)(2,1)}), bf16[256,8192]{1,0:T(8,128)(2,1)}) %reduce-scatter.16.cloned.1.call-update) | async-done | bytes 4194320 | tf_op jit(solution)/shard_map/reduce_scatter | solution.py:267
  3428.8 546.0 %reduce-scatter.18.cloned.1.call-done = bf16[256,8192]{1,0:T(8,128)(2,1)} async-done(((bf16[2048,8192]{1,0:T(8,128)(2,1)}), bf16[256,8192]{1,0:T(8,128)(2,1)}) %reduce-scatter.18.cloned.1.call-update) | async-done | bytes 4194320 | tf_op jit(solution)/shard_map/reduce_scatter | solution.py:273
  3974.8 545.9 %reduce-scatter.20.cloned.1.call-done = bf16[1024,2048]{1,0:T(8,128)(2,1)} async-done(((bf16[8192,2048]{1,0:T(8,128)(2,1)}), bf16[1024,2048]{1,0:T(8,128)(2,1)}) %reduce-scatter.20.cloned.1.call-update) | async-done | bytes 4194320 | tf_op jit(solution)/shard_map/reduce_scatter | solution.py:260
  4540.0 21.2 all-reduce.11
  4582.3 38.5 all-reduce.10
  4624.9 164.8 %all-reduce.16.cloned.1.call-done = (bf16[256,2048]{1,0:T(8,128)(2,1)}, bf16[256,512]{1,0:T(8,128)(2,1)}, bf16[256,512]{1,0:T(8,128)(2,1)}, bf16[256,2048]{1,0:T...) async-done(((bf16[256,2048]{1,0:T(8,128)(2,1)}, bf16[256,512]{1,0:T(8,128)(2,1)}, bf16[256,512]{1,0:T(8,128)(2,1)}, ...) | async-done | bytes 15204368 | tf_op jit(solution)/shard_map/psum | solution.py:313
  (516 shorter events, 319.3 us)
Async XLA Ops:
  7.2 55.1 %all-gather.12.cloned.1.call-start = ((), (), s32[]{:S(2)}) async-start(), calls=%async_computation.8 | async-start | bytes 2359296 | tf_op jit(solution)/shard_map/all_gather | solution.py:114
  7.9 104.3 %all-gather.10.cloned.1.call-start = ((), (), s32[]{:S(2)}) async-start(), calls=%async_computation.7 | async-start | bytes 2359296 | tf_op jit(solution)/shard_map/all_gather | solution.py:115
  8.7 229.1 %all-gather.14.cloned.1.call-start = ((), (), s32[]{:S(2)}) async-start(), calls=%async_computation.9 | async-start | bytes 9437184 | tf_op jit(solution)/shard_map/all_gather | solution.py:113
  9.4 353.5 %all-gather.16.cloned.1.call-start = ((), (), s32[]{:S(2)}) async-start(), calls=%async_computation.10 | async-start | bytes 9437184 | tf_op jit(solution)/shard_map/all_gather | solution.py:116
  10.0 990.3 %all-gather.18.cloned.1.call-start = ((), (), s32[]{:S(2)}) async-start(), calls=%async_computation.11 | async-start | bytes 37748736 | tf_op jit(solution)/shard_map/all_gather | solution.py:120
  10.6 1628.7 %all-gather.20.cloned.1.call-start = ((), (), s32[]{:S(2)}) async-start(), calls=%async_computation.12 | async-start | bytes 37748736 | tf_op jit(solution)/shard_map/all_gather | solution.py:121
  11.2 2267.4 %all-gather.22.cloned.1.call-start = ((), (), s32[]{:S(2)}) async-start(), calls=%async_computation.13 | async-start | bytes 37748736 | tf_op jit(solution)/shard_map/all_gather | solution.py:122
  11.9 2518.3 %reduce-scatter.10.cloned.1.call-start = ((), (), s32[]{:S(2)}) async-start(), calls=%async_computation.15 | async-start | bytes 2359296 | tf_op jit(solution)/shard_map/reduce_scatter | solution.py:290
  51.7 2358.7 %copy-start.119 = (f32[8,1,256]{2,1,0:T(1,128)}, f32[8,1,256]{2,1,0:T(1,128)S(1)}, u32[]{:S(2)}) copy-start(f32[8,1,256]{2,1,0:T(1,128)S(1)} %convert_element_type.366) | copy-start | bytes 24580
  52.6 202.0 %copy-start.130 = (pred[64,64]{0,1:T(8,128)(4,1)}, pred[64,64]{0,1:T(8,128)(4,1)S(1)}, u32[]{:S(2)}) copy-start(pred[64,64]{0,1:T(8,128)(4,1)S(1)} %compare_and_fusion.3) | copy-start | bytes 12292
  53.6 199.0 %copy-start.91 = (f32[64,32]{1,0:T(8,128)}, f32[64,32]{1,0:T(8,128)S(1)}, u32[]{:S(2)}) copy-start(f32[64,32]{1,0:T(8,128)S(1)} %get-tuple-element.120) | copy-start | bytes 24580
  53.6 199.0 %copy-start.94 = (f32[64,32]{1,0:T(8,128)}, f32[64,32]{1,0:T(8,128)S(1)}, u32[]{:S(2)}) copy-start(f32[64,32]{1,0:T(8,128)S(1)} %get-tuple-element.121) | copy-start | bytes 24580
  53.6 200.0 %copy-start.97 = (f32[64,32]{1,0:T(8,128)}, f32[64,32]{1,0:T(8,128)S(1)}, u32[]{:S(2)}) copy-start(f32[64,32]{1,0:T(8,128)S(1)} %get-tuple-element.136) | copy-start | bytes 24580
  53.7 200.0 %copy-start.100 = (f32[64,32]{1,0:T(8,128)}, f32[64,32]{1,0:T(8,128)S(1)}, u32[]{:S(2)}) copy-start(f32[64,32]{1,0:T(8,128)S(1)} %get-tuple-element.137) | copy-start | bytes 24580
  371.1 2039.2 %copy-start.147 = (f32[64]{0:T(128)}, f32[64]{0:T(128)S(1)}, u32[]{:S(2)}) copy-start(f32[64]{0:T(128)S(1)} %fusion.77) | copy-start | bytes 772
  371.2 2039.2 %copy-start.146 = (f32[64]{0:T(128)}, f32[64]{0:T(128)S(1)}, u32[]{:S(2)}) copy-start(f32[64]{0:T(128)S(1)} %fusion.79) | copy-start | bytes 772
  372.0 1267.4 %copy-start.44 = (bf16[64,2048]{1,0:T(8,128)(2,1)}, bf16[64,2048]{1,0:T(8,128)(2,1)S(1)}, u32[]{:S(2)}) copy-start(bf16[64,2048]{1,0:T(8,128)(2,1)S(1)} %get-tuple-element.119) | copy-start | bytes 786436
  2439.6 138.4 %reduce-scatter.12.cloned.1.call-start = ((), (), s32[]{:S(2)}) async-start(), calls=%async_computation.16 | async-start | bytes 2359296 | tf_op jit(solution)/shard_map/reduce_scatter | solution.py:296
  2445.0 285.2 %reduce-scatter.8.cloned.1.call-start = ((), (), s32[]{:S(2)}) async-start(), calls=%async_computation.14 | async-start | bytes 9437184 | tf_op jit(solution)/shard_map/reduce_scatter | solution.py:284
  2473.9 409.0 %reduce-scatter.14.cloned.1.call-start = ((), (), s32[]{:S(2)}) async-start(), calls=%async_computation.17 | async-start | bytes 9437184 | tf_op jit(solution)/shard_map/reduce_scatter | solution.py:302
  2481.0 947.9 %reduce-scatter.16.cloned.1.call-start = ((), (), s32[]{:S(2)}) async-start(), calls=%async_computation.18 | async-start | bytes 37748736 | tf_op jit(solution)/shard_map/reduce_scatter | solution.py:267
  2497.1 1477.7 %reduce-scatter.18.cloned.1.call-start = ((), (), s32[]{:S(2)}) async-start(), calls=%async_computation.19 | async-start | bytes 37748736 | tf_op jit(solution)/shard_map/reduce_scatter | solution.py:273
  2513.3 2007.4 %reduce-scatter.20.cloned.1.call-start = ((), (), s32[]{:S(2)}) async-start(), calls=%async_computation.20 | async-start | bytes 37748736 | tf_op jit(solution)/shard_map/reduce_scatter | solution.py:260
  2530.2 2259.5 %all-reduce.16.cloned.1.call-start = ((), (), s32[]{:S(2)}) async-start(), calls=%async_computation.21 | async-start | bytes 30408704 | tf_op jit(solution)/shard_map/psum | solution.py:313
  (156 other events, 3271.4 us)
Sparse Core Ops, SparseCore 0:
  10.1 52.0 all-gather.11
  64.4 47.7 all-gather.9
  114.3 123.4 all-gather.13
  239.8 123.1 all-gather.15
  364.3 635.8 all-gather.17
  1001.6 637.6 all-gather.19
  1640.9 637.6 all-gather.21
  2439.7 67.5 reduce-scatter.9
  2511.4 66.5 reduce-scatter.11
  2582.1 148.0 reduce-scatter.7
  2734.8 147.9 reduce-scatter.13
  2886.4 542.3 reduce-scatter.15
  3432.6 542.1 reduce-scatter.17
  3978.4 542.1 reduce-scatter.19
  4523.8 265.8 all-reduce.15
where the time goes:
time: 4830 us; the launch traced here: 4820 us
  waiting for transfers between devices  4280 us (89%)
  matrix products  322 us (7%)
  blocking collectives  105 us (2%)
  other arithmetic  59 us (1%)
    all_gather x1, waiting for transfers between devices, local(): lax.all_gather(w_gate, 'fsdp', axis=0, tiled=True)  628 us
    all_gather x1, waiting for transfers between devices, local(): lax.all_gather(w_up, 'fsdp', axis=0, tiled=True)  623 us
    all_gather x1, waiting for transfers between devices, local(): lax.all_gather(w_down, 'fsdp', axis=0, tiled=True)  593 us
    reduce_scatter x1, waiting for transfers between devices, local(): lax.psum_scatter(left_tmul(ffn_in_all, g_gate_all).astype(jnp.bfloat16),...  546 us
    reduce_scatter x1, waiting for transfers between devices, local(): lax.psum_scatter(left_tmul(ffn_in_all, g_up_all).astype(jnp.bfloat16), 'f...  546 us
    reduce_scatter x1, waiting for transfers between devices, local(): lax.psum_scatter(left_tmul(hidden_all, g_ffn_all).astype(jnp.bfloat16), '...  546 us
    psum x1, waiting for transfers between devices, local(): lax.psum(acc_attn[0].astype(jnp.bfloat16), 'rep').astype(jnp.float32)  165 us
    reduce_scatter x1, waiting for transfers between devices, local(): lax.psum_scatter(left_tmul(mixed_all, g_attn_all).astype(jnp.bfloat16), '...  153 us
  transfers between devices with their start and end apart: 15, of which 14 were waited for; matrix products, arithmetic and copies ran while one was open for 5% of the time, Pallas kernels for 0%

commit v1 on v0

v1 whole, which is shorter than its diff:
```python
import math

import jax
import jax.numpy as jnp
from jax import lax
from jax.sharding import PartitionSpec as P

HD = 64
EPS = 1e-05
THETA = 1000000.0
NEG = -1e30
BF = jnp.bfloat16
F32 = jnp.float32


def matmul(left, right):
    return jnp.dot(left, right, preferred_element_type=F32)


def left_tmul(left, right):
    return lax.dot_general(left, right, (((0,), (0,)), ((), ())), preferred_element_type=F32)


def right_tmul(left, right):
    return lax.dot_general(left, right, (((1,), (1,)), ((), ())), preferred_element_type=F32)


def unit_rows(values):
    root = lax.rsqrt(jnp.mean(values * values, axis=-1, keepdims=True) + EPS)
    return values * root, root


def unit_back(unit, root, grad):
    return root * (grad - unit * jnp.mean(grad * unit, axis=-1, keepdims=True))


def rotate(values, cosine, sine):
    half = values.shape[-1] // 2
    first, second = values[..., :half], values[..., half:]
    return jnp.concatenate(
        [first * cosine - second * sine, second * cosine + first * sine], axis=-1
    )


def phases(segments):
    index = jnp.arange(segments.shape[1])
    same = segments[:, :, None] == segments[:, None, :]
    position = jnp.sum((same & (index[None, :] < index[:, None])).astype(jnp.int32), axis=2)
    frequency = jnp.exp(jnp.arange(HD // 2).astype(F32) * (-2.0 * math.log(THETA) / HD))
    phase = position.astype(F32)[:, :, None, None] * frequency
    return jnp.cos(phase), jnp.sin(phase), same & (index[None, :] <= index[:, None])


def gather_rows(values):
    return lax.all_gather(values, "fsdp", axis=0, tiled=True)


def scatter_rows(values):
    return lax.psum_scatter(values.astype(BF), "fsdp", scatter_dimension=0, tiled=True)


def rows_to_columns(weight):
    return lax.all_to_all(weight, "fsdp", 1, 0, tiled=True)


def columns_to_rows(grad):
    ranks, copies = lax.axis_size("fsdp"), lax.axis_size("rep")
    rows, columns = grad.shape
    part = rows // (ranks * copies)
    blocks = grad.astype(BF).reshape(ranks, copies, part, columns)
    own = lax.psum_scatter(blocks, "rep", scatter_dimension=1, tiled=True)
    own = own.reshape(ranks, part, columns)
    moved = lax.all_to_all(own, "fsdp", 0, 0, tiled=True)
    whole = lax.all_gather(moved, "rep", axis=0, tiled=False)
    return whole.transpose(0, 2, 1, 3).reshape(copies * part, ranks, columns)


def local(
    tokens_in,
    segment_ids,
    w_query,
    w_key,
    w_value,
    w_out,
    w_gate,
    w_up,
    w_down,
    gain_attn,
    gain_ffn,
    gain_query,
    gain_key,
    d_out,
):
    ranks = lax.axis_size("fsdp")
    rank = lax.axis_index("fsdp")
    width = tokens_in.shape[1]
    pack = segment_ids.shape[1]
    heads = w_query.shape[1] // HD
    kv_heads = w_key.shape[1] // HD
    share = max(1, ranks // kv_heads)
    q_here = heads // ranks
    kv_here = max(1, kv_heads // ranks)
    group = q_here // kv_here
    q_cols, kv_cols = q_here * HD, kv_here * HD
    scale = HD ** (-0.5)

    gains = lax.all_gather(jnp.stack([gain_attn, gain_ffn]), "fsdp", axis=1, tiled=True)
    attn_gain = gains[0].astype(F32)
    ffn_gain = gains[1].astype(F32)
    q_gain = gain_query.astype(F32)
    k_gain = gain_key.astype(F32)

    def by_rank(weight, columns, repeats):
        split = weight.reshape(weight.shape[0], -1, columns)
        return jnp.repeat(split, repeats, axis=1) if repeats > 1 else split

    qkv_rows = jnp.concatenate(
        [
            by_rank(w_query, q_cols, 1),
            by_rank(w_key, kv_cols, share),
            by_rank(w_value, kv_cols, share),
        ],
        axis=2,
    ).reshape(w_query.shape[0], -1)
    w_qkv = rows_to_columns(qkv_rows)
    w_gate_here = rows_to_columns(w_gate)
    w_up_here = rows_to_columns(w_up)

    tokens = tokens_in.astype(F32)
    unit_tokens, root_tokens = unit_rows(tokens)
    attn_in = gather_rows((unit_tokens * attn_gain).astype(BF))
    segments = lax.all_gather(segment_ids, "fsdp", axis=0, tiled=True)
    g_ffn = gather_rows(d_out)
    cosine, sine, allowed = phases(segments)
    packs = segments.shape[0]
    total = packs * pack

    qkv = matmul(attn_in, w_qkv)
    q_raw = qkv[:, :q_cols].reshape(packs, pack, q_here, HD)
    k_raw = qkv[:, q_cols : q_cols + kv_cols].reshape(packs, pack, kv_here, HD)
    value = qkv[:, q_cols + kv_cols :].reshape(packs, pack, kv_here, HD).astype(BF)
    q_unit, q_root = unit_rows(q_raw)
    k_unit, k_root = unit_rows(k_raw)
    query = rotate(q_unit * q_gain, cosine, sine).astype(BF)
    query = query.reshape(packs, pack, kv_here, group, HD)
    key = rotate(k_unit * k_gain, cosine, sine).astype(BF)
    scores = jnp.einsum("pikgd,pjkd->pkgij", query, key, preferred_element_type=F32) * scale
    masked = jnp.where(allowed[:, None, None], scores, NEG)
    exponent = jnp.exp(masked - jnp.max(masked, axis=-1, keepdims=True))
    probs = exponent / jnp.sum(exponent, axis=-1, keepdims=True)
    probs_low = probs.astype(BF)
    mixed = jnp.einsum("pkgij,pjkd->pikgd", probs_low, value, preferred_element_type=F32)
    mixed = mixed.reshape(total, q_cols).astype(BF)
    attn_branch = scatter_rows(matmul(mixed, w_out)).astype(F32)

    middle = tokens + attn_branch
    unit_middle, root_middle = unit_rows(middle)
    ffn_in = gather_rows((unit_middle * ffn_gain).astype(BF))
    gate = matmul(ffn_in, w_gate_here)
    up = matmul(ffn_in, w_up_here)
    sig = jax.nn.sigmoid(gate)
    silu = gate * sig
    hidden = (silu * up).astype(BF)
    ffn_branch = scatter_rows(matmul(hidden, w_down)).astype(F32)
    block = middle + ffn_branch

    grad_down = left_tmul(hidden, g_ffn)
    g_hidden = right_tmul(g_ffn, w_down).astype(BF).astype(F32)
    g_gate = (g_hidden * up * sig * (1 + gate * (1 - sig))).astype(BF)
    g_up = (g_hidden * silu).astype(BF)
    g_ffn_in = scatter_rows(right_tmul(g_gate, w_gate_here) + right_tmul(g_up, w_up_here))
    g_ffn_in = g_ffn_in.astype(F32)
    grad_gate = left_tmul(ffn_in, g_gate)
    grad_up = left_tmul(ffn_in, g_up)
    ffn_gain_grad = jnp.sum(g_ffn_in * unit_middle, axis=0)
    g_middle = d_out.astype(F32) + unit_back(unit_middle, root_middle, g_ffn_in * ffn_gain)

    g_attn = gather_rows(g_middle.astype(BF))
    grad_out = left_tmul(mixed, g_attn)
    g_mixed = right_tmul(g_attn, w_out).astype(BF).reshape(packs, pack, kv_here, group, HD)
    g_probs = jnp.einsum("pikgd,pjkd->pkgij", g_mixed, value, preferred_element_type=F32)
    g_value = jnp.einsum("pkgij,pikgd->pjkd", probs_low, g_mixed, preferred_element_type=F32)
    g_scores = probs * (g_probs - jnp.sum(probs * g_probs, axis=-1, keepdims=True))
    g_scores = g_scores.astype(BF)
    g_query = jnp.einsum("pkgij,pjkd->pikgd", g_scores, key, preferred_element_type=F32) * scale
    g_key = jnp.einsum("pkgij,pikgd->pjkd", g_scores, query, preferred_element_type=F32) * scale
    owner = jnp.ones((), F32)
    if share > 1:
        together = [[first * share + step for step in range(share)] for first in range(kv_heads)]
        g_value, g_key = lax.psum((g_value, g_key), "fsdp", axis_index_groups=together)
        owner = (rank % share == 0).astype(F32)
    q_back = rotate(g_query.reshape(packs, pack, q_here, HD), cosine, -sine)
    k_back = rotate(g_key, cosine, -sine)
    q_gain_grad = jnp.sum(q_back * q_unit, axis=(0, 1, 2))
    k_gain_grad = jnp.sum(k_back * k_unit, axis=(0, 1, 2)) * owner
    g_qkv = jnp.concatenate(
        [
            unit_back(q_unit, q_root, q_back * q_gain).reshape(total, q_cols),
            unit_back(k_unit, k_root, k_back * k_gain).reshape(total, kv_cols) * owner,
            g_value.reshape(total, kv_cols) * owner,
        ],
        axis=1,
    ).astype(BF)
    g_attn_in = scatter_rows(right_tmul(g_qkv, w_qkv)).astype(F32)
    grad_qkv = left_tmul(attn_in, g_qkv)
    attn_gain_grad = jnp.sum(g_attn_in * unit_tokens, axis=0)
    d_tokens = g_middle + unit_back(unit_tokens, root_tokens, g_attn_in * attn_gain)

    qkv_sum = columns_to_rows(grad_qkv)
    q_sum = qkv_sum[:, :, :q_cols].reshape(qkv_sum.shape[0], -1)
    k_sum = qkv_sum[:, ::share, q_cols : q_cols + kv_cols].reshape(qkv_sum.shape[0], -1)
    v_sum = qkv_sum[:, ::share, q_cols + kv_cols :].reshape(qkv_sum.shape[0], -1)
    gate_sum = columns_to_rows(grad_gate).reshape(w_gate.shape)
    up_sum = columns_to_rows(grad_up).reshape(w_up.shape)
    out_sum = lax.psum(grad_out.astype(BF), "rep")
    down_sum = lax.psum(grad_down.astype(BF), "rep")
    squares = jnp.stack(
        [jnp.sum(item * item) for item in (middle, attn_branch, ffn_branch, block, d_tokens)]
    )
    small = jnp.concatenate([attn_gain_grad, ffn_gain_grad, q_gain_grad, k_gain_grad, squares])
    small = lax.psum(small, ("fsdp", "rep"))
    gain_rows = gain_attn.shape[0]
    attn_gain_sum = lax.dynamic_slice(small, (rank * gain_rows,), (gain_rows,))
    ffn_gain_sum = lax.dynamic_slice(small, (width + rank * gain_rows,), (gain_rows,))
    entries = tokens_in.shape[0] * ranks * lax.axis_size("rep") * width
    stats = jnp.sqrt(small[2 * width + 2 * HD :] / entries)
    return (
        block.astype(BF),
        d_tokens.astype(BF),
        q_sum.astype(F32),
        k_sum.astype(F32),
        v_sum.astype(F32),
        out_sum.astype(F32),
        gate_sum.astype(F32),
        up_sum.astype(F32),
        down_sum.astype(F32),
        attn_gain_sum,
        ffn_gain_sum,
        small[2 * width : 2 * width + HD],
        small[2 * width + HD : 2 * width + 2 * HD],
        stats,
    )


def solution(mesh):
    rows = P(("fsdp", "rep"), None)
    weight = P("fsdp", None)
    return jax.shard_map(
        local,
        mesh=mesh,
        in_specs=(rows, rows, *[weight] * 7, P("fsdp"), P("fsdp"), P(), P(), rows),
        out_specs=(rows, rows, *[weight] * 7, P("fsdp"), P("fsdp"), P(), P(), P()),
        check_vma=False,
    )
```

time: 4830 us -> 1390 us (0.29)
  waiting for transfers between devices: 4280 us -> 840 us
  matrix products: 322 us -> 107 us
  blocking collectives: 105 us -> 220 us
  local copies, waits for them, and re-layouts: 36.2 us -> 122 us
    all_gather x7, waiting for transfers between devices: 2120 us -> 166 us  [the longest x4 164 us: gather_rows(): return lax.all_gather(values, 'fsdp', axis=0, tiled=True)]
    reduce_scatter x7 -> x5, waiting for transfers between devices: 1990 us -> 257 us  [the longest x4 249 us: scatter_rows(): lax.psum_scatter(values.astype(BF), 'fsdp', scatter_dimension=0, tiled=True)]
    dot_general x47 -> x21, matrix products: 322 us -> 107 us  [the longest x5 35.5 us: right_tmul(): lax.dot_general(left, right, (((1,), (1,)), ((), ())), preferred_element_...]
    all_to_all x0 -> x3, waiting for transfers between devices: none -> 199 us  [rows_to_columns(): return lax.all_to_all(weight, 'fsdp', 1, 0, tiled=True)]
    all_to_all x0 -> x3, blocking collectives: none -> 104 us  [columns_to_rows(): moved = lax.all_to_all(own, 'fsdp', 0, 0, tiled=True)]
    psum x1, waiting for transfers between devices: 165 us -> 218 us  [local(): out_sum = lax.psum(grad_out.astype(BF), 'rep')]
  transfers between devices with their start and end apart: 15 -> 16, of which waited for: 14 -> 13; matrix products, arithmetic and copies ran while one was open for 5% -> 11% of each run, Pallas kernels for 0% -> 0%
where the time goes in v1:
time: 1390 us; the launch traced here: 1380 us
  waiting for transfers between devices  840 us (60%)
  blocking collectives  220 us (16%)
  local copies, waits for them, and re-layouts  122 us (9%)
  matrix products  107 us (8%)
  other arithmetic  60.8 us (4%)
  between operations  15 us (1%)
    reduce_scatter x4, waiting for transfers between devices, scatter_rows(): lax.psum_scatter(values.astype(BF), 'fsdp', scatter_dimension=0, tiled=True)  249 us
    psum x1, waiting for transfers between devices, local(): out_sum = lax.psum(grad_out.astype(BF), 'rep')  218 us
    all_to_all x3, waiting for transfers between devices, rows_to_columns(): return lax.all_to_all(weight, 'fsdp', 1, 0, tiled=True)  199 us
    all_gather x4, waiting for transfers between devices, gather_rows(): return lax.all_gather(values, 'fsdp', axis=0, tiled=True)  164 us
    all_to_all x3, blocking collectives, columns_to_rows(): moved = lax.all_to_all(own, 'fsdp', 0, 0, tiled=True)  104 us
    all_gather x1, blocking collectives, local(): segments = lax.all_gather(segment_ids, 'fsdp', axis=0, tiled=True)  52.9 us
    unnamed x151, local copies, waits for them, and re-layouts  48 us
    psum x1, blocking collectives, local(): small = lax.psum(small, ('fsdp', 'rep'))  41.1 us
  transfers between devices with their start and end apart: 16, of which 13 were waited for; matrix products, arithmetic and copies ran while one was open for 11% of the time, Pallas kernels for 0%

profile of v1, /device:TPU:0, one launch (start us, length us, event | category | flops | bytes accessed | tf_op | source)
XLA Modules:
  0.0 1378.3 jit_solution(10191666948179028450)
XLA Ops:
  8.7 22.3 %all_gather.36 = bf16[2,2048]{1,0:T(2,128)(2,1)S(1)} all-gather(bf16[2,256]{1,0:T(2,128)(2,1)S(1)} %pad_maximum_fusion.9), channel_id=1, replica_groups=mesh['fsdp'=8,'rep'=4] {'fsdp'}, dimensions={1}, use_global_device_ids=true | all-gather | bytes 9216 | tf_op jit(solution)/shard_map/all_gather | solution.py:107
  41.7 52.9 %all-gather.3 = s32[8,2,64]{2,1,0:T(2,128)S(1)} all-gather(s32[1,2,64]{2,1,0:T(2,128)S(1)} %bitcast.238), channel_id=1, replica_groups=mesh['fsdp'=8,'rep'=4] {'fsdp'}, dimensions={0}, use_global_device_ids=true | all-gather | bytes 4608 | tf_op jit(solution)/shard_map/all_gather | solution.py:132
  100.4 28.5 %all-gather.12.cloned.1.call-done = bf16[1024,2048]{1,0:T(8,128)(2,1)} async-done(((bf16[128,2048]{1,0:T(8,128)(2,1)}), bf16[1024,2048]{1,0:T(8,128)(2,1)}) %all-gather.12.cloned.1.call-update) | async-done | bytes 4194320 | tf_op jit(solution)/shard_map/all_gather | solution.py:55
  185.2 113.8 %all-to-all-done.1 = bf16[256,8,1024]{0,2,1:T(8,128)(2,1)} async-done(((bf16[256,8,1024]{0,2,1:T(8,128)(2,1)}), bf16[256,8,1024]{0,2,1:T(8,128)(2,1)}, u32[]{:S(2)}, u32[]{:S(2)}) %all-to-all-start.1) | async-done | bytes 4194336 | tf_op jit(solution)/shard_map/all_to_all | solution.py:63
  303.7 49.2 %reduce-scatter.12.cloned.1.call-done = bf16[128,2048]{1,0:T(8,128)(2,1)} async-done(((bf16[1024,2048]{1,0:T(8,128)(2,1)}), bf16[128,2048]{1,0:T(8,128)(2,1)}) %reduce-scatter.12.cloned.1.call-update) | async-done | bytes 524304 | tf_op jit(solution)/shard_map/reduce_scatter | solution.py:59
  362.8 84.8 %all-to-all-done.2 = bf16[256,8,1024]{0,2,1:T(8,128)(2,1)} async-done(((bf16[256,8,1024]{0,2,1:T(8,128)(2,1)}), bf16[256,8,1024]{0,2,1:T(8,128)(2,1)}, u32[]{:S(2)}, u32[]{:S(2)}) %all-to-all-start.2) | async-done | bytes 4194336 | tf_op jit(solution)/shard_map/all_to_all | solution.py:63
  454.0 10.9 all-gather.16.cloned.1.call-done
  464.9 9.3 convolution_convert_fusion.8
  474.2 65.8 %all-gather.14.cloned.1.call-done = bf16[1024,2048]{1,0:T(8,128)(2,1)} async-done(((bf16[128,2048]{1,0:T(8,128)(2,1)}), bf16[1024,2048]{1,0:T(8,128)(2,1)}) %all-gather.14.cloned.1.call-update) | async-done | bytes 4194320 | tf_op jit(solution)/shard_map/all_gather | solution.py:55
  561.8 9.3 add_convert_fusion
  571.2 9.3 convolution_convert_fusion.5
  580.6 77.0 %reduce-scatter.16.cloned.1.call-done = bf16[128,2048]{1,0:T(8,128)(2,1)} async-done(((bf16[1024,2048]{1,0:T(8,128)(2,1)}), bf16[128,2048]{1,0:T(8,128)(2,1)}) %reduce-scatter.16.cloned.1.call-update) | async-done | bytes 524304 | tf_op jit(solution)/shard_map/reduce_scatter | solution.py:59
  657.6 91.7 %reduce-scatter.14.cloned.1.call-done = bf16[128,2048]{1,0:T(8,128)(2,1)} async-done(((bf16[1024,2048]{1,0:T(8,128)(2,1)}), bf16[128,2048]{1,0:T(8,128)(2,1)}) %reduce-scatter.14.cloned.1.call-update) | async-done | bytes 524304 | tf_op jit(solution)/shard_map/reduce_scatter | solution.py:59
  759.4 9.7 convolution_convert_fusion.4
  769.1 58.5 %all-gather.18.cloned.1.call-done = bf16[1024,2048]{1,0:T(8,128)(2,1)} async-done(((bf16[128,2048]{1,0:T(8,128)(2,1)}), bf16[1024,2048]{1,0:T(8,128)(2,1)}) %all-gather.18.cloned.1.call-update) | async-done | bytes 4194320 | tf_op jit(solution)/shard_map/all_gather | solution.py:55
  873.4 9.5 convolution_convert_fusion.2
  899.9 17.7 %all_to_all.69 = bf16[8,64,384]{2,1,0:T(8,128)(2,1)} all-to-all(bf16[8,64,384]{2,1,0:T(8,128)(2,1)} %bitcast.228), channel_id=1, replica_groups=mesh['fsdp'=8,'rep'=4] {'fsdp'}, dimensions={0} | all-to-all | bytes 786432 | tf_op jit(solution)/shard_map/all_to_all | solution.py:73
  924.8 217.8 %all-reduce.5.cloned.1.call-done = (bf16[256,2048]{1,0:T(8,128)(2,1)}, bf16[8,4,64,1024]{3,2,1,0:T(8,128)(2,1)}, bf16[8,4,64,1024]{3,2,1,0:T(8,128)(2,1)}, bf16[1024,2048]{1,0:T(8,128)(2,1)}) async-done(((bf16[256,2048]{1,0:T(8,128)(2,1)}, bf16[8,4,64,1024]{3,2,1,0:T(8,128)(2,1)}, bf16[8,4,64,1024]{3,2,1,0:T(8,128)(2,1)}, bf16[1024,2048]{1,0:T(8,128)(2,1)}), (bf16[256,2048]{1,0:T(8,128)(2,1)}, ...) | async-done | bytes 13631504 | tf_op jit(solution)/shard_map/psum | solution.py:215
  1144.7 31.0 %all_to_all.70 = bf16[8,64,1024]{2,1,0:T(8,128)(2,1)} all-to-all(bf16[8,64,1024]{2,1,0:T(8,128)(2,1)S(1)} %dynamic-slice_bitcast_fusion.1), channel_id=1, replica_groups=mesh['fsdp'=8,'rep'=4] {'fsdp'}, dimensions={0} | all-to-all | bytes 2097152 | tf_op jit(solution)/shard_map/all_to_all | solution.py:73
  1177.7 54.8 %all_to_all.71 = bf16[8,64,1024]{2,1,0:T(8,128)(2,1)} all-to-all(bf16[8,64,1024]{2,1,0:T(8,128)(2,1)S(1)} %dynamic-slice_bitcast_fusion), channel_id=1, replica_groups=mesh['fsdp'=8,'rep'=4] {'fsdp'}, dimensions={0} | all-to-all | bytes 2097152 | tf_op jit(solution)/shard_map/all_to_all | solution.py:73
  1248.8 30.7 %reduce-scatter.18.cloned.1.call-done = bf16[128,2048]{1,0:T(8,128)(2,1)} async-done(((bf16[1024,2048]{1,0:T(8,128)(2,1)}), bf16[128,2048]{1,0:T(8,128)(2,1)}) %reduce-scatter.18.cloned.1.call-update) | async-done | bytes 524304 | tf_op jit(solution)/shard_map/reduce_scatter | solution.py:59
  1287.4 41.1 %psum.23 = f32[4229]{0:T(1024)S(1)} all-reduce(f32[4229]{0:T(1024)S(1)} %concatenate.60), channel_id=1, replica_groups=mesh['fsdp'=8,'rep'=4] {'fsdp','rep'}, use_global_device_ids=true, to_apply=%region_31.32 | all-reduce | flops 4229 | bytes 33832 | tf_op jit(solution)/shard_map/psum | solution.py:221
  1338.4 11.1 copy.335
  1360.3 11.2 copy.336
  (291 shorter events, 245.3 us)
Async XLA Ops:
  7.2 155.2 %copy-start = (bf16[256,2048]{1,0:T(8,128)(2,1)S(1)}, bf16[256,2048]{1,0:T(8,128)(2,1)}, u32[]{:S(2)}) copy-start(bf16[256,2048]{1,0:T(8,128)(2,1)} %param.19) | copy-start | bytes 3145732
  7.2 121.7 %all-gather.12.cloned.1.call-start = ((), (), s32[]{:S(2)}) async-start(), calls=%async_computation.11 | async-start | bytes 4718592 | tf_op jit(solution)/shard_map/all_gather | solution.py:55
  37.4 57.4 %copy-start.61 = (bf16[64]{0:T(256)(128)(2,1)S(1)}, bf16[64]{0:T(256)(128)(2,1)}, u32[]{:S(2)}) copy-start(bf16[64]{0:T(256)(128)(2,1)} %param.26) | copy-start | bytes 388
  37.4 61.3 %all-to-all-start = ((bf16[256,8,384]{0,2,1:T(8,128)(2,1)}), bf16[256,8,384]{0,2,1:T(8,128)(2,1)S(1)}, u32[]{:S(2)}, u32[]{:S(2)}) async-start(bf16[256,8,384]{0,2,1:T(8,128)(2,1)} %pad_maximum_fusion.1), calls=%async_computation | async-start | bytes 3145728 | tf_op jit(solution)/shard_map/all_to_all | solution.py:63
  41.2 311.7 %reduce-scatter.12.cloned.1.call-start = ((), (), s32[]{:S(2)}) async-start(), calls=%async_computation.12 | async-start | bytes 4718592 | tf_op jit(solution)/shard_map/reduce_scatter | solution.py:59
  173.2 125.8 %all-to-all-start.1 = ((bf16[256,8,1024]{0,2,1:T(8,128)(2,1)}), bf16[256,8,1024]{0,2,1:T(8,128)(2,1)}, u32[]{:S(2)}, u32[]{:S(2)}) async-start(bf16[256,8,1024]{0,2,1:T(8,128)(2,1)} %bitcast.201), calls=%async_computation.2 | async-start | bytes 8388608 | tf_op jit(solution)/shard_map/all_to_all | solution.py:63
  177.7 287.1 %all-gather.16.cloned.1.call-start = ((), (), s32[]{:S(2)}) async-start(), calls=%async_computation.15 | async-start | bytes 4718592 | tf_op jit(solution)/shard_map/all_gather | solution.py:55
  299.0 53.9 %copy-start.2 = (bf16[128,2048]{1,0:T(8,128)(2,1)S(1)}, bf16[128,2048]{1,0:T(8,128)(2,1)}, u32[]{:S(2)}) copy-start(bf16[128,2048]{1,0:T(8,128)(2,1)} %param.14) | copy-start | bytes 1572868
  299.0 148.6 %all-to-all-start.2 = ((bf16[256,8,1024]{0,2,1:T(8,128)(2,1)}), bf16[256,8,1024]{0,2,1:T(8,128)(2,1)}, u32[]{:S(2)}, u32[]{:S(2)}) async-start(bf16[256,8,1024]{0,2,1:T(8,128)(2,1)} %bitcast.200), calls=%async_computation.3 | async-start | bytes 8388608 | tf_op jit(solution)/shard_map/all_to_all | solution.py:63
  303.7 236.3 %all-gather.14.cloned.1.call-start = ((), (), s32[]{:S(2)}) async-start(), calls=%async_computation.13 | async-start | bytes 4718592 | tf_op jit(solution)/shard_map/all_gather | solution.py:55
  354.2 398.7 %copy-start.43 = (f32[128]{0:T(128)}, f32[128]{0:T(128)S(1)}, u32[]{:S(2)}) copy-start(f32[128]{0:T(128)S(1)} %add_rsqrt_fusion.2) | copy-start | bytes 1540
  356.3 301.4 %reduce-scatter.16.cloned.1.call-start = ((), (), s32[]{:S(2)}) async-start(), calls=%async_computation.16 | async-start | bytes 4718592 | tf_op jit(solution)/shard_map/reduce_scatter | solution.py:59
  571.2 178.2 %reduce-scatter.14.cloned.1.call-start = ((), (), s32[]{:S(2)}) async-start(), calls=%async_computation.14 | async-start | bytes 4718592 | tf_op jit(solution)/shard_map/reduce_scatter | solution.py:59
  580.6 168.8 %copy-start.7 = (bf16[128,2048]{1,0:T(8,128)(2,1)S(1)}, bf16[128,2048]{1,0:T(8,128)(2,1)}, u32[]{:S(2)}) copy-start(bf16[128,2048]{1,0:T(8,128)(2,1)} %reduce-scatter.12.cloned.1.call-done) | copy-start | bytes 1572868
  580.6 247.0 %all-gather.18.cloned.1.call-start = ((), (), s32[]{:S(2)}) async-start(), calls=%async_computation.17 | async-start | bytes 4718592 | tf_op jit(solution)/shard_map/all_gather | solution.py:55
  754.3 145.7 %reduce-scatter.20.cloned.1.call-start = ((), (), s32[]{:S(2)}) async-start(), calls=%async_computation.19 | async-start | bytes 1966080 | tf_op jit(solution)/shard_map/reduce_scatter | solution.py:71
  873.4 269.3 %all-reduce.5.cloned.1.call-start = ((), (), s32[]{:S(2)}) async-start(), calls=%async_computation.23 | async-start | bytes 27262976 | tf_op jit(solution)/shard_map/psum | solution.py:215
  891.9 340.7 %all-gather.20.cloned.1.call-start = ((), (), s32[]{:S(2)}) async-start(), calls=%async_computation.20 | async-start | bytes 1966080 | tf_op jit(solution)/shard_map/all_gather | solution.py:74
  917.7 361.8 %reduce-scatter.18.cloned.1.call-start = ((), (), s32[]{:S(2)}) async-start(), calls=%async_computation.18 | async-start | bytes 4718592 | tf_op jit(solution)/shard_map/reduce_scatter | solution.py:59
  923.6 406.6 %all-gather.22.cloned.1.call-start = ((), (), s32[]{:S(2)}) async-start(), calls=%async_computation.21 | async-start | bytes 5242880 | tf_op jit(solution)/shard_map/all_gather | solution.py:74
  1175.7 176.5 %all-gather.24.cloned.1.call-start = ((), (), s32[]{:S(2)}) async-start(), calls=%async_computation.22 | async-start | bytes 5242880 | tf_op jit(solution)/shard_map/all_gather | solution.py:74
  1247.2 33.8 %copy-start.14 = (bf16[128,2048]{1,0:T(8,128)(2,1)S(1)}, bf16[128,2048]{1,0:T(8,128)(2,1)}, u32[]{:S(2)}) copy-start(bf16[128,2048]{1,0:T(8,128)(2,1)} %param.27) | copy-start | bytes 1572868
  1247.2 33.8 %copy-start.16 = (bf16[128,2048]{1,0:T(8,128)(2,1)S(1)}, bf16[128,2048]{1,0:T(8,128)(2,1)}, u32[]{:S(2)}) copy-start(bf16[128,2048]{1,0:T(8,128)(2,1)} %reduce-scatter.16.cloned.1.call-done) | copy-start | bytes 1572868
  1248.8 35.4 %copy-start.42 = (f32[2048]{0:T(1024)S(1)}, f32[2048]{0:T(1024)}, u32[]{:S(2)}) copy-start(f32[2048]{0:T(1024)} %get-tuple-element.114) | copy-start | bytes 24580
  (61 other events, 410.9 us)
Sparse Core Ops, SparseCore 0:
  34.5 94.4 all-gather.11
  166.9 185.9 reduce-scatter.11
  355.2 109.5 all-gather.15
  467.6 72.2 all-gather.13
  571.3 86.3 reduce-scatter.15
  661.7 87.6 reduce-scatter.13
  754.4 73.1 all-gather.17
  873.5 26.4 reduce-scatter.19
  903.9 238.7 all-reduce.4
  1144.1 19.8 all-gather.19
  1168.2 111.2 reduce-scatter.17
  1281.0 34.9 all-gather.21
  1317.6 34.5 all-gather.23

commit v2 on v1

--- a/solution.py
+++ b/solution.py
@@ -51,28 +51,147 @@
     return jnp.cos(phase), jnp.sin(phase), same & (index[None, :] <= index[:, None])
 
 
+def move(values, send):
+    ranks, copies = lax.axis_size("fsdp"), lax.axis_size("rep")
+    pairs = []
+    for f in range(ranks):
+        for r in range(copies):
+            to = send(f, r)
+            if to is not None:
+                pairs.append((f * copies + r, to[0] * copies + to[1]))
+    return lax.ppermute(values, ("fsdp", "rep"), pairs)
+
+
+def ring(values, step):
+    ranks = lax.axis_size("fsdp")
+    return move(values, lambda f, r: ((f + 2 * step) % ranks, r))
+
+
+def swap_core(values):
+    return move(values, lambda f, r: (f, r ^ 1))
+
+
+def swap_x(values):
+    return move(values, lambda f, r: (f, r ^ 2))
+
+
+def swap_twin(values):
+    return move(values, lambda f, r: (f ^ 1, r ^ 1))
+
+
+def place():
+    f, r = lax.axis_index("fsdp"), lax.axis_index("rep")
+    return f // 2, f % 2, r // 2, r % 2
+
+
+def pick(values, index, axis=0):
+    return lax.dynamic_index_in_dim(values, index, axis, keepdims=False)
+
+
+def ordered(slots, z):
+    depth = len(slots)
+    out = jnp.zeros((depth, *slots[0].shape), slots[0].dtype)
+    for k, slot in enumerate(slots):
+        out = lax.dynamic_update_index_in_dim(out, slot, (z - k) % depth, 0)
+    return out
+
+
+def both(own, other, first):
+    return jnp.where(first == 0, jnp.stack([own, other]), jnp.stack([other, own]))
+
+
+def gather_group(values):
+    depth = lax.axis_size("fsdp") // 2
+    half = values.shape[0] // 2
+    rise, fall = values[:half], values[half:]
+    slots = []
+    for s in range(depth):
+        if s > 0:
+            rise, fall = ring(rise, 1), ring(fall, -1)
+        here = jnp.concatenate([rise, fall], axis=0)
+        slots.append(jnp.stack([here, swap_core(here)]))
+    return jnp.stack(slots)
+
+
+def scatter_group(partial):
+    depth, _, rows = partial.shape[:3]
+    half = rows // 2
+    rise = fall = None
+    for s in (*range(1, depth), 0):
+        there = swap_core(partial[s, 1])
+        total = partial[s, 0].astype(F32) + there.astype(F32)
+        up, down = total[:half], total[half:]
+        if rise is not None:
+            up = up + ring(rise, 1).astype(F32)
+            down = down + ring(fall, -1).astype(F32)
+        rise, fall = up.astype(BF), down.astype(BF)
+    return jnp.concatenate([rise, fall], axis=0)
+
+
+def rows_to_columns(weight):
+    z, y, x, core = place()
+    rows, ranks, columns = weight.shape
+    depth, half = ranks // 2, rows // 2
+    mine = lax.dynamic_slice_in_dim(weight, x * half, half, axis=0)
+    mine = pick(mine.reshape(half, depth, 2, columns), y ^ core, 2)
+    slots = [ring(pick(mine, (z + k) % depth, 1), k) if k else pick(mine, z, 1) for k in range(depth)]
+    same_x = ordered(slots, z)
+    same_y = both(same_x, swap_x(same_x), x)
+    whole = both(same_y, swap_twin(same_y), y)
+    return whole.transpose(2, 0, 1, 3, 4).reshape(rows * ranks, columns)
+
+
+def columns_to_rows(grad):
+    z, y, x, core = place()
+    ranks = lax.axis_size("fsdp")
+    depth = ranks // 2
+    rows, columns = grad.shape[0] // ranks, grad.shape[1]
+    half = rows // 2
+    blocks = grad.reshape(depth, 2, rows, columns).astype(BF)
+    total = pick(blocks, y, 1).astype(F32) + swap_twin(pick(blocks, 1 - y, 1)).astype(F32)
+    total = total.astype(BF).reshape(depth, 2, half, columns)
+    total = pick(total, x, 1).astype(F32) + swap_x(pick(total, 1 - x, 1)).astype(F32)
+    total = total.astype(BF)
+    slots = [ring(pick(total, (z + k) % depth), k) if k else pick(total, z) for k in range(depth)]
+    same_x = ordered(slots, z)
+    same_core = both(same_x, swap_x(same_x), x)
+    whole = both(same_core, swap_core(same_core), y ^ core)
+    return whole.transpose(1, 3, 2, 0, 4).reshape(rows, ranks, columns)
+
+
+def rows_here(weight):
+    z, y, x, core = place()
+    half = weight.shape[0] // 2
+    part = lax.dynamic_slice_in_dim(weight, x * half, half, axis=0)
+    part = move(part, lambda f, r: (f ^ 1, r) if r % 2 else None)
+    other = move(part, lambda f, r: (f, r ^ 2) if r % 2 else None)
+    return jnp.where(core == 0, weight, both(part, other, x).reshape(weight.shape))
+
+
+def rows_sum(grad):
+    z, y, x, core = place()
+    rows, columns = grad.shape
+    first, second = jnp.split(grad.astype(BF), 2, axis=0)
+    crossed = move(
+        jnp.where(core == 0, second, first),
+        lambda f, r: (f ^ 1, r ^ 1) if r % 2 else (f, r ^ 1),
+    )
+    beside = move(second, lambda f, r: (f ^ 1, r) if r % 2 else None)
+    total = jnp.where(core == 0, first, beside).astype(F32) + crossed.astype(F32)
+    total = total.astype(BF).reshape(2, rows // 4, columns)
+    quarter = pick(total, x).astype(F32) + swap_x(pick(total, 1 - x)).astype(F32)
+    quarter = quarter.astype(BF)
+    half = both(quarter, swap_x(quarter), x)
+    return both(half, swap_core(half), core).reshape(rows, columns)
+
+
 def gather_rows(values):
-    return lax.all_gather(values, "fsdp", axis=0, tiled=True)
+    return gather_group(values).reshape(-1, values.shape[1])
 
 
 def scatter_rows(values):
-    return lax.psum_scatter(values.astype(BF), "fsdp", scatter_dimension=0, tiled=True)
-
-
-def rows_to_columns(weight):
-    return lax.all_to_all(weight, "fsdp", 1, 0, tiled=True)
-
-
-def columns_to_rows(grad):
-    ranks, copies = lax.axis_size("fsdp"), lax.axis_size("rep")
-    rows, columns = grad.shape
-    part = rows // (ranks * copies)
-    blocks = grad.astype(BF).reshape(ranks, copies, part, columns)
-    own = lax.psum_scatter(blocks, "rep", scatter_dimension=1, tiled=True)
-    own = own.reshape(ranks, part, columns)
-    moved = lax.all_to_all(own, "fsdp", 0, 0, tiled=True)
-    whole = lax.all_gather(moved, "rep", axis=0, tiled=False)
-    return whole.transpose(0, 2, 1, 3).reshape(copies * part, ranks, columns)
+    depth = lax.axis_size("fsdp") // 2
+    return scatter_group(values.astype(BF).reshape(depth, 2, -1, values.shape[1]))
 
 
 def local(
@@ -93,6 +212,8 @@
 ):
     ranks = lax.axis_size("fsdp")
     rank = lax.axis_index("fsdp")
+    depth = ranks // 2
+    z, y, x, core = place()
     width = tokens_in.shape[1]
     pack = segment_ids.shape[1]
     heads = w_query.shape[1] // HD
@@ -104,9 +225,21 @@
     q_cols, kv_cols = q_here * HD, kv_here * HD
     scale = HD ** (-0.5)
 
-    gains = lax.all_gather(jnp.stack([gain_attn, gain_ffn]), "fsdp", axis=1, tiled=True)
-    attn_gain = gains[0].astype(F32)
-    ffn_gain = gains[1].astype(F32)
+    seg_size = segment_ids.size
+    pieces = jnp.concatenate([segment_ids.reshape(-1).astype(BF), gain_attn, gain_ffn])
+    pieces = [ring(pieces, k) if k else pieces for k in range(depth)]
+    packs_here = segment_ids.shape[0] // 2
+    seg_slots = []
+    for s in range(depth):
+        rise = pieces[s][:seg_size].reshape(2, packs_here, pack)[0]
+        fall = pieces[(depth - s) % depth][:seg_size].reshape(2, packs_here, pack)[1]
+        seg_slots.append(jnp.concatenate([rise, fall], axis=0))
+    seg_slots = jnp.stack(seg_slots)
+    segments = jnp.stack([seg_slots, swap_core(seg_slots)], axis=1).reshape(-1, pack)
+    gains = ordered([piece[seg_size:] for piece in pieces], z)
+    gains = both(gains, move(gains, lambda f, r: (f ^ 1, r)), y)
+    gains = gains.reshape(2, depth, 2, -1).transpose(2, 1, 0, 3).reshape(2, -1).astype(F32)
+    attn_gain, ffn_gain = gains[0], gains[1]
     q_gain = gain_query.astype(F32)
     k_gain = gain_key.astype(F32)
 
@@ -121,15 +254,16 @@
             by_rank(w_value, kv_cols, share),
         ],
         axis=2,
-    ).reshape(w_query.shape[0], -1)
+    )
     w_qkv = rows_to_columns(qkv_rows)
-    w_gate_here = rows_to_columns(w_gate)
-    w_up_here = rows_to_columns(w_up)
+    w_out_here = rows_here(w_out)
+    w_gate_here = rows_to_columns(w_gate.reshape(w_gate.shape[0], ranks, -1))
+    w_up_here = rows_to_columns(w_up.reshape(w_up.shape[0], ranks, -1))
+    w_down_here = rows_here(w_down)
 
     tokens = tokens_in.astype(F32)
     unit_tokens, root_tokens = unit_rows(tokens)
     attn_in = gather_rows((unit_tokens * attn_gain).astype(BF))
-    segments = lax.all_gather(segment_ids, "fsdp", axis=0, tiled=True)
     g_ffn = gather_rows(d_out)
     cosine, sine, allowed = phases(segments)
     packs = segments.shape[0]
@@ -151,7 +285,7 @@
     probs_low = probs.astype(BF)
     mixed = jnp.einsum("pkgij,pjkd->pikgd", probs_low, value, preferred_element_type=F32)
     mixed = mixed.reshape(total, q_cols).astype(BF)
-    attn_branch = scatter_rows(matmul(mixed, w_out)).astype(F32)
+    attn_branch = scatter_rows(matmul(mixed, w_out_here)).astype(F32)
 
     middle = tokens + attn_branch
     unit_middle, root_middle = unit_rows(middle)
@@ -161,11 +295,11 @@
     sig = jax.nn.sigmoid(gate)
     silu = gate * sig
     hidden = (silu * up).astype(BF)
-    ffn_branch = scatter_rows(matmul(hidden, w_down)).astype(F32)
+    ffn_branch = scatter_rows(matmul(hidden, w_down_here)).astype(F32)
     block = middle + ffn_branch
 
     grad_down = left_tmul(hidden, g_ffn)
-    g_hidden = right_tmul(g_ffn, w_down).astype(BF).astype(F32)
+    g_hidden = right_tmul(g_ffn, w_down_here).astype(BF).astype(F32)
     g_gate = (g_hidden * up * sig * (1 + gate * (1 - sig))).astype(BF)
     g_up = (g_hidden * silu).astype(BF)
     g_ffn_in = scatter_rows(right_tmul(g_gate, w_gate_here) + right_tmul(g_up, w_up_here))
@@ -177,27 +311,22 @@
 
     g_attn = gather_rows(g_middle.astype(BF))
     grad_out = left_tmul(mixed, g_attn)
-    g_mixed = right_tmul(g_attn, w_out).astype(BF).reshape(packs, pack, kv_here, group, HD)
+    g_mixed = right_tmul(g_attn, w_out_here).astype(BF).reshape(packs, pack, kv_here, group, HD)
     g_probs = jnp.einsum("pikgd,pjkd->pkgij", g_mixed, value, preferred_element_type=F32)
     g_value = jnp.einsum("pkgij,pikgd->pjkd", probs_low, g_mixed, preferred_element_type=F32)
     g_scores = probs * (g_probs - jnp.sum(probs * g_probs, axis=-1, keepdims=True))
     g_scores = g_scores.astype(BF)
     g_query = jnp.einsum("pkgij,pjkd->pikgd", g_scores, key, preferred_element_type=F32) * scale
     g_key = jnp.einsum("pkgij,pikgd->pjkd", g_scores, query, preferred_element_type=F32) * scale
-    owner = jnp.ones((), F32)
-    if share > 1:
-        together = [[first * share + step for step in range(share)] for first in range(kv_heads)]
-        g_value, g_key = lax.psum((g_value, g_key), "fsdp", axis_index_groups=together)
-        owner = (rank % share == 0).astype(F32)
     q_back = rotate(g_query.reshape(packs, pack, q_here, HD), cosine, -sine)
     k_back = rotate(g_key, cosine, -sine)
     q_gain_grad = jnp.sum(q_back * q_unit, axis=(0, 1, 2))
-    k_gain_grad = jnp.sum(k_back * k_unit, axis=(0, 1, 2)) * owner
+    k_gain_grad = jnp.sum(k_back * k_unit, axis=(0, 1, 2))
     g_qkv = jnp.concatenate(
         [
             unit_back(q_unit, q_root, q_back * q_gain).reshape(total, q_cols),
-            unit_back(k_unit, k_root, k_back * k_gain).reshape(total, kv_cols) * owner,
-            g_value.reshape(total, kv_cols) * owner,
+            unit_back(k_unit, k_root, k_back * k_gain).reshape(total, kv_cols),
+            g_value.reshape(total, kv_cols),
         ],
         axis=1,
     ).astype(BF)
@@ -208,12 +337,15 @@
 
     qkv_sum = columns_to_rows(grad_qkv)
     q_sum = qkv_sum[:, :, :q_cols].reshape(qkv_sum.shape[0], -1)
-    k_sum = qkv_sum[:, ::share, q_cols : q_cols + kv_cols].reshape(qkv_sum.shape[0], -1)
-    v_sum = qkv_sum[:, ::share, q_cols + kv_cols :].reshape(qkv_sum.shape[0], -1)
+    kv_sum = qkv_sum[:, :, q_cols:]
+    if share > 1:
+        kv_sum = kv_sum.astype(F32).reshape(kv_sum.shape[0], -1, share, 2 * kv_cols).sum(axis=2)
+    k_sum = kv_sum[:, :, :kv_cols].reshape(kv_sum.shape[0], -1)
+    v_sum = kv_sum[:, :, kv_cols:].reshape(kv_sum.shape[0], -1)
     gate_sum = columns_to_rows(grad_gate).reshape(w_gate.shape)
     up_sum = columns_to_rows(grad_up).reshape(w_up.shape)
-    out_sum = lax.psum(grad_out.astype(BF), "rep")
-    down_sum = lax.psum(grad_down.astype(BF), "rep")
+    out_sum = rows_sum(grad_out)
+    down_sum = rows_sum(grad_down)
     squares = jnp.stack(
         [jnp.sum(item * item) for item in (middle, attn_branch, ffn_branch, block, d_tokens)]
     )

time: 1390 us -> 1020 us (0.73)
  waiting for transfers between devices: 840 us -> 300 us
  starting transfers between devices: 13.5 us -> 232 us
  blocking collectives: 220 us -> 53.5 us
  other arithmetic: 60.8 us -> 138 us
  local copies, waits for them, and re-layouts: 122 us -> 199 us
  matrix products: 107 us -> 80.1 us
    ppermute x0 -> x135, waiting for transfers between devices: none -> 300 us  [move(): return lax.ppermute(values, ('fsdp', 'rep'), pairs)]
    reduce_scatter x5 -> x0, waiting for transfers between devices: 257 us -> none  [the longest x4 249 us: scatter_rows(): lax.psum_scatter(values.astype(BF), 'fsdp', scatter_dimension=0, tiled=True)]
    ppermute x0 -> x135, starting transfers between devices: none -> 232 us  [move(): return lax.ppermute(values, ('fsdp', 'rep'), pairs)]
    psum x1 -> x0, waiting for transfers between devices: 218 us -> none  [local(): out_sum = lax.psum(grad_out.astype(BF), 'rep')]
    all_to_all x3 -> x0, waiting for transfers between devices: 199 us -> none  [rows_to_columns(): return lax.all_to_all(weight, 'fsdp', 1, 0, tiled=True)]
    all_gather x7 -> x0, waiting for transfers between devices: 166 us -> none  [the longest x4 164 us: gather_rows(): return lax.all_gather(values, 'fsdp', axis=0, tiled=True)]
    all_to_all x3 -> x0, blocking collectives: 104 us -> none  [columns_to_rows(): moved = lax.all_to_all(own, 'fsdp', 0, 0, tiled=True)]
    all_gather x2 -> x0, blocking collectives: 75.1 us -> none  [the longest x1 52.9 us: local(): segments = lax.all_gather(segment_ids, 'fsdp', axis=0, tiled=True)]
  transfers between devices with their start and end apart: 16 -> 135, of which waited for: 13 -> 49; matrix products, arithmetic and copies ran while one was open for 11% -> 33% of each run, Pallas kernels for 0% -> 0%
where the time goes in v2:
time: 1020 us; the launch traced here: 1010 us
  waiting for transfers between devices  300 us (29%)
  starting transfers between devices  232 us (23%)
  local copies, waits for them, and re-layouts  199 us (20%)
  other arithmetic  138 us (14%)
  matrix products  80.1 us (8%)
  blocking collectives  53.5 us (5%)
    ppermute x135, waiting for transfers between devices, move(): return lax.ppermute(values, ('fsdp', 'rep'), pairs)  300 us
    ppermute x135, starting transfers between devices, move(): return lax.ppermute(values, ('fsdp', 'rep'), pairs)  232 us
    psum x1, blocking collectives, local(): small = lax.psum(small, ('fsdp', 'rep'))  53.5 us
    select_n x22, other arithmetic, both(): jnp.where(first == 0, jnp.stack([own, other]), jnp.stack([other, own]))  44.4 us
    unnamed x255, local copies, waits for them, and re-layouts  41.8 us
    dot_general x5, matrix products, matmul(): return jnp.dot(left, right, preferred_element_type=F32)  25 us
    dot_general x5, matrix products, right_tmul(): lax.dot_general(left, right, (((1,), (1,)), ((), ())), preferred_element_...  24.1 us
    dot_general x5, matrix products, left_tmul(): lax.dot_general(left, right, (((0,), (0,)), ((), ())), preferred_element_...  23.4 us
  transfers between devices with their start and end apart: 135, of which 49 were waited for; matrix products, arithmetic and copies ran while one was open for 33% of the time, Pallas kernels for 0%

profile of v2, /device:TPU:0, one launch (start us, length us, event | category | flops | bytes accessed | tf_op | source)
XLA Modules:
  0.0 1006.0 jit_solution(962169820197963528)
XLA Ops:
  112.7 11.2 %collective-permute-done.48 = bf16[128,1024]{1,0:T(8,128)(2,1)S(1)} collective-permute-done((bf16[128,1024]{1,0:T(8,128)(2,1)S(1)}, bf16[128,1024]{1,0:T(8,128)(2,1)S(1)}, u32[]{:S(2)}, u32[]{:S(2)}) %collective-permute-start.48) | collective-permute-done | bytes 262176 | tf_op jit(solution)/shard_map/ppermute | solution.py:62
  129.2 7.9 collective-permute-start.5
  253.6 14.3 %collective-permute-done.45 = bf16[4,128,1024]{2,1,0:T(8,128)(2,1)S(1)} collective-permute-done((bf16[4,128,1024]{2,1,0:T(8,128)(2,1)S(1)}, bf16[4,128,1024]{2,1,0:T(8,128)(2,1)S(1)}, u32[]{:S(2)}, u32[]{:S(2)}) %collective-permute-start.45) | collective-permute-done | bytes 1048608 | tf_op jit(solution)/shard_map/ppermute | solution.py:62
  354.0 21.9 %collective-permute-done.51 = bf16[2,4,128,1024]{3,2,1,0:T(8,128)(2,1)} collective-permute-done((bf16[2,4,128,1024]{3,2,1,0:T(8,128)(2,1)}, bf16[2,4,128,1024]{3,2,1,0:T(8,128)(2,1)}, u32[]{:S(2)}, u32[]{:S(2)}) %collective-permute-start.51) | collective-permute-done | bytes 2097184 | tf_op jit(solution)/shard_map/ppermute | solution.py:62
  390.4 9.9 fusion.131
  438.3 7.8 add_convert_fusion
  476.4 7.6 collective-permute-start.81
  487.7 7.6 collective-permute-start.62
  498.9 7.5 collective-permute-start.82
  510.4 7.4 collective-permute-start.63
  521.5 7.5 collective-permute-start.83
  556.0 9.0 collective-permute-done.88
  578.3 18.0 %collective-permute-done.123 = bf16[4,256,1024]{2,1,0:T(8,128)(2,1)S(1)} collective-permute-done((bf16[4,256,1024]{2,1,0:T(8,128)(2,1)S(1)}, bf16[4,256,1024]{2,1,0:T(8,128)(2,1)S(1)}, u32[]{:S(2)}, u32[]{:S(2)}) %collective-permute-start.123) | collective-permute-done | bytes 2097184 | tf_op jit(solution)/shard_map/ppermute | solution.py:62
  599.1 42.0 %collective-permute-done.116 = bf16[4,256,1024]{2,1,0:T(8,128)(2,1)S(1)} collective-permute-done((bf16[4,256,1024]{2,1,0:T(8,128)(2,1)S(1)}, bf16[4,256,1024]{2,1,0:T(8,128)(2,1)S(1)}, u32[]{:S(2)}, u32[]{:S(2)}) %collective-permute-start.116) | collective-permute-done | bytes 2097184 | tf_op jit(solution)/shard_map/ppermute | solution.py:62
  740.1 10.6 %collective-permute-done.126 = bf16[128,1024]{1,0:T(8,128)(2,1)S(1)} collective-permute-done((bf16[128,1024]{1,0:T(8,128)(2,1)S(1)}, bf16[128,1024]{1,0:T(8,128)(2,1)S(1)}, u32[]{:S(2)}, u32[]{:S(2)}) %collective-permute-start.126) | collective-permute-done | bytes 262176 | tf_op jit(solution)/shard_map/ppermute | solution.py:62
  756.4 12.0 %collective-permute-start.101 = (bf16[64,2048]{1,0:T(8,128)(2,1)S(1)}, bf16[64,2048]{1,0:T(8,128)(2,1)S(1)}, u32[]{:S(2)}, u32[]{:S(2)}) collective-permute-start(bf16[64,2048]{1,0:T(8,128)(2,1)S(1)} %get-tuple-element.225), channel_id=1, source_target_pairs={{0,24},{1,25},{2,26},{3,27},{4,28},{5,29},{6,30},{7,31},{8,0},{9,1... | collective-permute-start | bytes 786440 | tf_op jit(solution)/shard_map/ppermute | solution.py:62
  772.9 8.1 collective-permute-start.98
  794.1 10.7 %collective-permute-done.102 = bf16[64,2048]{1,0:T(8,128)(2,1)S(1)} collective-permute-done((bf16[64,2048]{1,0:T(8,128)(2,1)S(1)}, bf16[64,2048]{1,0:T(8,128)(2,1)S(1)}, u32[]{:S(2)}, u32[]{:S(2)}) %collective-permute-start.102) | collective-permute-done | bytes 262176 | tf_op jit(solution)/shard_map/ppermute | solution.py:62
  805.7 13.2 %collective-permute-done.114 = bf16[64,2048]{1,0:T(8,128)(2,1)S(1)} collective-permute-done((bf16[64,2048]{1,0:T(8,128)(2,1)S(1)}, bf16[64,2048]{1,0:T(8,128)(2,1)S(1)}, u32[]{:S(2)}, u32[]{:S(2)}) %collective-permute-start.114) | collective-permute-done | bytes 262176 | tf_op jit(solution)/shard_map/ppermute | solution.py:62
  854.6 53.5 %psum.7 = f32[4229]{0:T(1024)S(1)} all-reduce(f32[4229]{0:T(1024)S(1)} %concatenate.263), channel_id=1, replica_groups=mesh['fsdp'=8,'rep'=4] {'fsdp','rep'}, use_global_device_ids=true, to_apply=%region_22.23 | all-reduce | flops 4229 | bytes 33832 | tf_op jit(solution)/shard_map/psum | solution.py:353
  959.1 10.0 copy.445
  969.1 11.8 %reshape.1103 = f32[256,8192]{1,0:T(8,128)} reshape(f32[2,128,4,2,1024]{4,3,2,1,0:T(2,128)} %copy.445) | data formatting | bytes 16777216 | tf_op jit(solution)/shard_map/convert_element_type | solution.py:367
  984.0 10.0 copy.443
  994.0 11.8 %reshape.1100 = f32[256,8192]{1,0:T(8,128)} reshape(f32[2,128,4,2,1024]{4,3,2,1,0:T(2,128)} %copy.443) | data formatting | bytes 16777216 | tf_op jit(solution)/shard_map/convert_element_type | solution.py:366
  (790 shorter events, 671.0 us)
Async XLA Ops:
  5.5 53.0 %collective-permute-start = (bf16[640]{0:T(1024)(128)(2,1)}, bf16[640]{0:T(1024)(128)(2,1)}, u32[]{:S(2)}, u32[]{:S(2)}) collective-permute-start(bf16[640]{0:T(1024)(128)(2,1)} %dynamic-update-slice.26), channel_id=1, source_target_pairs={{0,8},{1,9},{2,10},{3,11},{4,12},{5,13},{6,14},{7,15},{8,16},{9,17... | collective-permute-start | bytes 3848 | tf_op jit(solution)/shard_map/ppermute | solution.py:62
  33.8 67.8 %collective-permute-start.42 = (bf16[128,1024]{1,0:T(8,128)(2,1)}, bf16[128,1024]{1,0:T(8,128)(2,1)}, u32[]{:S(2)}, u32[]{:S(2)}) collective-permute-start(bf16[128,1024]{1,0:T(8,128)(2,1)} %get-tuple-element.171), channel_id=1, source_target_pairs={{0,8},{1,9},{2,10},{3,11},{4,12},{5,13},{6,14},{7,15},{8,16},{9,17... | collective-permute-start | bytes 786440 | tf_op jit(solution)/shard_map/ppermute | solution.py:62
  34.4 124.6 %collective-permute-start.64 = (bf16[128,2048]{1,0:T(8,128)(2,1)S(1)}, bf16[128,2048]{1,0:T(8,128)(2,1)}, u32[]{:S(2)}, u32[]{:S(2)}) collective-permute-start(bf16[128,2048]{1,0:T(8,128)(2,1)S(1)} %copy-done.21), channel_id=1, source_target_pairs={{0,1},{1,0},{2,3},{3,2},{4,5},{5,4},{6,7},{7,6},{8,9},{9,8},{10,11... | collective-permute-start | bytes 1572872 | tf_op jit(solution)/shard_map/ppermute | solution.py:62
  100.8 83.3 %collective-permute-start.20 = (bf16[128,2048]{1,0:T(8,128)(2,1)S(1)}, bf16[128,2048]{1,0:T(8,128)(2,1)S(1)}, u32[]{:S(2)}, u32[]{:S(2)}) collective-permute-start(bf16[128,2048]{1,0:T(8,128)(2,1)S(1)} %copy-done.69), channel_id=1, source_target_pairs={{1,5},{3,7},{5,1},{7,3},{9,13},{11,15},{13,9},{15,11},{17,21},{19,... | collective-permute-start | bytes 1572872 | tf_op jit(solution)/shard_map/ppermute | solution.py:62
  152.5 86.0 %collective-permute-start.67 = (bf16[128,2048]{1,0:T(8,128)(2,1)}, bf16[128,2048]{1,0:T(8,128)(2,1)}, u32[]{:S(2)}, u32[]{:S(2)}) collective-permute-start(bf16[128,2048]{1,0:T(8,128)(2,1)} %constant_dynamic-update-slice_fusion.12), channel_id=1, source_target_pairs={{0,1},{1,0},{2,3},{3,2},{4,5},{5,4},{6,7},{7,6},{8,9},{9,8},{10,11... | collective-permute-start | bytes 1572872 | tf_op jit(solution)/shard_map/ppermute | solution.py:62
  238.5 86.0 %collective-permute-start.52 = (bf16[512,2048]{1,0:T(8,128)(2,1)}, bf16[512,2048]{1,0:T(8,128)(2,1)}, u32[]{:S(2)}, u32[]{:S(2)}) collective-permute-start(bf16[512,2048]{1,0:T(8,128)(2,1)} %constant_dynamic-slice_fusion), channel_id=1, source_target_pairs={{1,5},{3,7},{5,1},{7,3},{9,13},{11,15},{13,9},{15,11},{17,21},{19,... | collective-permute-start | bytes 6291464 | tf_op jit(solution)/shard_map/ppermute | solution.py:62
  283.3 56.0 %collective-permute-start.46 = (bf16[2,4,128,1024]{3,2,0,1:T(8,128)(2,1)}, bf16[2,4,128,1024]{3,2,0,1:T(8,128)(2,1)}, u32[]{:S(2)}, u32[]{:S(2)}) collective-permute-start(bf16[2,4,128,1024]{3,2,0,1:T(8,128)(2,1)} %maximum_select_fusion.6), channel_id=1, source_target_pairs={{0,5},{1,4},{2,7},{3,6},{4,1},{5,0},{6,3},{7,2},{8,13},{9,12},{10,... | collective-permute-start | bytes 6291464 | tf_op jit(solution)/shard_map/ppermute | solution.py:62
  292.7 83.2 %collective-permute-start.51 = (bf16[2,4,128,1024]{3,2,1,0:T(8,128)(2,1)}, bf16[2,4,128,1024]{3,2,1,0:T(8,128)(2,1)}, u32[]{:S(2)}, u32[]{:S(2)}) collective-permute-start(bf16[2,4,128,1024]{3,2,1,0:T(8,128)(2,1)} %maximum_select_fusion.8), channel_id=1, source_target_pairs={{0,5},{1,4},{2,7},{3,6},{4,1},{5,0},{6,3},{7,2},{8,13},{9,12},{10,... | collective-permute-start | bytes 6291464 | tf_op jit(solution)/shard_map/ppermute | solution.py:62
  335.5 64.8 %collective-permute-start.53 = (bf16[512,2048]{1,0:T(8,128)(2,1)}, bf16[512,2048]{1,0:T(8,128)(2,1)}, u32[]{:S(2)}, u32[]{:S(2)}) collective-permute-start(bf16[512,2048]{1,0:T(8,128)(2,1)} %collective-permute-done.52), channel_id=1, source_target_pairs={{1,3},{3,1},{5,7},{7,5},{9,11},{11,9},{13,15},{15,13},{17,19},{19,... | collective-permute-start | bytes 6291464 | tf_op jit(solution)/shard_map/ppermute | solution.py:62
  455.9 116.3 %collective-permute-start.130 = (bf16[512,2048]{1,0:T(8,128)(2,1)S(1)}, bf16[512,2048]{1,0:T(8,128)(2,1)}, u32[]{:S(2)}, u32[]{:S(2)}) collective-permute-start(bf16[512,2048]{1,0:T(8,128)(2,1)S(1)} %get-tuple-element.127), channel_id=1, source_target_pairs={{1,5},{3,7},{5,1},{7,3},{9,13},{11,15},{13,9},{15,11},{17,21},{19,... | collective-permute-start | bytes 6291464 | tf_op jit(solution)/shard_map/ppermute | solution.py:62
  460.8 112.0 %collective-permute-start.131 = (bf16[512,2048]{1,0:T(8,128)(2,1)S(1)}, bf16[512,2048]{1,0:T(8,128)(2,1)S(1)}, u32[]{:S(2)}, u32[]{:S(2)}) collective-permute-start(bf16[512,2048]{1,0:T(8,128)(2,1)S(1)} %get-tuple-element.128), channel_id=1, source_target_pairs={{0,1},{1,4},{2,3},{3,6},{4,5},{5,0},{6,7},{7,2},{8,9},{9,12},{10,1... | collective-permute-start | bytes 6291464 | tf_op jit(solution)/shard_map/ppermute | solution.py:62
  555.9 85.3 %collective-permute-start.116 = (bf16[4,256,1024]{2,1,0:T(8,128)(2,1)S(1)}, bf16[4,256,1024]{2,1,0:T(8,128)(2,1)S(1)}, u32[]{:S(2)}, u32[]{:S(2)}) collective-permute-start(bf16[4,256,1024]{2,1,0:T(8,128)(2,1)S(1)} %dynamic-slice_bitcast_fusion.1), channel_id=1, source_target_pairs={{0,5},{1,4},{2,7},{3,6},{4,1},{5,0},{6,3},{7,2},{8,13},{9,12},{10,... | collective-permute-start | bytes 6291464 | tf_op jit(solution)/shard_map/ppermute | solution.py:62
  572.3 74.3 %collective-permute-start.87 = (bf16[128,2048]{1,0:T(8,128)(2,1)S(1)}, bf16[128,2048]{1,0:T(8,128)(2,1)S(1)}, u32[]{:S(2)}, u32[]{:S(2)}) collective-permute-start(bf16[128,2048]{1,0:T(8,128)(2,1)S(1)} %constant_dynamic-update-slice_fusion.18), channel_id=1, source_target_pairs={{0,1},{1,0},{2,3},{3,2},{4,5},{5,4},{6,7},{7,6},{8,9},{9,8},{10,11... | collective-permute-start | bytes 1572872 | tf_op jit(solution)/shard_map/ppermute | solution.py:62
  572.3 76.3 %collective-permute-start.90 = (bf16[128,2048]{1,0:T(8,128)(2,1)S(1)}, bf16[128,2048]{1,0:T(8,128)(2,1)S(1)}, u32[]{:S(2)}, u32[]{:S(2)}) collective-permute-start(bf16[128,2048]{1,0:T(8,128)(2,1)S(1)} %constant_dynamic-update-slice_fusion.20), channel_id=1, source_target_pairs={{0,1},{1,0},{2,3},{3,2},{4,5},{5,4},{6,7},{7,6},{8,9},{9,8},{10,11... | collective-permute-start | bytes 1572872 | tf_op jit(solution)/shard_map/ppermute | solution.py:62
  574.2 71.0 %collective-permute-start.91 = (bf16[64,2048]{1,0:T(8,128)(2,1)S(1)}, bf16[64,2048]{1,0:T(8,128)(2,1)S(1)}, u32[]{:S(2)}, u32[]{:S(2)}) collective-permute-start(bf16[64,2048]{1,0:T(8,128)(2,1)S(1)} %collective-permute-done.88), channel_id=1, source_target_pairs={{0,8},{1,9},{2,10},{3,11},{4,12},{5,13},{6,14},{7,15},{8,16},{9,17... | collective-permute-start | bytes 786440 | tf_op jit(solution)/shard_map/ppermute | solution.py:62
  641.2 73.2 %collective-permute-start.132 = (bf16[256,2048]{1,0:T(8,128)(2,1)}, bf16[256,2048]{1,0:T(8,128)(2,1)}, u32[]{:S(2)}, u32[]{:S(2)}) collective-permute-start(bf16[256,2048]{1,0:T(8,128)(2,1)} %dynamic-slice_bitcast_fusion.2), channel_id=1, source_target_pairs={{0,2},{1,3},{2,0},{3,1},{4,6},{5,7},{6,4},{7,5},{8,10},{9,11},{10,... | collective-permute-start | bytes 3145736 | tf_op jit(solution)/shard_map/ppermute | solution.py:62
  645.2 58.8 %collective-permute-start.124 = (bf16[4,128,1024]{2,1,0:T(8,128)(2,1)}, bf16[4,128,1024]{2,1,0:T(8,128)(2,1)}, u32[]{:S(2)}, u32[]{:S(2)}) collective-permute-start(bf16[4,128,1024]{2,1,0:T(8,128)(2,1)} %dynamic-slice_bitcast_fusion.3), channel_id=1, source_target_pairs={{0,2},{1,3},{2,0},{3,1},{4,6},{5,7},{6,4},{7,5},{8,10},{9,11},{10,... | collective-permute-start | bytes 3145736 | tf_op jit(solution)/shard_map/ppermute | solution.py:62
  646.6 65.2 %collective-permute-start.117 = (bf16[4,128,1024]{2,1,0:T(8,128)(2,1)}, bf16[4,128,1024]{2,1,0:T(8,128)(2,1)}, u32[]{:S(2)}, u32[]{:S(2)}) collective-permute-start(bf16[4,128,1024]{2,1,0:T(8,128)(2,1)} %dynamic-slice_bitcast_fusion.4), channel_id=1, source_target_pairs={{0,2},{1,3},{2,0},{3,1},{4,6},{5,7},{6,4},{7,5},{8,10},{9,11},{10,... | collective-permute-start | bytes 3145736 | tf_op jit(solution)/shard_map/ppermute | solution.py:62
  727.1 66.3 %collective-permute-start.104 = (bf16[4,256,384]{2,1,0:T(8,128)(2,1)S(1)}, bf16[4,256,384]{2,1,0:T(8,128)(2,1)S(1)}, u32[]{:S(2)}, u32[]{:S(2)}) collective-permute-start(bf16[4,256,384]{2,1,0:T(8,128)(2,1)S(1)} %dynamic-slice_bitcast_fusion.5), channel_id=1, source_target_pairs={{0,5},{1,4},{2,7},{3,6},{4,1},{5,0},{6,3},{7,2},{8,13},{9,12},{10,... | collective-permute-start | bytes 2359304 | tf_op jit(solution)/shard_map/ppermute | solution.py:62
  727.3 182.5 %collective-permute-start.133 = (bf16[256,2048]{1,0:T(8,128)(2,1)S(1)}, bf16[256,2048]{1,0:T(8,128)(2,1)}, u32[]{:S(2)}, u32[]{:S(2)}) collective-permute-start(bf16[256,2048]{1,0:T(8,128)(2,1)S(1)} %fusion.8), channel_id=1, source_target_pairs={{0,2},{1,3},{2,0},{3,1},{4,6},{5,7},{6,4},{7,5},{8,10},{9,11},{10,... | collective-permute-start | bytes 3145736 | tf_op jit(solution)/shard_map/ppermute | solution.py:62
  784.0 139.1 %collective-permute-start.128 = (bf16[4,128,1024]{2,1,0:T(8,128)(2,1)S(1)}, bf16[4,128,1024]{2,1,0:T(8,128)(2,1)}, u32[]{:S(2)}, u32[]{:S(2)}) collective-permute-start(bf16[4,128,1024]{2,1,0:T(8,128)(2,1)S(1)} %bitcast_dynamic-update-slice_fusion), channel_id=1, source_target_pairs={{0,2},{1,3},{2,0},{3,1},{4,6},{5,7},{6,4},{7,5},{8,10},{9,11},{10,... | collective-permute-start | bytes 3145736 | tf_op jit(solution)/shard_map/ppermute | solution.py:62
  845.8 80.5 %collective-permute-start.121 = (bf16[4,128,1024]{2,1,0:T(8,128)(2,1)}, bf16[4,128,1024]{2,1,0:T(8,128)(2,1)}, u32[]{:S(2)}, u32[]{:S(2)}) collective-permute-start(bf16[4,128,1024]{2,1,0:T(8,128)(2,1)} %bitcast_dynamic-update-slice_fusion.3), channel_id=1, source_target_pairs={{0,2},{1,3},{2,0},{3,1},{4,6},{5,7},{6,4},{7,5},{8,10},{9,11},{10,... | collective-permute-start | bytes 3145736 | tf_op jit(solution)/shard_map/ppermute | solution.py:62
  847.0 69.4 %collective-permute-start.115 = (bf16[2,64,2048]{2,1,0:T(8,128)(2,1)}, bf16[2,64,2048]{2,1,0:T(8,128)(2,1)}, u32[]{:S(2)}, u32[]{:S(2)}) collective-permute-start(bf16[2,64,2048]{2,1,0:T(8,128)(2,1)} %maximum_select_fusion.23), channel_id=1, source_target_pairs={{0,1},{1,0},{2,3},{3,2},{4,5},{5,4},{6,7},{7,6},{8,9},{9,8},{10,11... | collective-permute-start | bytes 1572872 | tf_op jit(solution)/shard_map/ppermute | solution.py:62
  847.0 72.4 %collective-permute-start.109 = (bf16[4,128,384]{2,1,0:T(8,128)(2,1)}, bf16[4,128,384]{2,1,0:T(8,128)(2,1)}, u32[]{:S(2)}, u32[]{:S(2)}) collective-permute-start(bf16[4,128,384]{2,1,0:T(8,128)(2,1)} %bitcast_dynamic-update-slice_fusion.14), channel_id=1, source_target_pairs={{0,2},{1,3},{2,0},{3,1},{4,6},{5,7},{6,4},{7,5},{8,10},{9,11},{10,... | collective-permute-start | bytes 1179656 | tf_op jit(solution)/shard_map/ppermute | solution.py:62
  (225 other events, 3065.9 us)

commit v3 on v1

v3 whole, which is shorter than its diff:
```python
import functools
import math

import jax
import jax.numpy as jnp
from jax import lax
from jax.experimental import pallas as pl
from jax.experimental.pallas import tpu as pltpu
from jax.sharding import PartitionSpec as P

HD = 64
EPS = 1e-05
THETA = 1000000.0
NEG = -1e30
BF = jnp.bfloat16
F32 = jnp.float32
ATTENTION_BYTES = 24 * 1024 * 1024
PLACE_BYTES = 24 * 1024 * 1024


def matmul(left, right):
    return jnp.dot(left, right, preferred_element_type=F32)


def left_tmul(left, right):
    return lax.dot_general(left, right, (((0,), (0,)), ((), ())), preferred_element_type=F32)


def right_tmul(left, right):
    return lax.dot_general(left, right, (((1,), (1,)), ((), ())), preferred_element_type=F32)


def unit_rows(values):
    root = lax.rsqrt(jnp.mean(values * values, axis=-1, keepdims=True) + EPS)
    return values * root, root


def unit_back(unit, root, grad):
    return root * (grad - unit * jnp.mean(grad * unit, axis=-1, keepdims=True))


def turn(values, cosine, sine):
    half = values.shape[-1] // 2
    swapped = jnp.concatenate([values[:, half:], values[:, :half]], axis=1)
    return values * cosine + swapped * sine


def phases(segments):
    index = jnp.arange(segments.shape[1])
    same = segments[:, :, None] == segments[:, None, :]
    position = jnp.sum((same & (index[None, :] < index[:, None])).astype(jnp.int32), axis=2)
    frequency = jnp.exp(jnp.arange(HD // 2).astype(F32) * (-2.0 * math.log(THETA) / HD))
    phase = position.astype(F32).reshape(-1, 1) * frequency
    cosine, sine = jnp.cos(phase), jnp.sin(phase)
    return jnp.concatenate([cosine, cosine], axis=1), jnp.concatenate([-sine, sine], axis=1)


def head(values, index):
    return values[:, index * HD : (index + 1) * HD]


def allowed_block(column, row):
    size = column.shape[0]
    later = lax.broadcasted_iota(jnp.int32, (size, size), 1)
    return (column == row) & (later <= lax.broadcasted_iota(jnp.int32, (size, size), 0))


def probabilities(query, key, allowed):
    scores = right_tmul(query, key) * HD ** (-0.5)
    exponent = jnp.where(allowed, jnp.exp(scores), 0.0)
    return exponent * (1.0 / jnp.sum(exponent, axis=-1, keepdims=True))


def attention_kernel(q_here, kv_here, *refs):
    (here_ref, other_ref, column_ref, row_ref, cos_ref, sin_ref, gain_ref, q_gain_ref, k_gain_ref) = refs[:9]
    w_qkv_ref, w_out_ref, attn_in_ref, qkv_ref, mixed_ref, own_ref, away_ref = refs[9:]
    group = q_here // kv_here
    rows = here_ref.shape[0]
    gain = gain_ref[...]
    for index, tokens_ref in enumerate((here_ref, other_ref)):
        unit, _ = unit_rows(tokens_ref[...].astype(F32))
        attn_in_ref[index * rows : (index + 1) * rows, :] = (unit * gain).astype(BF)
    qkv = matmul(attn_in_ref[...], w_qkv_ref[...])
    qkv_ref[...] = qkv
    blocks = [slice(index * rows, (index + 1) * rows) for index in range(2)]
    allowed = [allowed_block(column_ref[part, :], row_ref[index]) for index, part in enumerate(blocks)]
    cosine, sine = cos_ref[...], sin_ref[...]
    for kv in range(kv_here):
        key = turn(unit_rows(head(qkv, q_here + kv))[0] * k_gain_ref[...], cosine, sine).astype(BF)
        value = head(qkv, q_here + kv_here + kv).astype(BF)
        for h in range(kv * group, (kv + 1) * group):
            query = turn(unit_rows(head(qkv, h))[0] * q_gain_ref[...], cosine, sine).astype(BF)
            for index, part in enumerate(blocks):
                probs = probabilities(query[part], key[part], allowed[index])
                mixed_ref[part, h * HD : (h + 1) * HD] = matmul(probs.astype(BF), value[part]).astype(BF)
    mixed = mixed_ref[...]
    own_ref[...] = matmul(mixed[:rows], w_out_ref[...]).astype(BF)
    away_ref[...] = matmul(mixed[rows:], w_out_ref[...]).astype(BF)


def attention_back_kernel(q_here, kv_here, *refs):
    (here_ref, other_ref, qkv_ref, column_ref, row_ref, cos_ref, sin_ref, q_gain_ref, k_gain_ref) = refs[:9]
    w_qkv_ref, w_out_ref, g_attn_ref, g_qkv_ref, own_ref, away_ref, gains_ref = refs[9:]
    group = q_here // kv_here
    rows = here_ref.shape[0]
    g_attn_ref[:rows, :] = here_ref[...]
    g_attn_ref[rows:, :] = other_ref[...]
    g_mixed = right_tmul(g_attn_ref[...], w_out_ref[...]).astype(BF)
    qkv = qkv_ref[...]
    blocks = [slice(index * rows, (index + 1) * rows) for index in range(2)]
    allowed = [allowed_block(column_ref[part, :], row_ref[index]) for index, part in enumerate(blocks)]
    cosine, sine = cos_ref[...], sin_ref[...]
    q_gain, k_gain = q_gain_ref[...], k_gain_ref[...]
    scale = HD ** (-0.5)
    q_sum = jnp.zeros((1, HD), F32)
    k_sum = jnp.zeros((1, HD), F32)
    pieces = {}
    for kv in range(kv_here):
        k_unit, k_root = unit_rows(head(qkv, q_here + kv))
        key = turn(k_unit * k_gain, cosine, sine).astype(BF)
        value = head(qkv, q_here + kv_here + kv).astype(BF)
        g_k, g_v = [0.0, 0.0], [0.0, 0.0]
        for h in range(kv * group, (kv + 1) * group):
            q_unit, q_root = unit_rows(head(qkv, h))
            query = turn(q_unit * q_gain, cosine, sine).astype(BF)
            g_head = head(g_mixed, h)
            g_query = []
            for index, part in enumerate(blocks):
                probs = probabilities(query[part], key[part], allowed[index])
                g_probs = right_tmul(g_head[part], value[part])
                g_v[index] = g_v[index] + left_tmul(probs.astype(BF), g_head[part])
                g_scores = probs * (g_probs - jnp.sum(probs * g_probs, axis=-1, keepdims=True))
                g_scores = g_scores.astype(BF)
                g_k[index] = g_k[index] + left_tmul(g_scores, query[part])
                g_query.append(matmul(g_scores, key[part]))
            back = turn(jnp.concatenate(g_query, axis=0) * scale, cosine, -sine)
            q_sum = q_sum + jnp.sum(back * q_unit, axis=0, keepdims=True)
            pieces[h] = unit_back(q_unit, q_root, back * q_gain).astype(BF)
        back = turn(jnp.concatenate(g_k, axis=0) * scale, cosine, -sine)
        k_sum = k_sum + jnp.sum(back * k_unit, axis=0, keepdims=True)
        pieces[q_here + kv] = unit_back(k_unit, k_root, back * k_gain).astype(BF)
        pieces[q_here + kv_here + kv] = jnp.concatenate(g_v, axis=0).astype(BF)
    g_qkv = jnp.concatenate([pieces[index] for index in range(q_here + 2 * kv_here)], axis=1)
    g_qkv_ref[...] = g_qkv
    own_ref[...] = right_tmul(g_qkv[:rows], w_qkv_ref[...]).astype(BF)
    away_ref[...] = right_tmul(g_qkv[rows:], w_qkv_ref[...]).astype(BF)
    gains_ref[...] = jnp.concatenate([q_sum, k_sum], axis=0)


def in_vmem(count):
    return [pl.BlockSpec(memory_space=pltpu.VMEM)] * count


def attention(here, other, extras, w_qkv, w_out, q_here, kv_here):
    rows, width = here.shape
    wide = w_qkv.shape[1]
    return pl.pallas_call(
        functools.partial(attention_kernel, q_here, kv_here),
        in_specs=in_vmem(11),
        out_specs=in_vmem(5),
        out_shape=[
            jax.ShapeDtypeStruct((2 * rows, width), BF),
            jax.ShapeDtypeStruct((2 * rows, wide), F32),
            jax.ShapeDtypeStruct((2 * rows, q_here * HD), BF),
            jax.ShapeDtypeStruct((rows, width), BF),
            jax.ShapeDtypeStruct((rows, width), BF),
        ],
        compiler_params=pltpu.CompilerParams(vmem_limit_bytes=ATTENTION_BYTES),
        cost_estimate=pl.CostEstimate(
            flops=16 * rows * width * wide, bytes_accessed=40 * rows * width, transcendentals=0
        ),
        name="attention",
    )(here, other, *extras, w_qkv, w_out)


def attention_back(here, other, qkv, extras, w_qkv, w_out, q_here, kv_here):
    rows, width = here.shape
    wide = w_qkv.shape[1]
    return pl.pallas_call(
        functools.partial(attention_back_kernel, q_here, kv_here),
        in_specs=in_vmem(11),
        out_specs=in_vmem(5),
        out_shape=[
            jax.ShapeDtypeStruct((2 * rows, width), BF),
            jax.ShapeDtypeStruct((2 * rows, wide), BF),
            jax.ShapeDtypeStruct((rows, width), BF),
            jax.ShapeDtypeStruct((rows, width), BF),
            jax.ShapeDtypeStruct((2, HD), F32),
        ],
        compiler_params=pltpu.CompilerParams(vmem_limit_bytes=ATTENTION_BYTES),
        cost_estimate=pl.CostEstimate(
            flops=16 * rows * width * wide, bytes_accessed=40 * rows * width, transcendentals=0
        ),
        name="attention_back",
    )(here, other, qkv, *extras, w_qkv, w_out)


def place_kernel(starts, widths, row_ref, column_ref, *refs):
    source_refs, out_refs = refs[: len(starts)], refs[len(starts) :]
    step = pl.program_id(0)
    ends = [*starts[1:], pl.num_programs(0)]
    for source_ref, start, end in zip(source_refs, starts, ends):

        @pl.when((step >= start) & (step < end))
        def _(source_ref=source_ref):
            first = 0
            for width, out_ref in zip(widths, out_refs):
                block = source_ref[0, :, first : first + width].astype(out_ref.dtype)
                out_ref[...] = block.reshape(out_ref.shape)
                first += width


def place_blocks(sources, row_blocks, column_blocks, row_count, column_count, widths, dtype, rows):
    columns = sources[0].shape[2]
    counts = [source.shape[0] for source in sources]
    starts = [sum(counts[:index]) for index in range(len(counts))]

    def source_spec(start, count):
        return pl.BlockSpec(
            (1, rows, columns),
            lambda step, row, column: (jnp.clip(step - start, 0, count - 1), 0, 0),
        )

    if column_count > 1 and any(width % 128 for width in widths):
        widths = [columns]
        shapes = [(column_count, row_count * rows, columns)]
        out_specs = [
            pl.BlockSpec((1, rows, columns), lambda step, row, column: (column[step], row[step], 0))
        ]
    else:
        shapes = [(row_count * rows, column_count * width) for width in widths]
        out_specs = [
            pl.BlockSpec((rows, width), lambda step, row, column: (row[step], column[step]))
            for width in widths
        ]
    return pl.pallas_call(
        functools.partial(place_kernel, starts, widths),
        grid_spec=pltpu.PrefetchScalarGridSpec(
            num_scalar_prefetch=2,
            grid=(sum(counts),),
            in_specs=[source_spec(start, count) for start, count in zip(starts, counts)],
            out_specs=out_specs,
        ),
        out_shape=[jax.ShapeDtypeStruct(shape, dtype) for shape in shapes],
        compiler_params=pltpu.CompilerParams(vmem_limit_bytes=PLACE_BYTES),
        name="place_blocks",
    )(row_blocks.astype(jnp.int32), column_blocks.astype(jnp.int32), *sources)


def after(values, *others):
    return lax.optimization_barrier((values, *others))[0]


def move(values, send):
    ranks, copies = lax.axis_size("fsdp"), lax.axis_size("rep")
    pairs = []
    for f in range(ranks):
        for r in range(copies):
            to = send(f, r)
            if to is not None:
                pairs.append((f * copies + r, to[0] * copies + to[1]))
    return lax.ppermute(values, ("fsdp", "rep"), pairs)


def ring(values, step):
    ranks = lax.axis_size("fsdp")
    return move(values, lambda f, r: ((f + 2 * step) % ranks, r))


def swap_core(values):
    return move(values, lambda f, r: (f, r ^ 1))


def swap_x(values):
    return move(values, lambda f, r: (f, r ^ 2))


def swap_twin(values):
    return move(values, lambda f, r: (f ^ 1, r ^ 1))


def place():
    f, r = lax.axis_index("fsdp"), lax.axis_index("rep")
    return f // 2, f % 2, r // 2, r % 2


def pick(values, index, axis=0):
    return lax.dynamic_index_in_dim(values, index, axis, keepdims=False)


def ordered(slots, z):
    depth = len(slots)
    out = jnp.zeros((depth, *slots[0].shape), slots[0].dtype)
    for k, slot in enumerate(slots):
        out = lax.dynamic_update_index_in_dim(out, slot, (z - k) % depth, 0)
    return out


def add(left, right):
    return (left.astype(F32) + right.astype(F32)).astype(BF)


def gather_group(values, name):
    slots = []
    for s in range(lax.axis_size("fsdp") // 2):
        with jax.named_scope(f"gather_{name}_{s}"):
            if s > 0:
                values = ring(values, 1)
            slots.append((values, swap_core(values)))
    return slots


def scatter_group(partial, name, beside=None):
    moving = None
    for step, (own, away) in enumerate((*partial[1:], partial[0])):
        with jax.named_scope(f"scatter_{name}_{step}"):
            total = own.astype(F32) + swap_core(away).astype(F32)
            if moving is not None:
                total = total + ring(moving, 1).astype(F32)
            moving = total.astype(BF)
        if beside is not None:
            beside(step, moving)
    return total


def total_sum(values):
    for bit in range(2):
        values = values + move(values, lambda f, r: (f, r ^ (1 << bit)))
    for bit in range((lax.axis_size("fsdp") - 1).bit_length()):
        values = values + move(values, lambda f, r: (f ^ (1 << bit), r))
    return values


def columns_in(cut, rows, y_first, name):
    z, y, x, core = place()
    depth = lax.axis_size("fsdp") // 2
    slots = []
    with jax.named_scope(f"{name}_along_z"):
        for k in range(depth):
            part = cut(2 * ((z + k) % depth) + (y ^ core))
            slots.append(ring(part, k) if k else part)
        same = jnp.stack(slots)
    with jax.named_scope(f"{name}_across"):
        across_x, across_y = swap_x(same), swap_twin(same)
    with jax.named_scope(f"{name}_across_both"):
        rest = swap_x(across_y) if y_first else swap_twin(across_x)
    where_z = (z - jnp.arange(depth)) % depth
    index = lambda yy, xx: (where_z * 2 + yy) * 2 + xx
    places = [index(y, x), index(y, 1 - x), index(1 - y, x), index(1 - y, 1 - x)]
    places = jnp.concatenate(places)
    sources = [same, across_x, across_y, rest]
    joined = place_blocks(sources, places, jnp.zeros_like(places), 4 * depth, 1, [same.shape[2]], BF, rows)[0]
    return joined, same, across_y


def scoped(step):
    def wrap(method):
        def named(self):
            with jax.named_scope(f"{self.name}_{step}"):
                return method(self)

        return named

    return wrap


class ColumnsOut:
    def __init__(self, grad, y_first, name):
        self.name = name
        z, y, x, core = place()
        self.depth = lax.axis_size("fsdp") // 2
        self.y_first = y_first
        columns = grad.shape[1]
        self.blocks = grad.reshape(self.depth, 2, 2, -1, columns)
        axis, index = (1, 1 - y) if y_first else (2, 1 - x)
        self.payload = pick(self.blocks, index, axis)

    @scoped("first")
    def first(self):
        z, y, x, core = place()
        axis, index = (1, y) if self.y_first else (2, x)
        swap = swap_twin if self.y_first else swap_x
        came, own = swap(self.payload), pick(self.blocks, index, axis)
        here, there = (x, 1 - x) if self.y_first else (y, 1 - y)
        self.payload = add(pick(own, there, 1), pick(came, there, 1))
        self.kept = (pick(own, here, 1), pick(came, here, 1))

    @scoped("second")
    def second(self):
        z, y, x, core = place()
        swap = swap_x if self.y_first else swap_twin
        came = swap(self.payload).astype(F32)
        total = (self.kept[0].astype(F32) + self.kept[1].astype(F32) + came).astype(BF)
        self.payload = [pick(total, (z + k) % self.depth) for k in range(self.depth)]

    @scoped("third")
    def third(self):
        slots = [ring(part, k) if k else part for k, part in enumerate(self.payload)]
        self.payload = jnp.stack(slots)

    @scoped("last")
    def last(self):
        same = self.payload
        across = swap_x(same)
        return same, across, swap_core(same), swap_core(across)


def columns_placed(parts, widths):
    z, y, x, core = place()
    depth = parts[0].shape[0]
    ones = jnp.ones((depth,), jnp.int32)
    rows = jnp.concatenate([x * ones, (1 - x) * ones] * 2)
    where_z = (z - jnp.arange(depth)) % depth
    own, other = 2 * where_z + (y ^ core), 2 * where_z + (1 - (y ^ core))
    columns = jnp.concatenate([own, own, other, other])
    return place_blocks(parts, rows, columns, 2, 2 * depth, widths, F32, parts[0].shape[1])


def rows_here(weights):
    z, y, x, core = place()
    halves = [weight.shape[0] // 2 for weight in weights]
    parts = [lax.dynamic_slice_in_dim(w, x * half, half, axis=0) for w, half in zip(weights, halves)]
    part = jnp.concatenate(parts, axis=0)
    with jax.named_scope("w_down_across"):
        part = move(part, lambda f, r: (f ^ 1, r) if r % 2 else None)
        other = move(part, lambda f, r: (f, r ^ 2) if r % 2 else None)
    out, first = [], 0
    for weight, half in zip(weights, halves):
        mine, its = part[first : first + half], other[first : first + half]
        low = jnp.where(core == 0, weight[:half], jnp.where(x == 0, mine, its))
        high = jnp.where(core == 0, weight[half:], jnp.where(x == 0, its, mine))
        out.append(jnp.concatenate([low, high], axis=0))
        first += half
    return out


class RowsOut:
    def __init__(self, grad, name):
        self.name = name
        self.grad = self.payload = grad

    @scoped("first")
    def first(self):
        z, y, x, core = place()
        came = move(self.payload, lambda f, r: (f ^ 1, r ^ 1) if r % 2 else None)
        half = self.grad.shape[0] // 2
        part = lambda array, index: lax.dynamic_slice_in_dim(array, index * half, half, axis=0)
        self.payload = add(part(self.grad, 1 - x), part(came, 1 - x))
        self.kept = (part(self.grad, x), part(came, x))

    @scoped("second")
    def second(self):
        came = move(self.payload, lambda f, r: None if r % 2 else (f, r ^ 2)).astype(F32)
        self.payload = (self.kept[0].astype(F32) + self.kept[1].astype(F32) + came).astype(BF)

    @scoped("third")
    def third(self):
        came = move(self.payload, lambda f, r: None if r % 2 else (f, r ^ 2))
        self.payload = jnp.stack([self.payload, came])

    @scoped("last")
    def last(self):
        z, y, x, core = place()
        came = move(self.payload, lambda f, r: None if r % 2 else (f, r ^ 1))
        parts = jnp.where(core == 0, self.payload, came)
        places = jnp.stack([x, 1 - x])
        rows, columns = parts.shape[1:]
        return place_blocks([parts], places, jnp.zeros_like(places), 2, 1, [columns], F32, rows)[0]


def local(
    tokens_in,
    segment_ids,
    w_query,
    w_key,
    w_value,
    w_out,
    w_gate,
    w_up,
    w_down,
    gain_attn,
    gain_ffn,
    gain_query,
    gain_key,
    d_out,
):
    ranks = lax.axis_size("fsdp")
    rank = lax.axis_index("fsdp")
    depth = ranks // 2
    z, y, x, core = place()
    width = tokens_in.shape[1]
    pack = segment_ids.shape[1]
    heads = w_query.shape[1] // HD
    kv_heads = w_key.shape[1] // HD
    share = max(1, ranks // kv_heads)
    q_here = heads // ranks
    kv_here = max(1, kv_heads // ranks)
    group = q_here // kv_here
    q_cols, kv_cols = q_here * HD, kv_here * HD
    scale = HD ** (-0.5)

    q_gain = gain_query.astype(F32)[None]
    k_gain = gain_key.astype(F32)[None]

    token_slots = gather_group(tokens_in, "tokens")
    rows_x = w_query.shape[0] // 2
    cut = lambda weight, start, size: lax.dynamic_slice(weight, (x * rows_x, start), (rows_x, size))
    wide = q_cols + 2 * kv_cols
    seg_size = segment_ids.size
    extra = jnp.concatenate([segment_ids.reshape(-1).astype(BF), gain_attn, gain_ffn])
    extra = jnp.pad(extra, (0, 16 * wide - extra.size)).reshape(16, wide)

    def cut_qkv(block):
        kv = block // share * kv_cols
        parts = [cut(w_query, block * q_cols, q_cols), cut(w_key, kv, kv_cols), cut(w_value, kv, kv_cols)]
        return jnp.concatenate([jnp.concatenate(parts, axis=1), extra], axis=0)

    def cutter(weight):
        size = weight.shape[1] // ranks
        return lambda block: cut(weight, block * size, size)

    w_qkv, own_slots, twin_slots = columns_in(cut_qkv, rows_x, False, "w_qkv")
    w_out_here, w_down_here = rows_here((w_out, w_down))
    own_extra = own_slots[:, rows_x:].reshape(depth, -1)
    twin_extra = twin_slots[:, rows_x:].reshape(depth, -1)
    seg_slots = own_extra[:, :seg_size].reshape(depth, 1, -1, pack)
    segments = jnp.concatenate([seg_slots, swap_core(seg_slots)], axis=1).reshape(-1, pack).astype(jnp.int32)
    span = slice(seg_size, seg_size + 2 * gain_attn.size)
    pieces = jnp.stack([own_extra[:, span], twin_extra[:, span]], axis=1)
    pieces = ordered([pieces[k] for k in range(depth)], z).astype(F32)
    pieces = jnp.where(y == 0, pieces, pieces[:, ::-1])
    gains = pieces.reshape(depth, 2, 2, -1).transpose(2, 0, 1, 3).reshape(2, -1)
    attn_gain, ffn_gain = gains[0], gains[1]

    w_gate_here, gate_slots, _ = columns_in(cutter(after(w_gate, token_slots[-1][0])), rows_x, False, "w_gate")
    w_up_here, _, _ = columns_in(cutter(after(w_up, gate_slots)), rows_x, True, "w_up")

    cosine, sine = phases(segments)
    block_rows = tokens_in.shape[0]
    marks = segments + 4 * (jnp.arange(segments.shape[0], dtype=jnp.int32) % (block_rows // pack))[:, None]
    column = marks.reshape(depth, 2 * block_rows, 1)
    row = marks.reshape(depth, 2, 1, block_rows)
    cosine, sine = cosine.reshape(depth, -1, HD), sine.reshape(depth, -1, HD)
    kept, partial = [], []
    for s, (here, other) in enumerate(token_slots):
        extras = (column[s], row[s], cosine[s], sine[s], attn_gain[None], q_gain, k_gain)
        *keep, own, away = attention(here, other, extras, w_qkv, w_out_here, q_here, kv_here)
        kept.append(keep)
        partial.append((own, away))
    tokens = tokens_in.astype(F32)
    unit_tokens, root_tokens = unit_rows(tokens)
    attn_branch = scatter_group(partial, "attn_branch")

    middle = tokens + attn_branch
    unit_middle, root_middle = unit_rows(middle)
    ffn_slots = gather_group((unit_middle * ffn_gain).astype(BF), "ffn_in")
    grad_slots = gather_group(after(d_out, ffn_slots[-1][0]), "d_out")
    glu_kept, back_partial, down_partial = [], [], []
    for pair, grad_pair in zip(ffn_slots, grad_slots):
        ffn_in = jnp.concatenate(pair, axis=0)
        g_ffn = jnp.concatenate(grad_pair, axis=0)
        gate, up = matmul(ffn_in, w_gate_here), matmul(ffn_in, w_up_here)
        sig = jax.nn.sigmoid(gate)
        silu = gate * sig
        hidden = (silu * up).astype(BF)
        g_hidden = right_tmul(g_ffn, w_down_here).astype(BF).astype(F32)
        g_gate = (g_hidden * up * sig * (1 + gate * (1 - sig))).astype(BF)
        g_up = (g_hidden * silu).astype(BF)
        part = (right_tmul(g_gate, w_gate_here) + right_tmul(g_up, w_up_here)).astype(BF)
        back_partial.append((part[:block_rows], part[block_rows:]))
        glu_kept.append((ffn_in, g_ffn, hidden, g_gate, g_up))
    ffn_in, g_ffn, hidden, g_gate, g_up = (jnp.concatenate(items, axis=0) for items in zip(*glu_kept))
    out_steps = {}

    def beside(step, sent):
        if step == 0:
            grad = left_tmul(*after((hidden, g_ffn), sent)).astype(BF)
            name = "down"
            out_steps[name] = RowsOut(grad, "sum_" + name)
        if step == 1:
            grad = left_tmul(*after((ffn_in, g_gate), sent)).astype(BF)
            name = "gate"
            out_steps[name] = ColumnsOut(grad, True, "sum_" + name)
        if step == 2:
            grad = left_tmul(*after((ffn_in, g_up), sent)).astype(BF)
            name = "up"
            out_steps[name] = ColumnsOut(grad, False, "sum_" + name)

    g_ffn_in = scatter_group(back_partial, "g_ffn_in", beside)
    down_steps, gate_steps, up_steps = (out_steps[name] for name in ("down", "gate", "up"))
    g_ffn_in = after(g_ffn_in, down_steps.payload, gate_steps.payload, up_steps.payload)
    ffn_gain_grad = jnp.sum(g_ffn_in * unit_middle, axis=0)
    g_middle = d_out.astype(F32) + unit_back(unit_middle, root_middle, g_ffn_in * ffn_gain)

    attn_slots = gather_group(g_middle.astype(BF), "g_attn")
    down_steps.first()
    up_steps.first()
    back_kept, partial = [None] * depth, [None] * depth
    head_gains = 0.0
    for s in (*range(1, depth), 0):
        here, other = attn_slots[s]
        if s == min(2, depth - 1):
            here = after(here, down_steps.payload, up_steps.payload)
            down_steps.second()
        if s == min(3, depth - 1):
            here = after(here, down_steps.payload)
            gate_steps.first()
            up_steps.second()
            down_steps.third()
        extras = (column[s], row[s], cosine[s], sine[s], q_gain, k_gain)
        g_attn, g_qkv, own, away, gain_part = attention_back(
            here, other, kept[s][1], extras, w_qkv, w_out_here, q_here, kv_here
        )
        head_gains = head_gains + gain_part
        back_kept[s] = (g_attn, g_qkv)
        partial[s] = (own, away)
    attn_in, _, mixed = (jnp.concatenate(items, axis=0) for items in zip(*kept))
    g_attn, g_qkv = (jnp.concatenate(items, axis=0) for items in zip(*back_kept))

    def beside_back(step, sent):
        if step == 0:
            grad = left_tmul(*after((attn_in, g_qkv), sent)).astype(BF)
            name = "qkv"
            out_steps[name] = ColumnsOut(grad, True, "sum_" + name)
        if step == 1:
            grad = left_tmul(*after((mixed, g_attn), sent)).astype(BF)
            name = "out"
            out_steps[name] = RowsOut(grad, "sum_" + name)

    g_attn_in = scatter_group(partial, "g_attn_in", beside_back)
    g_attn_in = after(g_attn_in, gate_steps.payload, up_steps.payload, out_steps["qkv"].payload)
    attn_gain_grad = jnp.sum(g_attn_in * unit_tokens, axis=0)
    d_tokens = g_middle + unit_back(unit_tokens, root_tokens, g_attn_in * attn_gain)

    for s in range(depth):
        part = matmul(after(glu_kept[s][2], attn_slots[-1][0]), w_down_here).astype(BF)
        down_partial.append((part[:block_rows], part[block_rows:]))
    ffn_branch = scatter_group(down_partial, "ffn_branch")
    block = middle + ffn_branch

    qkv_steps, out_proj_steps = out_steps["qkv"], out_steps["out"]
    gate_steps.second()
    for steps in (qkv_steps, out_proj_steps):
        steps.first()
        steps.second()
    for steps in (up_steps, gate_steps, qkv_steps, out_proj_steps):
        steps.third()
    qkv_sum = columns_placed(qkv_steps.last(), [q_cols, 2 * kv_cols])
    if len(qkv_sum) == 2:
        q_sum = qkv_sum[0]
        kv_sum = qkv_sum[1].reshape(q_sum.shape[0], ranks, 2 * kv_cols)
    else:
        rows = qkv_sum[0].transpose(1, 0, 2)
        q_sum = rows[:, :, :q_cols].reshape(rows.shape[0], -1)
        kv_sum = rows[:, :, q_cols:]
    if share > 1:
        kv_sum = kv_sum.reshape(kv_sum.shape[0], -1, share, 2 * kv_cols).sum(axis=2)
    k_sum = kv_sum[:, :, :kv_cols].reshape(kv_sum.shape[0], -1)
    v_sum = kv_sum[:, :, kv_cols:].reshape(kv_sum.shape[0], -1)
    (up_sum,) = columns_placed(up_steps.last(), [w_up_here.shape[1]])
    (gate_sum,) = columns_placed(gate_steps.last(), [w_gate_here.shape[1]])
    out_sum = out_proj_steps.last()
    down_sum = down_steps.last()
    squares = jnp.stack(
        [jnp.sum(item * item) for item in (middle, attn_branch, ffn_branch, block, d_tokens)]
    )
    small = jnp.concatenate([attn_gain_grad, ffn_gain_grad, head_gains[0], head_gains[1], squares])
    with jax.named_scope("total_sum"):
        small = total_sum(small)
    gain_rows = gain_attn.shape[0]
    attn_gain_sum = lax.dynamic_slice(small, (rank * gain_rows,), (gain_rows,))
    ffn_gain_sum = lax.dynamic_slice(small, (width + rank * gain_rows,), (gain_rows,))
    entries = tokens_in.shape[0] * ranks * lax.axis_size("rep") * width
    stats = jnp.sqrt(small[2 * width + 2 * HD :] / entries)
    return (
        block.astype(BF),
        d_tokens.astype(BF),
        q_sum,
        k_sum,
        v_sum,
        out_sum,
        gate_sum,
        up_sum,
        down_sum,
        attn_gain_sum,
        ffn_gain_sum,
        small[2 * width : 2 * width + HD],
        small[2 * width + HD : 2 * width + 2 * HD],
        stats,
    )


def solution(mesh):
    rows = P(("fsdp", "rep"), None)
    weight = P("fsdp", None)
    return jax.shard_map(
        local,
        mesh=mesh,
        in_specs=(rows, rows, *[weight] * 7, P("fsdp"), P("fsdp"), P(), P(), rows),
        out_specs=(rows, rows, *[weight] * 7, P("fsdp"), P("fsdp"), P(), P(), P()),
        check_vma=False,
    )
```

time: 1390 us -> 769 us (0.55)
  waiting for transfers between devices: 840 us -> 337 us
  blocking collectives: 220 us -> 0 us
  starting transfers between devices: 13.5 us -> 139 us
  Pallas kernels: 0 us -> 101 us
  local copies, waits for them, and re-layouts: 122 us -> 66.7 us
  matrix products: 107 us -> 53.5 us
    ppermute x0 -> x114, waiting for transfers between devices: none -> 337 us  [move(): return lax.ppermute(values, ('fsdp', 'rep'), pairs)]
    reduce_scatter x5 -> x0, waiting for transfers between devices: 257 us -> none  [the longest x4 249 us: scatter_rows(): lax.psum_scatter(values.astype(BF), 'fsdp', scatter_dimension=0, tiled=True)]
    psum x1 -> x0, waiting for transfers between devices: 218 us -> none  [local(): out_sum = lax.psum(grad_out.astype(BF), 'rep')]
    all_to_all x3 -> x0, waiting for transfers between devices: 199 us -> none  [rows_to_columns(): return lax.all_to_all(weight, 'fsdp', 1, 0, tiled=True)]
    all_gather x7 -> x0, waiting for transfers between devices: 166 us -> none  [the longest x4 164 us: gather_rows(): return lax.all_gather(values, 'fsdp', axis=0, tiled=True)]
    ppermute x0 -> x114, starting transfers between devices: none -> 139 us  [move(): return lax.ppermute(values, ('fsdp', 'rep'), pairs)]
    all_to_all x3 -> x0, blocking collectives: 104 us -> none  [columns_to_rows(): moved = lax.all_to_all(own, 'fsdp', 0, 0, tiled=True)]
    pallas_call x0 -> x16, Pallas kernels: none -> 101 us  [the longest x8 52.5 us: place_blocks(): pl.pallas_call(functools.partial(place_kernel, starts, widths), grid_spec...]
  transfers between devices with their start and end apart: 16 -> 114, of which waited for: 13 -> 36; matrix products, arithmetic and copies ran while one was open for 11% -> 19% of each run, Pallas kernels for 0% -> 13%
where the time goes in v3:
time: 769 us; the launch traced here: 757 us
  waiting for transfers between devices  337 us (44%)
  starting transfers between devices  139 us (18%)
  Pallas kernels  101 us (13%)
  local copies, waits for them, and re-layouts  66.7 us (9%)
  other arithmetic  56 us (7%)
  matrix products  53.5 us (7%)
    ppermute x114, waiting for transfers between devices, move(): return lax.ppermute(values, ('fsdp', 'rep'), pairs)  337 us
    ppermute x114, starting transfers between devices, move(): return lax.ppermute(values, ('fsdp', 'rep'), pairs)  139 us
    pallas_call x8, Pallas kernels, place_blocks(): pl.pallas_call(functools.partial(place_kernel, starts, widths), grid_spec...  52.5 us
    unnamed x291, local copies, waits for them, and re-layouts  38.8 us
    pallas_call x4, Pallas kernels, attention_back(): pl.pallas_call(functools.partial(attention_back_kernel, q_here, kv_here),...  25.2 us
    pallas_call x4, Pallas kernels, attention(): pl.pallas_call(functools.partial(attention_kernel, q_here, kv_here), in_s...  23.1 us
    dot_general x5, matrix products, left_tmul(): lax.dot_general(left, right, (((0,), (0,)), ((), ())), preferred_element_...  20.8 us
    dot_general x12, matrix products, right_tmul(): lax.dot_general(left, right, (((1,), (1,)), ((), ())), preferred_element_...  16.5 us
  transfers between devices with their start and end apart: 114, of which 36 were waited for; matrix products, arithmetic and copies ran while one was open for 19% of the time, Pallas kernels for 13%

profile of v3, /device:TPU:0, one launch (start us, length us, event | category | flops | bytes accessed | tf_op | source)
XLA Modules:
  0.0 757.4 jit_solution(1455136511230168974)
XLA Ops:
  16.4 10.4 %collective-permute-done.3 = bf16[144,384]{1,0:T(8,128)(2,1)S(1)} collective-permute-done((bf16[144,384]{1,0:T(8,128)(2,1)S(1)}, bf16[144,384]{1,0:T(8,128)(2,1)S(1)}, u32[]{:S(2)}, u32[]{:S(2)}) %collective-permute-start.3) | collective-permute-done | bytes 110624 | tf_op jit(solution)/shard_map/w_qkv_along_z/ppermute | solution.py:262
  53.8 14.4 %collective-permute-done.12.refs_0_ = bf16[128,2048]{1,0:T(8,128)(2,1)} collective-permute-done((bf16[128,2048]{1,0:T(8,128)(2,1)}, bf16[128,2048]{1,0:T(8,128)(2,1)}, u32[]{:S(2)}, u32[]{:S(2)}) %collective-permute-start.12) | collective-permute-done | bytes 524320 | tf_op jit(solution)/shard_map/gather_tokens_2/ppermute | solution.py:262
  70.3 10.5 %collective-permute-done.7.refs_3_ = bf16[4,144,384]{2,1,0:T(8,128)(2,1)S(1)} collective-permute-done((bf16[4,144,384]{2,1,0:T(8,128)(2,1)S(1)}, bf16[4,144,384]{2,1,0:T(8,128)(2,1)S(1)}, u32[]{:S(2)}, u32[]{:S(2)}) %collective-permute-start.7) | collective-permute-done | bytes 442400 | tf_op jit(solution)/shard_map/w_qkv_across_both/ppermute | solution.py:262
  133.8 17.3 %collective-permute-start.20 = (bf16[128,2048]{1,0:T(8,128)(2,1)}, bf16[128,2048]{1,0:T(8,128)(2,1)}, u32[]{:S(2)}, u32[]{:S(2)}) collective-permute-start(bf16[128,2048]{1,0:T(8,128)(2,1)} %add_convert_fusion.15), channel_id=1, source_target_pairs={{0,8},{1,9},{2,10},{3,11},{4,12},{5,13},{6,14},{7,15},{8,16},{9,17... | collective-permute-start | bytes 1572872 | tf_op jit(solution)/shard_map/scatter_attn_branch_1/ppermute | solution.py:262
  203.8 21.2 %collective-permute-done.29.refs_3_ = bf16[4,128,1024]{2,1,0:T(8,128)(2,1)} collective-permute-done((bf16[4,128,1024]{2,1,0:T(8,128)(2,1)}, bf16[4,128,1024]{2,1,0:T(8,128)(2,1)}, u32[]{:S(2)}, u32[]{:S(2)}) %collective-permute-start.29) | collective-permute-done | bytes 1048608 | tf_op jit(solution)/shard_map/w_gate_across_both/ppermute | solution.py:262
  233.0 8.0 %place_blocks.10 = bf16[2048,1024]{1,0:T(8,128)(2,1)S(1)} custom-call(s32[16]{0:T(128)S(1)} %pad_add_fusion.row_ref, s32[16]{0:T(128)S(1)} %jit_remainder_.2.column_ref, bf16[4,128,1024]{2,1,0:T(8,128)(2,1)S(1)} %pad_maximum_fusion.11.refs_0_, bf16[4,128,1024]{2,1,0:T(8,128)(2,1)} %collective-permute-done.33.refs_1_, ...), custom_call_target="tpu_custom_call" | custom-call | tf_op jit(solution)/shard_map/place_blocks/pallas_call | solution.py:236
  246.6 12.4 %collective-permute-done.36 = bf16[128,2048]{1,0:T(8,128)(2,1)S(1)} collective-permute-done((bf16[128,2048]{1,0:T(8,128)(2,1)S(1)}, bf16[128,2048]{1,0:T(8,128)(2,1)S(1)}, u32[]{:S(2)}, u32[]{:S(2)}) %collective-permute-start.36) | collective-permute-done | bytes 524320 | tf_op jit(solution)/shard_map/gather_ffn_in_1/ppermute | solution.py:262
  260.4 12.7 %collective-permute-done.37 = bf16[128,2048]{1,0:T(8,128)(2,1)S(1)} collective-permute-done((bf16[128,2048]{1,0:T(8,128)(2,1)S(1)}, bf16[128,2048]{1,0:T(8,128)(2,1)S(1)}, u32[]{:S(2)}, u32[]{:S(2)}) %collective-permute-start.37) | collective-permute-done | bytes 524320 | tf_op jit(solution)/shard_map/gather_ffn_in_2/ppermute | solution.py:262
  274.5 11.7 %collective-permute-done.38 = bf16[128,2048]{1,0:T(8,128)(2,1)S(1)} collective-permute-done((bf16[128,2048]{1,0:T(8,128)(2,1)S(1)}, bf16[128,2048]{1,0:T(8,128)(2,1)S(1)}, u32[]{:S(2)}, u32[]{:S(2)}) %collective-permute-start.38) | collective-permute-done | bytes 524320 | tf_op jit(solution)/shard_map/gather_ffn_in_3/ppermute | solution.py:262
  325.1 9.1 %collective-permute-done.43 = bf16[128,2048]{1,0:T(8,128)(2,1)S(1)} collective-permute-done((bf16[128,2048]{1,0:T(8,128)(2,1)S(1)}, bf16[128,2048]{1,0:T(8,128)(2,1)S(1)}, u32[]{:S(2)}, u32[]{:S(2)}) %collective-permute-start.43) | collective-permute-done | bytes 524320 | tf_op jit(solution)/shard_map/gather_d_out_3/ppermute | solution.py:262
  335.9 9.2 %collective-permute-done.53 = bf16[128,2048]{1,0:T(8,128)(2,1)S(1)} collective-permute-done((bf16[128,2048]{1,0:T(8,128)(2,1)S(1)}, bf16[128,2048]{1,0:T(8,128)(2,1)S(1)}, u32[]{:S(2)}, u32[]{:S(2)}) %collective-permute-start.53) | collective-permute-done | bytes 524320 | tf_op jit(solution)/shard_map/scatter_g_ffn_in_1/ppermute | solution.py:262
  377.4 8.4 %collective-permute-done.55 = bf16[128,2048]{1,0:T(8,128)(2,1)S(1)} collective-permute-done((bf16[128,2048]{1,0:T(8,128)(2,1)S(1)}, bf16[128,2048]{1,0:T(8,128)(2,1)S(1)}, u32[]{:S(2)}, u32[]{:S(2)}) %collective-permute-start.55) | collective-permute-done | bytes 524320 | tf_op jit(solution)/shard_map/scatter_g_ffn_in_3/ppermute | solution.py:262
  388.4 14.4 %collective-permute-done.56.refs_0_ = bf16[128,2048]{1,0:T(8,128)(2,1)} collective-permute-done((bf16[128,2048]{1,0:T(8,128)(2,1)S(1)}, bf16[128,2048]{1,0:T(8,128)(2,1)}, u32[]{:S(2)}, u32[]{:S(2)}) %collective-permute-start.56) | collective-permute-done | bytes 524320 | tf_op jit(solution)/shard_map/gather_g_attn_1/ppermute | solution.py:262
  405.1 12.8 %collective-permute-done.57.refs_0_ = bf16[128,2048]{1,0:T(8,128)(2,1)S(1)} collective-permute-done((bf16[128,2048]{1,0:T(8,128)(2,1)}, bf16[128,2048]{1,0:T(8,128)(2,1)S(1)}, u32[]{:S(2)}, u32[]{:S(2)}) %collective-permute-start.57) | collective-permute-done | bytes 524320 | tf_op jit(solution)/shard_map/gather_g_attn_2/ppermute | solution.py:262
  453.9 22.5 %collective-permute-done.81 = bf16[4,128,1024]{2,1,0:T(8,128)(2,1)S(1)} collective-permute-done((bf16[4,128,1024]{2,1,0:T(8,128)(2,1)S(1)}, bf16[4,128,1024]{2,1,0:T(8,128)(2,1)S(1)}, u32[]{:S(2)}, u32[]{:S(2)}) %collective-permute-start.81) | collective-permute-done | bytes 1048608 | tf_op jit(solution)/shard_map/sum_up_second/ppermute | solution.py:262
  483.4 9.6 %collective-permute-done.63 = bf16[128,2048]{1,0:T(8,128)(2,1)S(1)} collective-permute-done((bf16[128,2048]{1,0:T(8,128)(2,1)S(1)}, bf16[128,2048]{1,0:T(8,128)(2,1)S(1)}, u32[]{:S(2)}, u32[]{:S(2)}) %collective-permute-start.63) | collective-permute-done | bytes 524320 | tf_op jit(solution)/shard_map/scatter_ffn_branch_1/ppermute | solution.py:262
  505.7 9.0 %collective-permute-done.96 = bf16[128,1024]{1,0:T(8,128)(2,1)S(1)} collective-permute-done((bf16[128,1024]{1,0:T(8,128)(2,1)}, bf16[128,1024]{1,0:T(8,128)(2,1)S(1)}, u32[]{:S(2)}, u32[]{:S(2)}) %collective-permute-start.96) | collective-permute-done | bytes 262176 | tf_op jit(solution)/shard_map/sum_gate_third/ppermute | solution.py:262
  519.1 24.2 %collective-permute-start.101 = (bf16[128,1024]{1,0:T(8,128)(2,1)S(1)}, bf16[128,1024]{1,0:T(8,128)(2,1)S(1)}, u32[]{:S(2)}, u32[]{:S(2)}) collective-permute-start(bf16[128,1024]{1,0:T(8,128)(2,1)S(1)} %get-tuple-element.240), channel_id=1, source_target_pairs={{0,8},{1,9},{2,10},{3,11},{4,12},{5,13},{6,14},{7,15},{8,16},{9,17... | collective-permute-start | bytes 786440 | tf_op jit(solution)/shard_map/sum_up_third/ppermute | solution.py:262
  550.4 14.1 %collective-permute-done.77 = bf16[128,2048]{1,0:T(8,128)(2,1)S(1)} collective-permute-done((bf16[128,2048]{1,0:T(8,128)(2,1)S(1)}, bf16[128,2048]{1,0:T(8,128)(2,1)S(1)}, u32[]{:S(2)}, u32[]{:S(2)}) %collective-permute-start.77) | collective-permute-done | bytes 524320 | tf_op jit(solution)/shard_map/scatter_g_attn_in_1/ppermute | solution.py:262
  584.7 23.9 %collective-permute-done.79 = bf16[128,2048]{1,0:T(8,128)(2,1)S(1)} collective-permute-done((bf16[128,2048]{1,0:T(8,128)(2,1)S(1)}, bf16[128,2048]{1,0:T(8,128)(2,1)S(1)}, u32[]{:S(2)}, u32[]{:S(2)}) %collective-permute-start.79) | collective-permute-done | bytes 524320 | tf_op jit(solution)/shard_map/scatter_g_attn_in_3/ppermute | solution.py:262
  630.2 36.9 %collective-permute-done.83 = bf16[4,128,384]{2,1,0:T(8,128)(2,1)S(1)} collective-permute-done((bf16[4,128,384]{2,1,0:T(8,128)(2,1)S(1)}, bf16[4,128,384]{2,1,0:T(8,128)(2,1)S(1)}, u32[]{:S(2)}, u32[]{:S(2)}) %collective-permute-start.83) | collective-permute-done | bytes 393248 | tf_op jit(solution)/shard_map/sum_qkv_second/ppermute | solution.py:262
  694.6 10.4 %collective-permute-done.92 = bf16[128,2048]{1,0:T(8,128)(2,1)} collective-permute-done((bf16[128,2048]{1,0:T(8,128)(2,1)S(1)}, bf16[128,2048]{1,0:T(8,128)(2,1)}, u32[]{:S(2)}, u32[]{:S(2)}) %collective-permute-start.92) | collective-permute-done | bytes 524320 | tf_op jit(solution)/shard_map/sum_out_third/ppermute | solution.py:262
  711.3 11.5 %place_blocks.13 = f32[256,8192]{1,0:T(8,128)} custom-call(s32[16]{0:T(128)S(1)} %pad_add_fusion.1.row_ref, s32[16]{0:T(128)S(1)} %pad_add_fusion.2.column_ref, bf16[4,128,1024]{2,1,0:T(8,128)(2,1)S(1)} %pad_maximum_fusion.13.refs_0_, bf16[4,128,1024]{2,1,0:T(8,128)(2,1)} %collective-permute-done.98.refs_1_, ...), custom_call_target="tpu_custom_call" | custom-call | tf_op jit(solution)/shard_map/place_blocks/pallas_call | solution.py:236
  722.7 11.5 %place_blocks.14 = f32[256,8192]{1,0:T(8,128)} custom-call(s32[16]{0:T(128)S(1)} %pad_add_fusion.1.row_ref, s32[16]{0:T(128)S(1)} %pad_add_fusion.2.column_ref, bf16[4,128,1024]{2,1,0:T(8,128)(2,1)S(1)} %pad_maximum_fusion.14.refs_0_, bf16[4,128,1024]{2,1,0:T(8,128)(2,1)} %collective-permute-done.104.refs_1_, ...), custom_call_target="tpu_custom_call" | custom-call | tf_op jit(solution)/shard_map/place_blocks/pallas_call | solution.py:236
  (682 shorter events, 407.8 us)
Async XLA Ops:
  37.1 55.6 %collective-permute-start.9 = (bf16[640,2048]{1,0:T(8,128)(2,1)}, bf16[640,2048]{1,0:T(8,128)(2,1)}, u32[]{:S(2)}, u32[]{:S(2)}) collective-permute-start(bf16[640,2048]{1,0:T(8,128)(2,1)} %collective-permute-done.8), channel_id=1, source_target_pairs={{1,3},{3,1},{5,7},{7,5},{9,11},{11,9},{13,15},{15,13},{17,19},{19,... | collective-permute-start | bytes 7864328 | tf_op jit(solution)/shard_map/w_down_across/ppermute | solution.py:262
  45.1 49.8 %collective-permute-start.18 = (bf16[128,2048]{1,0:T(8,128)(2,1)}, bf16[128,2048]{1,0:T(8,128)(2,1)}, u32[]{:S(2)}, u32[]{:S(2)}) collective-permute-start(bf16[128,2048]{1,0:T(8,128)(2,1)} %collective-permute-done.11.refs_0_), channel_id=1, source_target_pairs={{0,1},{1,0},{2,3},{3,2},{4,5},{5,4},{6,7},{7,6},{8,9},{9,8},{10,11... | collective-permute-start | bytes 1572872 | tf_op jit(solution)/shard_map/gather_tokens_1/ppermute | solution.py:262
  106.7 50.1 %collective-permute-start.14 = (bf16[128,2048]{1,0:T(8,128)(2,1)}, bf16[128,2048]{1,0:T(8,128)(2,1)}, u32[]{:S(2)}, u32[]{:S(2)}) collective-permute-start(bf16[128,2048]{1,0:T(8,128)(2,1)} %collective-permute-done.13.refs_0_), channel_id=1, source_target_pairs={{0,1},{1,0},{2,3},{3,2},{4,5},{5,4},{6,7},{7,6},{8,9},{9,8},{10,11... | collective-permute-start | bytes 1572872 | tf_op jit(solution)/shard_map/gather_tokens_3/ppermute | solution.py:262
  178.2 54.8 %collective-permute-start.33 = (bf16[4,128,1024]{2,1,0:T(8,128)(2,1)S(1)}, bf16[4,128,1024]{2,1,0:T(8,128)(2,1)}, u32[]{:S(2)}, u32[]{:S(2)}) collective-permute-start(bf16[4,128,1024]{2,1,0:T(8,128)(2,1)S(1)} %pad_maximum_fusion.11.refs_0_), channel_id=1, source_target_pairs={{0,2},{1,3},{2,0},{3,1},{4,6},{5,7},{6,4},{7,5},{8,10},{9,11},{10,... | collective-permute-start | bytes 3145736 | tf_op jit(solution)/shard_map/w_up_across/ppermute | solution.py:262
  180.8 44.2 %collective-permute-start.29 = (bf16[4,128,1024]{2,1,0:T(8,128)(2,1)}, bf16[4,128,1024]{2,1,0:T(8,128)(2,1)}, u32[]{:S(2)}, u32[]{:S(2)}) collective-permute-start(bf16[4,128,1024]{2,1,0:T(8,128)(2,1)} %collective-permute-done.27.refs_1_), channel_id=1, source_target_pairs={{0,5},{1,4},{2,7},{3,6},{4,1},{5,0},{6,3},{7,2},{8,13},{9,12},{10,... | collective-permute-start | bytes 3145736 | tf_op jit(solution)/shard_map/w_gate_across_both/ppermute | solution.py:262
  181.0 52.0 %collective-permute-start.35 = (bf16[4,128,1024]{2,1,0:T(8,128)(2,1)}, bf16[4,128,1024]{2,1,0:T(8,128)(2,1)}, u32[]{:S(2)}, u32[]{:S(2)}) collective-permute-start(bf16[4,128,1024]{2,1,0:T(8,128)(2,1)} %collective-permute-done.34.refs_2_), channel_id=1, source_target_pairs={{0,2},{1,3},{2,0},{3,1},{4,6},{5,7},{6,4},{7,5},{8,10},{9,11},{10,... | collective-permute-start | bytes 3145736 | tf_op jit(solution)/shard_map/w_up_across_both/ppermute | solution.py:262
  195.8 45.3 %collective-permute-start.10 = (bf16[128,2048]{1,0:T(8,128)(2,1)}, bf16[128,2048]{1,0:T(8,128)(2,1)}, u32[]{:S(2)}, u32[]{:S(2)}) collective-permute-start(bf16[128,2048]{1,0:T(8,128)(2,1)} %get-tuple-element.78), channel_id=1, source_target_pairs={{0,1},{1,0},{2,3},{3,2},{4,5},{5,4},{6,7},{7,6},{8,9},{9,8},{10,11... | collective-permute-start | bytes 1572872 | tf_op jit(solution)/shard_map/scatter_attn_branch_3/ppermute | solution.py:262
  301.2 76.2 %collective-permute-start.40 = (bf16[128,2048]{1,0:T(8,128)(2,1)S(1)}, bf16[128,2048]{1,0:T(8,128)(2,1)S(1)}, u32[]{:S(2)}, u32[]{:S(2)}) collective-permute-start(bf16[128,2048]{1,0:T(8,128)(2,1)S(1)} %slice.291), channel_id=1, source_target_pairs={{0,1},{1,0},{2,3},{3,2},{4,5},{5,4},{6,7},{7,6},{8,9},{9,8},{10,11... | collective-permute-start | bytes 1572872 | tf_op jit(solution)/shard_map/scatter_g_ffn_in_3/ppermute | solution.py:262
  359.2 65.9 %collective-permute-start.80 = (bf16[4,2,128,1024]{3,2,0,1:T(8,128)(2,1)}, bf16[4,2,128,1024]{3,2,0,1:T(8,128)(2,1)}, u32[]{:S(2)}, u32[]{:S(2)}) collective-permute-start(bf16[4,2,128,1024]{3,2,0,1:T(8,128)(2,1)} %copy_bitcast_fusion.1), channel_id=1, source_target_pairs={{0,5},{1,4},{2,7},{3,6},{4,1},{5,0},{6,3},{7,2},{8,13},{9,12},{10,... | collective-permute-start | bytes 6291464 | tf_op jit(solution)/shard_map/sum_gate_first/ppermute | solution.py:262
  375.9 59.6 %collective-permute-start.72 = (bf16[4,2,128,1024]{3,2,0,1:T(8,128)(2,1)}, bf16[4,2,128,1024]{3,2,0,1:T(8,128)(2,1)}, u32[]{:S(2)}, u32[]{:S(2)}) collective-permute-start(bf16[4,2,128,1024]{3,2,0,1:T(8,128)(2,1)} %copy_bitcast_fusion), channel_id=1, source_target_pairs={{0,2},{1,3},{2,0},{3,1},{4,6},{5,7},{6,4},{7,5},{8,10},{9,11},{10,... | collective-permute-start | bytes 6291464 | tf_op jit(solution)/shard_map/sum_up_first/ppermute | solution.py:262
  387.1 91.2 %collective-permute-start.68 = (bf16[1024,2048]{1,0:T(8,128)(2,1)}, bf16[1024,2048]{1,0:T(8,128)(2,1)S(1)}, u32[]{:S(2)}, u32[]{:S(2)}) collective-permute-start(bf16[1024,2048]{1,0:T(8,128)(2,1)} %convolution_convert_fusion.2), channel_id=1, source_target_pairs={{1,4},{3,6},{5,0},{7,2},{9,12},{11,14},{13,8},{15,10},{17,20},{19,... | collective-permute-start | bytes 12582920 | tf_op jit(solution)/shard_map/sum_down_first/ppermute | solution.py:262
  435.6 62.2 %collective-permute-start.73 = (bf16[128,2048]{1,0:T(8,128)(2,1)S(1)}, bf16[128,2048]{1,0:T(8,128)(2,1)S(1)}, u32[]{:S(2)}, u32[]{:S(2)}) collective-permute-start(bf16[128,2048]{1,0:T(8,128)(2,1)S(1)} %collective-permute-done.57.refs_0_), channel_id=1, source_target_pairs={{0,1},{1,0},{2,3},{3,2},{4,5},{5,4},{6,7},{7,6},{8,9},{9,8},{10,11... | collective-permute-start | bytes 1572872 | tf_op jit(solution)/shard_map/gather_g_attn_2/ppermute | solution.py:262
  437.7 38.6 %collective-permute-start.81 = (bf16[4,128,1024]{2,1,0:T(8,128)(2,1)S(1)}, bf16[4,128,1024]{2,1,0:T(8,128)(2,1)S(1)}, u32[]{:S(2)}, u32[]{:S(2)}) collective-permute-start(bf16[4,128,1024]{2,1,0:T(8,128)(2,1)S(1)} %fusion.9), channel_id=1, source_target_pairs={{0,5},{1,4},{2,7},{3,6},{4,1},{5,0},{6,3},{7,2},{8,13},{9,12},{10,... | collective-permute-start | bytes 3145736 | tf_op jit(solution)/shard_map/sum_up_second/ppermute | solution.py:262
  453.2 96.3 %collective-permute-start.60 = (bf16[128,2048]{1,0:T(8,128)(2,1)}, bf16[128,2048]{1,0:T(8,128)(2,1)S(1)}, u32[]{:S(2)}, u32[]{:S(2)}) collective-permute-start(bf16[128,2048]{1,0:T(8,128)(2,1)} %slice.301), channel_id=1, source_target_pairs={{0,1},{1,0},{2,3},{3,2},{4,5},{5,4},{6,7},{7,6},{8,9},{9,8},{10,11... | collective-permute-start | bytes 1572872 | tf_op jit(solution)/shard_map/scatter_ffn_branch_2/ppermute | solution.py:262
  493.1 72.6 %collective-permute-start.69 = (bf16[512,2048]{1,0:T(8,128)(2,1)S(1)}, bf16[512,2048]{1,0:T(8,128)(2,1)S(1)}, u32[]{:S(2)}, u32[]{:S(2)}) collective-permute-start(bf16[512,2048]{1,0:T(8,128)(2,1)S(1)} %add_convert_fusion.1), channel_id=1, source_target_pairs={{0,2},{2,0},{4,6},{6,4},{8,10},{10,8},{12,14},{14,12},{16,18},{18,... | collective-permute-start | bytes 6291464 | tf_op jit(solution)/shard_map/sum_down_second/ppermute | solution.py:262
  550.1 64.4 %collective-permute-start.59 = (bf16[128,2048]{1,0:T(8,128)(2,1)S(1)}, bf16[128,2048]{1,0:T(8,128)(2,1)S(1)}, u32[]{:S(2)}, u32[]{:S(2)}) collective-permute-start(bf16[128,2048]{1,0:T(8,128)(2,1)S(1)} %slice.299), channel_id=1, source_target_pairs={{0,1},{1,0},{2,3},{3,2},{4,5},{5,4},{6,7},{7,6},{8,9},{9,8},{10,11... | collective-permute-start | bytes 1572872 | tf_op jit(solution)/shard_map/scatter_ffn_branch_3/ppermute | solution.py:262
  567.1 43.4 %collective-permute-start.107 = (bf16[512,2048]{1,0:T(8,128)(2,1)S(1)}, bf16[512,2048]{1,0:T(8,128)(2,1)S(1)}, u32[]{:S(2)}, u32[]{:S(2)}) collective-permute-start(bf16[512,2048]{1,0:T(8,128)(2,1)S(1)} %add_convert_fusion), channel_id=1, source_target_pairs={{0,2},{2,0},{4,6},{6,4},{8,10},{10,8},{12,14},{14,12},{16,18},{18,... | collective-permute-start | bytes 6291464 | tf_op jit(solution)/shard_map/sum_down_third/ppermute | solution.py:262
  610.5 61.3 %collective-permute-start.98 = (bf16[4,128,1024]{2,1,0:T(8,128)(2,1)S(1)}, bf16[4,128,1024]{2,1,0:T(8,128)(2,1)}, u32[]{:S(2)}, u32[]{:S(2)}) collective-permute-start(bf16[4,128,1024]{2,1,0:T(8,128)(2,1)S(1)} %pad_maximum_fusion.13.refs_0_), channel_id=1, source_target_pairs={{0,2},{1,3},{2,0},{3,1},{4,6},{5,7},{6,4},{7,5},{8,10},{9,11},{10,... | collective-permute-start | bytes 3145736 | tf_op jit(solution)/shard_map/sum_gate_last/ppermute | solution.py:262
  614.5 58.0 %collective-permute-start.99 = (bf16[4,128,1024]{2,1,0:T(8,128)(2,1)S(1)}, bf16[4,128,1024]{2,1,0:T(8,128)(2,1)}, u32[]{:S(2)}, u32[]{:S(2)}) collective-permute-start(bf16[4,128,1024]{2,1,0:T(8,128)(2,1)S(1)} %pad_maximum_fusion.13.refs_0_), channel_id=1, source_target_pairs={{0,1},{1,0},{2,3},{3,2},{4,5},{5,4},{6,7},{7,6},{8,9},{9,8},{10,11... | collective-permute-start | bytes 3145736 | tf_op jit(solution)/shard_map/sum_gate_last/ppermute | solution.py:262
  615.6 62.8 %collective-permute-start.104 = (bf16[4,128,1024]{2,1,0:T(8,128)(2,1)S(1)}, bf16[4,128,1024]{2,1,0:T(8,128)(2,1)}, u32[]{:S(2)}, u32[]{:S(2)}) collective-permute-start(bf16[4,128,1024]{2,1,0:T(8,128)(2,1)S(1)} %pad_maximum_fusion.14.refs_0_), channel_id=1, source_target_pairs={{0,2},{1,3},{2,0},{3,1},{4,6},{5,7},{6,4},{7,5},{8,10},{9,11},{10,... | collective-permute-start | bytes 3145736 | tf_op jit(solution)/shard_map/sum_up_last/ppermute | solution.py:262
  616.5 135.8 %collective-permute-start.108 = (bf16[2,512,2048]{2,1,0:T(8,128)(2,1)}, bf16[2,512,2048]{2,1,0:T(8,128)(2,1)}, u32[]{:S(2)}, u32[]{:S(2)}) collective-permute-start(bf16[2,512,2048]{2,1,0:T(8,128)(2,1)} %pad_maximum_fusion.3), channel_id=1, source_target_pairs={{0,1},{2,3},{4,5},{6,7},{8,9},{10,11},{12,13},{14,15},{16,17},{18,... | collective-permute-start | bytes 12582920 | tf_op jit(solution)/shard_map/sum_down_last/ppermute | solution.py:262
  627.6 39.6 %collective-permute-start.83 = (bf16[4,128,384]{2,1,0:T(8,128)(2,1)S(1)}, bf16[4,128,384]{2,1,0:T(8,128)(2,1)S(1)}, u32[]{:S(2)}, u32[]{:S(2)}) collective-permute-start(bf16[4,128,384]{2,1,0:T(8,128)(2,1)S(1)} %fusion.51), channel_id=1, source_target_pairs={{0,2},{1,3},{2,0},{3,1},{4,6},{5,7},{6,4},{7,5},{8,10},{9,11},{10,... | collective-permute-start | bytes 1179656 | tf_op jit(solution)/shard_map/sum_qkv_second/ppermute | solution.py:262
  683.9 38.8 %collective-permute-start.106 = (bf16[4,128,1024]{2,1,0:T(8,128)(2,1)}, bf16[4,128,1024]{2,1,0:T(8,128)(2,1)}, u32[]{:S(2)}, u32[]{:S(2)}) collective-permute-start(bf16[4,128,1024]{2,1,0:T(8,128)(2,1)} %collective-permute-done.104.refs_1_), channel_id=1, source_target_pairs={{0,1},{1,0},{2,3},{3,2},{4,5},{5,4},{6,7},{7,6},{8,9},{9,8},{10,11... | collective-permute-start | bytes 3145736 | tf_op jit(solution)/shard_map/sum_up_last/ppermute | solution.py:262
  708.7 40.1 %collective-permute-start.93 = (bf16[2,128,2048]{2,1,0:T(8,128)(2,1)}, bf16[2,128,2048]{2,1,0:T(8,128)(2,1)}, u32[]{:S(2)}, u32[]{:S(2)}) collective-permute-start(bf16[2,128,2048]{2,1,0:T(8,128)(2,1)} %pad_maximum_fusion.12), channel_id=1, source_target_pairs={{0,1},{2,3},{4,5},{6,7},{8,9},{10,11},{12,13},{14,15},{16,17},{18,... | collective-permute-start | bytes 3145736 | tf_op jit(solution)/shard_map/sum_out_last/ppermute | solution.py:262
  (226 other events, 3608.6 us)

commit v4 on v3

v4 whole, which is shorter than its diff:
```python
import functools
import math

import jax
import jax.numpy as jnp
from jax import lax
from jax.experimental import pallas as pl
from jax.experimental.pallas import tpu as pltpu
from jax.sharding import PartitionSpec as P

HD = 64
EPS = 1e-05
THETA = 1000000.0
NEG = -1e30
BF = jnp.bfloat16
F32 = jnp.float32
ATTENTION_BYTES = 24 * 1024 * 1024
PLACE_BYTES = 44 * 1024 * 1024
LOW_COST = pl.CostEstimate(flops=1, bytes_accessed=1, transcendentals=0)


def matmul(left, right):
    return jnp.dot(left, right, preferred_element_type=F32)


def left_tmul(left, right):
    return lax.dot_general(left, right, (((0,), (0,)), ((), ())), preferred_element_type=F32)


def right_tmul(left, right):
    return lax.dot_general(left, right, (((1,), (1,)), ((), ())), preferred_element_type=F32)


def unit_rows(values):
    root = lax.rsqrt(jnp.mean(values * values, axis=-1, keepdims=True) + EPS)
    return values * root, root


def unit_back(unit, root, grad):
    return root * (grad - unit * jnp.mean(grad * unit, axis=-1, keepdims=True))


def turn(values, cosine, sine):
    half = values.shape[-1] // 2
    swapped = jnp.concatenate([values[:, half:], values[:, :half]], axis=1)
    return values * cosine + swapped * sine


def token_table(segments, width):
    index = jnp.arange(segments.shape[1])
    same = segments[:, :, None] == segments[:, None, :]
    position = jnp.sum((same & (index[None, :] < index[:, None])).astype(jnp.int32), axis=2)
    frequency = jnp.exp(jnp.arange(HD // 2).astype(F32) * (-2.0 * math.log(THETA) / HD))
    phase = position.astype(F32).reshape(-1, 1) * frequency
    cosine, sine = jnp.cos(phase), jnp.sin(phase)
    packs = jnp.arange(segments.shape[0], dtype=jnp.int32) % (width // segments.shape[1])
    marks = (segments + 4 * packs[:, None]).astype(F32).reshape(-1, 1)
    marks = jnp.broadcast_to(marks, (marks.shape[0], width))
    return jnp.concatenate([cosine, cosine, -sine, sine, marks], axis=1)


def head(values, index):
    return values[:, index * HD : (index + 1) * HD]


def allowed_block(marks):
    later = lax.broadcasted_iota(jnp.int32, marks.shape, 1)
    return (marks == marks.T) & (later <= lax.broadcasted_iota(jnp.int32, marks.shape, 0))


def probabilities(query, key, allowed):
    scores = right_tmul(query, key) * HD ** (-0.5)
    exponent = jnp.where(allowed, jnp.exp(scores), 0.0)
    return exponent * (1.0 / jnp.sum(exponent, axis=-1, keepdims=True))


def attention_kernel(q_here, kv_here, *refs):
    here_ref, other_ref, table_ref, gain_ref, q_gain_ref, k_gain_ref, w_qkv_ref, w_out_ref = refs[:8]
    attn_in_ref, qkv_ref, mixed_ref, own_ref, away_ref = refs[8:]
    group = q_here // kv_here
    rows = here_ref.shape[0]
    gain = gain_ref[...]
    for index, tokens_ref in enumerate((here_ref, other_ref)):
        unit, _ = unit_rows(tokens_ref[...].astype(F32))
        attn_in_ref[index * rows : (index + 1) * rows, :] = (unit * gain).astype(BF)
    qkv = matmul(attn_in_ref[...], w_qkv_ref[...])
    qkv_ref[...] = qkv
    blocks = [slice(index * rows, (index + 1) * rows) for index in range(2)]
    allowed = [allowed_block(table_ref[part, 2 * HD :]) for part in blocks]
    cosine, sine = table_ref[:, :HD], table_ref[:, HD : 2 * HD]
    for kv in range(kv_here):
        key = turn(unit_rows(head(qkv, q_here + kv))[0] * k_gain_ref[...], cosine, sine).astype(BF)
        value = head(qkv, q_here + kv_here + kv).astype(BF)
        for h in range(kv * group, (kv + 1) * group):
            query = turn(unit_rows(head(qkv, h))[0] * q_gain_ref[...], cosine, sine).astype(BF)
            for index, part in enumerate(blocks):
                probs = probabilities(query[part], key[part], allowed[index])
                mixed_ref[part, h * HD : (h + 1) * HD] = matmul(probs.astype(BF), value[part]).astype(BF)
    mixed = mixed_ref[...]
    own_ref[...] = matmul(mixed[:rows], w_out_ref[...]).astype(BF)
    away_ref[...] = matmul(mixed[rows:], w_out_ref[...]).astype(BF)


def attention_back_kernel(q_here, kv_here, *refs):
    here_ref, other_ref, qkv_ref, table_ref, q_gain_ref, k_gain_ref, w_qkv_ref, w_out_ref = refs[:8]
    g_attn_ref, g_qkv_ref, own_ref, away_ref, gains_ref = refs[8:]
    group = q_here // kv_here
    rows = here_ref.shape[0]
    g_attn_ref[:rows, :] = here_ref[...]
    g_attn_ref[rows:, :] = other_ref[...]
    g_mixed = right_tmul(g_attn_ref[...], w_out_ref[...]).astype(BF)
    qkv = qkv_ref[...]
    blocks = [slice(index * rows, (index + 1) * rows) for index in range(2)]
    allowed = [allowed_block(table_ref[part, 2 * HD :]) for part in blocks]
    cosine, sine = table_ref[:, :HD], table_ref[:, HD : 2 * HD]
    q_gain, k_gain = q_gain_ref[...], k_gain_ref[...]
    scale = HD ** (-0.5)
    q_sum = jnp.zeros((1, HD), F32)
    k_sum = jnp.zeros((1, HD), F32)
    pieces = {}
    for kv in range(kv_here):
        k_unit, k_root = unit_rows(head(qkv, q_here + kv))
        key = turn(k_unit * k_gain, cosine, sine).astype(BF)
        value = head(qkv, q_here + kv_here + kv).astype(BF)
        g_k, g_v = [0.0, 0.0], [0.0, 0.0]
        for h in range(kv * group, (kv + 1) * group):
            q_unit, q_root = unit_rows(head(qkv, h))
            query = turn(q_unit * q_gain, cosine, sine).astype(BF)
            g_head = head(g_mixed, h)
            g_query = []
            for index, part in enumerate(blocks):
                probs = probabilities(query[part], key[part], allowed[index])
                g_probs = right_tmul(g_head[part], value[part])
                g_v[index] = g_v[index] + left_tmul(probs.astype(BF), g_head[part])
                g_scores = probs * (g_probs - jnp.sum(probs * g_probs, axis=-1, keepdims=True))
                g_scores = g_scores.astype(BF)
                g_k[index] = g_k[index] + left_tmul(g_scores, query[part])
                g_query.append(matmul(g_scores, key[part]))
            back = turn(jnp.concatenate(g_query, axis=0) * scale, cosine, -sine)
            q_sum = q_sum + jnp.sum(back * q_unit, axis=0, keepdims=True)
            pieces[h] = unit_back(q_unit, q_root, back * q_gain).astype(BF)
        back = turn(jnp.concatenate(g_k, axis=0) * scale, cosine, -sine)
        k_sum = k_sum + jnp.sum(back * k_unit, axis=0, keepdims=True)
        pieces[q_here + kv] = unit_back(k_unit, k_root, back * k_gain).astype(BF)
        pieces[q_here + kv_here + kv] = jnp.concatenate(g_v, axis=0).astype(BF)
    g_qkv = jnp.concatenate([pieces[index] for index in range(q_here + 2 * kv_here)], axis=1)
    g_qkv_ref[...] = g_qkv
    own_ref[...] = right_tmul(g_qkv[:rows], w_qkv_ref[...]).astype(BF)
    away_ref[...] = right_tmul(g_qkv[rows:], w_qkv_ref[...]).astype(BF)
    gains_ref[...] = jnp.concatenate([q_sum, k_sum], axis=0)


def single(array, block=None, index=0):
    block = array.shape if block is None else block
    return pl.BlockSpec(block, lambda step: (index,) + (0,) * (len(block) - 1))


def slot_call(kernel, name, arrays, specs, shapes):
    return pl.pallas_call(
        kernel,
        grid=(1,),
        in_specs=specs,
        out_specs=[single(shape) for shape in shapes],
        out_shape=shapes,
        compiler_params=pltpu.CompilerParams(vmem_limit_bytes=ATTENTION_BYTES),
        cost_estimate=LOW_COST,
        name=name,
    )(*arrays)


def attention(slot, here, other, table, gain, q_gain, k_gain, w_qkv, w_out, q_here, kv_here):
    rows, width = here.shape
    arrays = (here, other, table, gain, q_gain, k_gain, w_qkv, w_out)
    specs = [single(array) for array in arrays]
    specs[2] = single(table, (2 * rows, table.shape[1]), slot)
    shapes = [
        jax.ShapeDtypeStruct((2 * rows, width), BF),
        jax.ShapeDtypeStruct((2 * rows, w_qkv.shape[1]), F32),
        jax.ShapeDtypeStruct((2 * rows, q_here * HD), BF),
        jax.ShapeDtypeStruct((rows, width), BF),
        jax.ShapeDtypeStruct((rows, width), BF),
    ]
    kernel = functools.partial(attention_kernel, q_here, kv_here)
    return slot_call(kernel, "attention", arrays, specs, shapes)


def attention_back(slot, here, other, qkv, table, q_gain, k_gain, w_qkv, w_out, q_here, kv_here):
    rows, width = here.shape
    arrays = (here, other, qkv, table, q_gain, k_gain, w_qkv, w_out)
    specs = [single(array) for array in arrays]
    specs[3] = single(table, (2 * rows, table.shape[1]), slot)
    shapes = [
        jax.ShapeDtypeStruct((2 * rows, width), BF),
        jax.ShapeDtypeStruct((2 * rows, w_qkv.shape[1]), BF),
        jax.ShapeDtypeStruct((rows, width), BF),
        jax.ShapeDtypeStruct((rows, width), BF),
        jax.ShapeDtypeStruct((2, HD), F32),
    ]
    kernel = functools.partial(attention_back_kernel, q_here, kv_here)
    return slot_call(kernel, "attention_back", arrays, specs, shapes)


def place_kernel(moves, source_count, out_count, row_ref, column_ref, *refs):
    sources, outs = refs[:source_count], refs[source_count : source_count + out_count]
    refs = refs[source_count + out_count :]
    cast = outs[0].dtype != sources[0].dtype
    staged = refs[source_count:-2] if cast else ()
    loaded, loads, stores = refs[:source_count], refs[-2], refs[-1]
    reads = [
        pltpu.make_async_copy(source, buffer, loads.at[index])
        for index, (source, buffer) in enumerate(zip(sources, loaded))
    ]
    for read in reads:
        read.start()
    writes = []
    arrived = set()
    for index, (source, slot, rows, columns, out) in enumerate(moves):
        height, width = rows.stop - rows.start, columns.stop - columns.start
        row = pl.multiple_of(row_ref[index] * height, height)
        if source not in arrived:
            reads[source].wait()
            arrived.add(source)
        if cast:
            staged[index][...] = loaded[source][slot, rows, columns].astype(outs[out].dtype)
            block = staged[index]
        else:
            block = loaded[source].at[slot, rows, columns]
        if len(outs[out].shape) == 3:
            target = outs[out].at[column_ref[index], pl.ds(row, height), :]
        elif outs[out].shape[1] == width:
            target = outs[out].at[pl.ds(row, height), :]
        else:
            column = pl.multiple_of(column_ref[index] * width, width)
            target = outs[out].at[pl.ds(row, height), pl.ds(column, width)]
        writes.append(pltpu.make_async_copy(block, target, stores.at[index]))
        writes[-1].start()
    for write in writes:
        write.wait()


def place_blocks(sources, moves, row_blocks, column_blocks, shapes, dtype):
    scratch = [pltpu.VMEM(source.shape, source.dtype) for source in sources]
    if dtype != sources[0].dtype:
        scratch += [
            pltpu.VMEM((rows.stop - rows.start, columns.stop - columns.start), dtype)
            for _, _, rows, columns, _ in moves
        ]
    scratch += [pltpu.SemaphoreType.DMA((len(sources),)), pltpu.SemaphoreType.DMA((len(moves),))]
    anywhere = pl.BlockSpec(memory_space=pl.ANY)
    return pl.pallas_call(
        functools.partial(place_kernel, moves, len(sources), len(shapes)),
        in_specs=[pl.BlockSpec(memory_space=pltpu.SMEM)] * 2 + [anywhere] * len(sources),
        out_specs=[anywhere] * len(shapes),
        out_shape=[jax.ShapeDtypeStruct(shape, dtype) for shape in shapes],
        scratch_shapes=scratch,
        compiler_params=pltpu.CompilerParams(vmem_limit_bytes=PLACE_BYTES),
        cost_estimate=LOW_COST,
        name="place_blocks",
    )(row_blocks.astype(jnp.int32), column_blocks.astype(jnp.int32), *sources)


def after(values, *others):
    return lax.optimization_barrier((values, *others))[0]


def move(values, send):
    ranks, copies = lax.axis_size("fsdp"), lax.axis_size("rep")
    pairs = []
    for f in range(ranks):
        for r in range(copies):
            to = send(f, r)
            if to is not None:
                pairs.append((f * copies + r, to[0] * copies + to[1]))
    return lax.ppermute(values, ("fsdp", "rep"), pairs)


def ring(values, step):
    ranks = lax.axis_size("fsdp")
    return move(values, lambda f, r: ((f + 2 * step) % ranks, r))


def swap_core(values):
    return move(values, lambda f, r: (f, r ^ 1))


def swap_x(values):
    return move(values, lambda f, r: (f, r ^ 2))


def swap_twin(values):
    return move(values, lambda f, r: (f ^ 1, r ^ 1))


def place():
    f, r = lax.axis_index("fsdp"), lax.axis_index("rep")
    return f // 2, f % 2, r // 2, r % 2


def pick(values, index, axis=0):
    return lax.dynamic_index_in_dim(values, index, axis, keepdims=False)


def ordered(slots, z):
    depth = len(slots)
    out = jnp.zeros((depth, *slots[0].shape), slots[0].dtype)
    for k, slot in enumerate(slots):
        out = lax.dynamic_update_index_in_dim(out, slot, (z - k) % depth, 0)
    return out


def add(left, right):
    return (left.astype(F32) + right.astype(F32)).astype(BF)


def gather_group(values, name, beside=None):
    slots = []
    for s in range(lax.axis_size("fsdp") // 2):
        with jax.named_scope(f"gather_{name}_{s}"):
            if s > 0:
                values = ring(values if beside is None else beside(s, values), 1)
            slots.append((values, swap_core(values)))
    return slots


def scatter_group(partial, name, beside=None):
    moving = None
    for step, (own, away) in enumerate((*partial[1:], partial[0])):
        with jax.named_scope(f"scatter_{name}_{step}"):
            total = own.astype(F32) + swap_core(away).astype(F32)
            if moving is not None:
                total = total + ring(moving, 1).astype(F32)
            moving = total.astype(BF)
        if beside is not None:
            moving = beside(step, moving)
    return total


def total_sum(values):
    for bit in range(2):
        values = values + move(values, lambda f, r: (f, r ^ (1 << bit)))
    for bit in range((lax.axis_size("fsdp") - 1).bit_length()):
        values = values + move(values, lambda f, r: (f ^ (1 << bit), r))
    return values


class ColumnsIn:
    def __init__(self, parts, rows, name, hold=lambda slots: slots):
        with jax.named_scope(f"{name}_along_z"):
            slots = [ring(part, k) if k else part for k, part in enumerate(parts)]
            self.same = jnp.stack(hold(slots))
        with jax.named_scope(f"{name}_across"):
            self.across_x, self.across_y = swap_x(self.same), swap_twin(self.same)
        self.rows, self.name = rows, name

    def joined(self, split, *others):
        z, y, x, core = place()
        depth, columns = self.same.shape[0], self.same.shape[2]
        middle = depth // 2 if split else depth
        with jax.named_scope(f"{self.name}_across_both"):
            across_x, across_y = after((self.across_x, self.across_y), *others)
            rest = [swap_twin(across_x[:middle])]
            if split:
                rest.append(swap_x(across_y[middle:]))
        sources = [self.same, self.across_x, self.across_y, *rest]
        moves = [
            (source, slot, slice(0, self.rows), slice(0, columns), 0)
            for source, array in enumerate(sources)
            for slot in range(array.shape[0])
        ]
        where_z = (z - jnp.arange(depth)) % depth
        index = lambda yy, xx: (where_z * 2 + yy) * 2 + xx
        places = [index(y, x), index(y, 1 - x), index(1 - y, x), index(1 - y, 1 - x)]
        places = jnp.concatenate(places)
        shape = (4 * depth * self.rows, columns)
        return place_blocks(sources, moves, places, jnp.zeros_like(places), [shape], BF)[0]


def scoped(step):
    def wrap(method):
        def named(self, *others):
            with jax.named_scope(f"{self.name}_{step}"):
                return method(self, *others)

        return named

    return wrap


class ColumnsOut:
    def __init__(self, grad, y_first, name):
        self.name = name
        z, y, x, core = place()
        self.depth = lax.axis_size("fsdp") // 2
        self.y_first = y_first
        columns = grad.shape[1]
        self.blocks = grad.reshape(self.depth, 2, 2, -1, columns)
        axis, index = (1, 1 - y) if y_first else (2, 1 - x)
        self.payload = pick(self.blocks, index, axis)

    @scoped("first")
    def first(self, *others):
        z, y, x, core = place()
        axis, index = (1, y) if self.y_first else (2, x)
        swap = swap_twin if self.y_first else swap_x
        came, own = after(swap(self.payload), *others), pick(self.blocks, index, axis)
        here, there = (x, 1 - x) if self.y_first else (y, 1 - y)
        self.payload = add(pick(own, there, 1), pick(came, there, 1))
        self.kept = (pick(own, here, 1), pick(came, here, 1))

    @scoped("second")
    def second(self, *others):
        z, y, x, core = place()
        swap = swap_x if self.y_first else swap_twin
        came = after(swap(self.payload), *others).astype(F32)
        total = (self.kept[0].astype(F32) + self.kept[1].astype(F32) + came).astype(BF)
        self.payload = [pick(total, (z + k) % self.depth) for k in range(self.depth)]


def along_z(payloads, name):
    with jax.named_scope(f"sum_{name}_along_z"):
        parts = [jnp.concatenate(items, axis=1) for items in zip(*payloads)]
        return [ring(part, k) if k else part for k, part in enumerate(parts)]


def across_x(same, name):
    with jax.named_scope(f"sum_{name}_across"):
        return swap_x(same)


def columns_placed(same, across, widths, name):
    z, y, x, core = place()
    depth, rows, total = same.shape
    with jax.named_scope(f"sum_{name}_core"):
        parts = same, across, swap_core(same), swap_core(across)
    ones = jnp.ones((depth,), jnp.int32)
    row_blocks = jnp.concatenate([x * ones, (1 - x) * ones] * 2)
    where_z = (z - jnp.arange(depth)) % depth
    own, other = 2 * where_z + (y ^ core), 2 * where_z + (1 - (y ^ core))
    column_blocks = jnp.concatenate([own, own, other, other])
    aligned = all(width % 128 == 0 for width in widths)
    spans = []
    for width in widths if aligned else [total]:
        first = spans[-1].stop if spans else 0
        spans.append(slice(first, first + width))
    moves = [
        (source, slot, slice(0, rows), span, out)
        for source in range(4)
        for slot in range(depth)
        for out, span in enumerate(spans)
    ]
    if aligned:
        shapes = [(2 * rows, 2 * depth * width) for width in widths]
    else:
        shapes = [(2 * depth, 2 * rows, total)]
    repeat = lambda blocks: jnp.repeat(blocks, len(spans))
    outs = place_blocks(parts, moves, repeat(row_blocks), repeat(column_blocks), shapes, F32)
    if aligned:
        return outs
    rows_first = outs[0].transpose(1, 0, 2)
    pieces, first = [], 0
    for width in widths:
        pieces.append(rows_first[:, :, first : first + width].reshape(2 * rows, -1))
        first += width
    return pieces


def rows_across_y(weight, name):
    half = weight.shape[0] // 2
    with jax.named_scope(f"{name}_across_y"):
        part = lax.dynamic_slice_in_dim(weight, place()[2] * half, half, axis=0)
        return move(part, lambda f, r: (f ^ 1, r) if r % 2 else None)


def rows_here(weight, part, name):
    z, y, x, core = place()
    half = weight.shape[0] // 2
    with jax.named_scope(f"{name}_across_x"):
        other = move(part, lambda f, r: (f, r ^ 2) if r % 2 else None)
    low = jnp.where(core == 0, weight[:half], jnp.where(x == 0, part, other))
    high = jnp.where(core == 0, weight[half:], jnp.where(x == 0, other, part))
    return jnp.concatenate([low, high], axis=0)


class RowsOut:
    def __init__(self, grad, name):
        self.name = name
        self.grad = self.payload = grad.reshape(2, -1, grad.shape[1])

    @scoped("first")
    def first(self, *others):
        z, y, x, core = place()
        came = after(move(self.payload, lambda f, r: (f ^ 1, r ^ 1) if r % 2 else None), *others)
        self.payload = add(pick(self.grad, 1 - x), pick(came, 1 - x))
        self.kept = (pick(self.grad, x), pick(came, x))

    @scoped("second")
    def second(self, *others):
        came = move(self.payload, lambda f, r: None if r % 2 else (f, r ^ 2))
        came = after(came, *others).astype(F32)
        self.payload = (self.kept[0].astype(F32) + self.kept[1].astype(F32) + came).astype(BF)

    @scoped("third")
    def third(self, *others):
        came = after(move(self.payload, lambda f, r: None if r % 2 else (f, r ^ 2)), *others)
        self.payload = jnp.stack([self.payload, came])

    @scoped("last")
    def last(self):
        z, y, x, core = place()
        came = move(self.payload, lambda f, r: None if r % 2 else (f, r ^ 1))
        parts = jnp.where(core == 0, self.payload, came)
        rows, columns = parts.shape[1:]
        moves = [(0, slot, slice(0, rows), slice(0, columns), 0) for slot in range(2)]
        places = jnp.stack([x, 1 - x])
        return place_blocks([parts], moves, places, jnp.zeros_like(places), [(2 * rows, columns)], F32)[0]


def local(
    tokens_in,
    segment_ids,
    w_query,
    w_key,
    w_value,
    w_out,
    w_gate,
    w_up,
    w_down,
    gain_attn,
    gain_ffn,
    gain_query,
    gain_key,
    d_out,
):
    ranks = lax.axis_size("fsdp")
    rank = lax.axis_index("fsdp")
    depth = ranks // 2
    z, y, x, core = place()
    width = tokens_in.shape[1]
    pack = segment_ids.shape[1]
    heads = w_query.shape[1] // HD
    kv_heads = w_key.shape[1] // HD
    share = max(1, ranks // kv_heads)
    q_here = heads // ranks
    kv_here = max(1, kv_heads // ranks)
    group = q_here // kv_here
    q_cols, kv_cols = q_here * HD, kv_here * HD
    scale = HD ** (-0.5)

    q_gain = gain_query.astype(F32)[None]
    k_gain = gain_key.astype(F32)[None]

    rows_x = w_query.shape[0] // 2
    cut = lambda weight, start, size: lax.dynamic_slice(weight, (x * rows_x, start), (rows_x, size))
    wide = q_cols + 2 * kv_cols
    seg_size = segment_ids.size
    extra = jnp.concatenate([segment_ids.reshape(-1).astype(BF), gain_attn, gain_ffn])
    extra = jnp.pad(extra, (0, 16 * wide - extra.size)).reshape(16, wide)

    def cut_qkv(block):
        kv = block // share * kv_cols
        parts = [cut(w_query, block * q_cols, q_cols), cut(w_key, kv, kv_cols), cut(w_value, kv, kv_cols)]
        return jnp.concatenate([jnp.concatenate(parts, axis=1), extra], axis=0)

    def cutter(weight):
        size = weight.shape[1] // ranks
        return lambda block: cut(weight, block * size, size)

    qkv_parts = [cut_qkv(2 * ((z + k) % depth) + (y ^ core)) for k in range(depth)]
    qkv_in = ColumnsIn(qkv_parts, rows_x, "w_qkv")
    w_qkv = qkv_in.joined(False)
    w_out_here = rows_here(w_out, rows_across_y(w_out, "w_out"), "w_out")
    down_part = rows_across_y(after(w_down, w_qkv), "w_down")
    w_down_here = rows_here(w_down, down_part, "w_down")
    w_gate_late, w_up_late = after((w_gate, w_up), qkv_in.same)
    columns_here = w_gate.shape[1] // ranks

    def cut_glu(block):
        first = block * columns_here
        return jnp.concatenate(
            [cut(w_gate_late, first, columns_here), cut(w_up_late, first, columns_here)], axis=1
        )

    glu_parts = [cut_glu(2 * ((z + k) % depth) + (y ^ core)) for k in range(depth)]
    glu_in = ColumnsIn(glu_parts, rows_x, "w_glu", lambda slots: after((*slots,), w_qkv, w_out_here))
    own_slots, twin_slots = qkv_in.same, qkv_in.across_y
    own_extra = own_slots[:, rows_x:].reshape(depth, -1)
    twin_extra = twin_slots[:, rows_x:].reshape(depth, -1)
    seg_slots = own_extra[:, :seg_size].reshape(depth, 1, -1, pack)
    segments = jnp.concatenate([seg_slots, swap_core(seg_slots)], axis=1).reshape(-1, pack).astype(jnp.int32)
    span = slice(seg_size, seg_size + 2 * gain_attn.size)
    pieces = jnp.stack([own_extra[:, span], twin_extra[:, span]], axis=1)
    pieces = ordered([pieces[k] for k in range(depth)], z).astype(F32)
    pieces = jnp.where(y == 0, pieces, pieces[:, ::-1])
    gains = pieces.reshape(depth, 2, 2, -1).transpose(2, 0, 1, 3).reshape(2, -1)
    attn_gain, ffn_gain = gains[0], gains[1]

    token_ties = {1: (glu_in.same, attn_gain, down_part), 2: (w_down_here,)}
    beside_tokens = lambda s, sent: after(sent, *token_ties.get(s, ()))
    token_slots = gather_group(tokens_in, "tokens", beside_tokens)
    block_rows = tokens_in.shape[0]
    table = token_table(segments, block_rows)
    kept, partial = [None] * depth, [None] * depth
    order = (*range(1, depth), 0)
    for s in order:
        here, other = token_slots[s]
        if s == depth - 1:
            here = after(here, glu_in.across_x, glu_in.across_y)
        *kept[s], own, away = attention(
            s, here, other, table, attn_gain[None], q_gain, k_gain, w_qkv, w_out_here, q_here, kv_here
        )
        partial[s] = (own, away)
    tokens = tokens_in.astype(F32)
    unit_tokens, root_tokens = unit_rows(tokens)

    w_glu = glu_in.joined(True)
    attn_branch = after(scatter_group(partial, "attn_branch"), w_glu)

    middle = tokens + attn_branch
    unit_middle, root_middle = unit_rows(middle)
    ffn_slots = gather_group((unit_middle * ffn_gain).astype(BF), "ffn_in")
    beside_d_out = lambda s, sent: after(sent, ffn_slots[-1][0]) if s == 1 else sent
    grad_slots = gather_group(d_out, "d_out", beside_d_out)
    glu_kept, back_partial, down_partial = [None] * depth, [None] * depth, []
    for s in order:
        ffn_in = jnp.concatenate(ffn_slots[s], axis=0)
        g_ffn = jnp.concatenate(grad_slots[s], axis=0)
        gate_up = matmul(ffn_in, w_glu)
        gate, up = gate_up[:, :columns_here], gate_up[:, columns_here:]
        sig = jax.nn.sigmoid(gate)
        silu = gate * sig
        hidden = (silu * up).astype(BF)
        g_hidden = right_tmul(g_ffn, w_down_here).astype(BF).astype(F32)
        g_gate = (g_hidden * up * sig * (1 + gate * (1 - sig))).astype(BF)
        g_up = (g_hidden * silu).astype(BF)
        part = right_tmul(jnp.concatenate([g_gate, g_up], axis=1), w_glu).astype(BF)
        back_partial[s] = (part[:block_rows], part[block_rows:])
        glu_kept[s] = (ffn_in, g_ffn, hidden, g_gate, g_up)
    ffn_in, g_ffn, hidden, g_gate, g_up = (jnp.concatenate(items, axis=0) for items in zip(*glu_kept))
    sums = {}

    def beside_feed(step, sent):
        if step == depth - 3:
            grad = left_tmul(*after((ffn_in, g_gate), sent)).astype(BF)
            sums["gate"] = ColumnsOut(grad, True, "sum_gate")
            grad = left_tmul(*after((ffn_in, g_up), sums["gate"].payload)).astype(BF)
            sums["up"] = ColumnsOut(grad, False, "sum_up")
        if step == depth - 2:
            sent = after(sent, sums["up"].payload)
        return sent

    g_ffn_in = scatter_group(back_partial, "g_ffn_in", beside_feed)
    gate_sum, up_sum = sums["gate"], sums["up"]
    g_ffn_in = after(g_ffn_in, gate_sum.payload, up_sum.payload)
    ffn_gain_grad = jnp.sum(g_ffn_in * unit_middle, axis=0)
    g_middle = d_out.astype(F32) + unit_back(unit_middle, root_middle, g_ffn_in * ffn_gain)

    attn_slots = gather_group(g_middle.astype(BF), "g_attn")
    back_kept, partial = [None] * depth, [None] * depth
    head_gains = 0.0
    for s in order:
        here, other = attn_slots[s]
        if s == 2:
            gate_sum.first(partial[1][1])
            up_sum.first(partial[1][1])
            here = after(here, gate_sum.payload, up_sum.payload)
        if s == 3:
            gate_sum.second(partial[2][1])
            up_sum.second(partial[2][1])
            grad_down = left_tmul(*after((hidden, g_ffn), up_sum.payload)).astype(BF)
            down_sum = RowsOut(grad_down, "sum_down")
            here = after(here, gate_sum.payload, up_sum.payload, down_sum.payload)
        g_attn, g_qkv, own, away, gain_part = attention_back(
            s, here, other, kept[s][1], table, q_gain, k_gain, w_qkv, w_out_here, q_here, kv_here
        )
        head_gains = head_gains + gain_part
        back_kept[s] = (g_attn, g_qkv)
        partial[s] = (own, away)
    attn_in, _, mixed = (jnp.concatenate(items, axis=0) for items in zip(*kept))
    g_attn, g_qkv = (jnp.concatenate(items, axis=0) for items in zip(*back_kept))
    grad_qkv = left_tmul(attn_in, g_qkv).astype(BF)
    qkv_sum = ColumnsOut(grad_qkv, True, "sum_qkv")
    grad_out = left_tmul(*after((mixed, g_attn), qkv_sum.payload)).astype(BF)
    out_sum = RowsOut(grad_out, "sum_out")
    glu_parts = [jnp.concatenate(pair, axis=1) for pair in zip(gate_sum.payload, up_sum.payload)]
    glu_slots = {0: glu_parts[0]}
    steps = sorted(range(1, depth), key=lambda k: -min(k, depth - k))
    last = None
    for k in steps:
        with jax.named_scope(f"sum_glu_along_z_{k}"):
            part = glu_parts[k] if last is None else after(glu_parts[k], last)
            last = glu_slots[k] = ring(part, k)
        if k == steps[0]:
            last = after(last, qkv_sum.payload, out_sum.payload)
    glu_same = jnp.stack([glu_slots[k] for k in range(depth)])
    glu_across = across_x(glu_same, "glu")

    def beside_back(step, sent):
        if step == 0:
            sent = after(sent, glu_slots[steps[0]])
        if step == 1:
            sent = after(sent, glu_same)
            for item in (down_sum, qkv_sum, out_sum):
                item.first(sent)
        if step == 2:
            sent = after(sent, down_sum.payload, qkv_sum.payload, out_sum.payload)
        return sent

    g_attn_in = scatter_group(partial, "g_attn_in", beside_back)
    attn_gain_grad = jnp.sum(g_attn_in * unit_tokens, axis=0)
    d_tokens = g_middle + unit_back(unit_tokens, root_tokens, g_attn_in * attn_gain)

    for s in range(depth):
        part = matmul(after(glu_kept[s][2], glu_same), w_down_here).astype(BF)
        down_partial.append((part[:block_rows], part[block_rows:]))
    ffn_ties = {0: (glu_across, d_tokens)}
    glu_placed = []

    def beside_branch(step, sent):
        if step == 0:
            glu_placed.extend(columns_placed(glu_same, glu_across, [columns_here, columns_here], "glu"))
        if step == 1:
            qkv_sum.second(sent)
            out_sum.second(sent)
            ffn_ties[1] = (qkv_sum.payload, out_sum.payload)
        if step == 2:
            down_sum.second(sent)
            ffn_ties[2] = (down_sum.payload, *glu_placed)
        return after(sent, *ffn_ties.get(step, ()))

    ffn_branch = scatter_group(down_partial, "ffn_branch", beside_branch)
    block = middle + ffn_branch
    grad_gate, grad_up = glu_placed
    qkv_slots = along_z([qkv_sum.payload], "qkv")
    qkv_same = jnp.stack(qkv_slots)
    qkv_across = across_x(qkv_same, "qkv")
    grad_query, grad_kv = columns_placed(qkv_same, qkv_across, [q_cols, 2 * kv_cols], "qkv")
    down_sum.third(ffn_branch)
    out_sum.third(ffn_branch)
    grad_down, grad_out = down_sum.last(), out_sum.last()
    grad_kv = grad_kv.reshape(grad_kv.shape[0], -1, share, 2 * kv_cols).sum(axis=2)
    grad_key = grad_kv[:, :, :kv_cols].reshape(grad_kv.shape[0], -1)
    grad_value = grad_kv[:, :, kv_cols:].reshape(grad_kv.shape[0], -1)
    squares = jnp.stack(
        [jnp.sum(item * item) for item in (middle, attn_branch, ffn_branch, block, d_tokens)]
    )
    small = jnp.concatenate([attn_gain_grad, ffn_gain_grad, head_gains[0], head_gains[1], squares])
    with jax.named_scope("total_sum"):
        small = total_sum(small)
    gain_rows = gain_attn.shape[0]
    attn_gain_sum = lax.dynamic_slice(small, (rank * gain_rows,), (gain_rows,))
    ffn_gain_sum = lax.dynamic_slice(small, (width + rank * gain_rows,), (gain_rows,))
    entries = tokens_in.shape[0] * ranks * lax.axis_size("rep") * width
    stats = jnp.sqrt(small[2 * width + 2 * HD :] / entries)
    return (
        block.astype(BF),
        d_tokens.astype(BF),
        grad_query,
        grad_key,
        grad_value,
        grad_out,
        grad_gate,
        grad_up,
        grad_down,
        attn_gain_sum,
        ffn_gain_sum,
        small[2 * width : 2 * width + HD],
        small[2 * width + HD : 2 * width + 2 * HD],
        stats,
    )


def solution(mesh):
    rows = P(("fsdp", "rep"), None)
    weight = P("fsdp", None)
    return jax.shard_map(
        local,
        mesh=mesh,
        in_specs=(rows, rows, *[weight] * 7, P("fsdp"), P("fsdp"), P(), P(), rows),
        out_specs=(rows, rows, *[weight] * 7, P("fsdp"), P("fsdp"), P(), P(), P()),
        check_vma=False,
    )
```

time: 769 us -> 669 us (0.87)
  waiting for transfers between devices: 337 us -> 294 us
  Pallas kernels: 101 us -> 71.2 us
  starting transfers between devices: 139 us -> 113 us
  local copies, waits for them, and re-layouts: 66.7 us -> 46.7 us
  matrix products: 53.5 us -> 69.4 us
    ppermute x114 -> x105, waiting for transfers between devices: 337 us -> 294 us  [move(): return lax.ppermute(values, ('fsdp', 'rep'), pairs)]
    pallas_call x16 -> x14, Pallas kernels: 101 us -> 71.2 us  [the longest x8 42.2 us: slot_call(): pl.pallas_call(kernel, grid=(1,), in_specs=specs, out_specs=[single(shape...]
    ppermute x114 -> x105, starting transfers between devices: 139 us -> 113 us  [move(): return lax.ppermute(values, ('fsdp', 'rep'), pairs)]
    unnamed x291 -> x207, local copies, waits for them, and re-layouts: 38.8 us -> 17.3 us
    dot_general x12 -> x8, matrix products: 16.5 us -> 27.3 us  [right_tmul(): lax.dot_general(left, right, (((1,), (1,)), ((), ())), preferred_element_...]
    dot_general x12 -> x8, matrix products: 16.3 us -> 19.3 us  [matmul(): return jnp.dot(left, right, preferred_element_type=F32)]
  transfers between devices with their start and end apart: 114 -> 105, of which waited for: 36 -> 43; matrix products, arithmetic and copies ran while one was open for 19% -> 24% of each run, Pallas kernels for 13% -> 10%
where the time goes in v4:
time: 669 us; the launch traced here: 661 us
  waiting for transfers between devices  294 us (44%)
  starting transfers between devices  113 us (17%)
  Pallas kernels  71.2 us (11%)
  matrix products  69.4 us (10%)
  other arithmetic  63.2 us (9%)
  local copies, waits for them, and re-layouts  46.7 us (7%)
    ppermute x105, waiting for transfers between devices, move(): return lax.ppermute(values, ('fsdp', 'rep'), pairs)  294 us
    ppermute x105, starting transfers between devices, move(): return lax.ppermute(values, ('fsdp', 'rep'), pairs)  113 us
    pallas_call x8, Pallas kernels, slot_call(): pl.pallas_call(kernel, grid=(1,), in_specs=specs, out_specs=[single(shape...  42.2 us
    pallas_call x6, Pallas kernels, place_blocks(): pl.pallas_call(functools.partial(place_kernel, moves, len(sources), len(s...  29.1 us
    dot_general x8, matrix products, right_tmul(): lax.dot_general(left, right, (((1,), (1,)), ((), ())), preferred_element_...  27.3 us
    dot_general x5, matrix products, left_tmul(): lax.dot_general(left, right, (((0,), (0,)), ((), ())), preferred_element_...  22.8 us
    dot_general x8, matrix products, matmul(): return jnp.dot(left, right, preferred_element_type=F32)  19.3 us
    unnamed x207, local copies, waits for them, and re-layouts  17.3 us
  transfers between devices with their start and end apart: 105, of which 43 were waited for; matrix products, arithmetic and copies ran while one was open for 24% of the time, Pallas kernels for 10%

profile of v4, /device:TPU:0, one launch (start us, length us, event | category | flops | bytes accessed | tf_op | source)
XLA Modules:
  0.0 660.6 jit_solution(476307533237425177)
XLA Ops:
  37.9 7.4 %collective-permute-done.7.refs_3_ = bf16[4,144,384]{2,1,0:T(8,128)(2,1)S(1)} collective-permute-done((bf16[4,144,384]{2,1,0:T(8,128)(2,1)S(1)}, bf16[4,144,384]{2,1,0:T(8,128)(2,1)S(1)}, u32[]{:S(2)}, u32[]{:S(2)}) %collective-permute-start.7) | collective-permute-done | bytes 442400 | tf_op jit(solution)/shard_map/w_qkv_across_both/ppermute | solution.py:274
  66.3 11.5 %collective-permute-start.15 = (bf16[128,2048]{1,0:T(8,128)(2,1)S(1)}, bf16[128,2048]{1,0:T(8,128)(2,1)}, u32[]{:S(2)}, u32[]{:S(2)}) collective-permute-start(bf16[128,2048]{1,0:T(8,128)(2,1)S(1)} %copy-done.3), channel_id=1, source_target_pairs={{0,8},{1,9},{2,10},{3,11},{4,12},{5,13},{6,14},{7,15},{8,16},{9,17... | collective-permute-start | bytes 1572872 | tf_op jit(solution)/shard_map/gather_tokens_1/ppermute | solution.py:274
  114.5 9.4 %collective-permute-done.18.refs_0_ = bf16[128,2048]{1,0:T(8,128)(2,1)S(1)} collective-permute-done((bf16[128,2048]{1,0:T(8,128)(2,1)S(1)}, bf16[128,2048]{1,0:T(8,128)(2,1)S(1)}, u32[]{:S(2)}, u32[]{:S(2)}) %collective-permute-start.18) | collective-permute-done | bytes 524320 | tf_op jit(solution)/shard_map/gather_tokens_3/ppermute | solution.py:274
  154.2 14.0 %collective-permute-done.31.refs_4_ = bf16[2,128,2048]{2,1,0:T(8,128)(2,1)} collective-permute-done((bf16[2,128,2048]{2,1,0:T(8,128)(2,1)}, bf16[2,128,2048]{2,1,0:T(8,128)(2,1)}, u32[]{:S(2)}, u32[]{:S(2)}) %collective-permute-start.31) | collective-permute-done | bytes 1048608 | tf_op jit(solution)/shard_map/w_glu_across_both/ppermute | solution.py:274
  171.8 7.2 %place_blocks.7 = bf16[2048,2048]{1,0:T(8,128)(2,1)} custom-call(s32[16]{0:T(128)S(1)} %copy-done.21, s32[16]{0:T(128)S(1)} %copy-done.23, bf16[4,128,2048]{2,1,0:T(8,128)(2,1)} %pad_maximum_fusion.3.refs_0_, bf16[4,128,2048]{2,1,0:T(8,128)(2,1)} %collective-permute-done.19.refs_1_, bf16[4,128,2048]{2,1,0:T(8,128)(2,1)} %collective-permute-done.20.refs_2_, ...), custom_call_target="tpu_custom_call" | custom-call | flops 1 | bytes 1 | tf_op jit(solution)/shard_map/place_blocks/pallas_call | solution.py:250
  185.4 13.2 %collective-permute-done.33 = bf16[128,2048]{1,0:T(8,128)(2,1)S(1)} collective-permute-done((bf16[128,2048]{1,0:T(8,128)(2,1)S(1)}, bf16[128,2048]{1,0:T(8,128)(2,1)S(1)}, u32[]{:S(2)}, u32[]{:S(2)}) %collective-permute-start.33) | collective-permute-done | bytes 524320 | tf_op jit(solution)/shard_map/gather_ffn_in_1/ppermute | solution.py:274
  218.1 10.3 %collective-permute-done.37 = bf16[128,2048]{1,0:T(8,128)(2,1)S(1)} collective-permute-done((bf16[128,2048]{1,0:T(8,128)(2,1)S(1)}, bf16[128,2048]{1,0:T(8,128)(2,1)S(1)}, u32[]{:S(2)}, u32[]{:S(2)}) %collective-permute-start.37) | collective-permute-done | bytes 524320 | tf_op jit(solution)/shard_map/gather_ffn_in_3/ppermute | solution.py:274
  233.7 8.0 %collective-permute-done.40 = bf16[128,2048]{1,0:T(8,128)(2,1)S(1)} collective-permute-done((bf16[128,2048]{1,0:T(8,128)(2,1)S(1)}, bf16[128,2048]{1,0:T(8,128)(2,1)S(1)}, u32[]{:S(2)}, u32[]{:S(2)}) %collective-permute-start.40) | collective-permute-done | bytes 524320 | tf_op jit(solution)/shard_map/gather_d_out_1/ppermute | solution.py:274
  246.3 7.9 %collective-permute-done.42 = bf16[128,2048]{1,0:T(8,128)(2,1)S(1)} collective-permute-done((bf16[128,2048]{1,0:T(8,128)(2,1)S(1)}, bf16[128,2048]{1,0:T(8,128)(2,1)S(1)}, u32[]{:S(2)}, u32[]{:S(2)}) %collective-permute-start.42) | collective-permute-done | bytes 524320 | tf_op jit(solution)/shard_map/gather_d_out_2/ppermute | solution.py:274
  310.5 11.5 %collective-permute-done.53 = bf16[128,2048]{1,0:T(8,128)(2,1)S(1)} collective-permute-done((bf16[128,2048]{1,0:T(8,128)(2,1)S(1)}, bf16[128,2048]{1,0:T(8,128)(2,1)S(1)}, u32[]{:S(2)}, u32[]{:S(2)}) %collective-permute-start.53) | collective-permute-done | bytes 524320 | tf_op jit(solution)/shard_map/scatter_g_ffn_in_3/ppermute | solution.py:274
  323.7 13.0 %collective-permute-done.54.refs_0_ = bf16[128,2048]{1,0:T(8,128)(2,1)S(1)} collective-permute-done((bf16[128,2048]{1,0:T(8,128)(2,1)S(1)}, bf16[128,2048]{1,0:T(8,128)(2,1)S(1)}, u32[]{:S(2)}, u32[]{:S(2)}) %collective-permute-start.54) | collective-permute-done | bytes 524320 | tf_op jit(solution)/shard_map/gather_g_attn_1/ppermute | solution.py:274
  346.0 8.8 %collective-permute-done.58 = bf16[4,2,128,1024]{3,2,0,1:T(8,128)(2,1)S(1)} collective-permute-done((bf16[4,2,128,1024]{3,2,0,1:T(8,128)(2,1)S(1)}, bf16[4,2,128,1024]{3,2,0,1:T(8,128)(2,1)S(1)}, u32[]{:S(2)}, u32[]{:S(2)}) %collective-permute-start.58) | collective-permute-done | bytes 2097184 | tf_op jit(solution)/shard_map/sum_up_first/ppermute | solution.py:274
  387.5 7.2 %convolution_convert_fusion = bf16[1024,2048]{1,0:T(8,128)(2,1)S(1)} fusion(bf16[1024,1024]{1,0:T(8,128)(2,1)S(1)} %pad_maximum_fusion.7, bf16[1024,2048]{1,0:T(8,128)(2,1)} %constant_dynamic-update-slice_fusion.8), kind=kOutput, calls=%fused_computation.15 | convolution fusion | flops 4297064448 | bytes 10485760 | tf_op jit(solution)/shard_map/dot_general | solution.py:27
  415.3 21.2 %collective-permute-done.62 = bf16[128,2048]{1,0:T(8,128)(2,1)} collective-permute-done((bf16[128,2048]{1,0:T(8,128)(2,1)}, bf16[128,2048]{1,0:T(8,128)(2,1)}, u32[]{:S(2)}, u32[]{:S(2)}) %collective-permute-start.62) | collective-permute-done | bytes 524320 | tf_op jit(solution)/shard_map/sum_glu_along_z_2/ppermute | solution.py:274
  436.5 9.1 %collective-permute-start.76 = (bf16[128,2048]{1,0:T(8,128)(2,1)S(1)}, bf16[128,2048]{1,0:T(8,128)(2,1)S(1)}, u32[]{:S(2)}, u32[]{:S(2)}) collective-permute-start(bf16[128,2048]{1,0:T(8,128)(2,1)S(1)} %copy-done.53), channel_id=1, source_target_pairs={{0,8},{1,9},{2,10},{3,11},{4,12},{5,13},{6,14},{7,15},{8,16},{9,17... | collective-permute-start | bytes 1572872 | tf_op jit(solution)/shard_map/scatter_g_attn_in_1/ppermute | solution.py:274
  452.7 7.8 %collective-permute-done.76 = bf16[128,2048]{1,0:T(8,128)(2,1)S(1)} collective-permute-done((bf16[128,2048]{1,0:T(8,128)(2,1)S(1)}, bf16[128,2048]{1,0:T(8,128)(2,1)S(1)}, u32[]{:S(2)}, u32[]{:S(2)}) %collective-permute-start.76) | collective-permute-done | bytes 524320 | tf_op jit(solution)/shard_map/scatter_g_attn_in_1/ppermute | solution.py:274
  464.0 9.0 %collective-permute-done.80 = bf16[2,128,2048]{2,1,0:T(8,128)(2,1)S(1)} collective-permute-done((bf16[2,128,2048]{2,1,0:T(8,128)(2,1)S(1)}, bf16[2,128,2048]{2,1,0:T(8,128)(2,1)S(1)}, u32[]{:S(2)}, u32[]{:S(2)}) %collective-permute-start.80) | collective-permute-done | bytes 1048608 | tf_op jit(solution)/shard_map/sum_out_first/ppermute | solution.py:274
  480.9 13.7 %collective-permute-done.81 = bf16[128,2048]{1,0:T(8,128)(2,1)S(1)} collective-permute-done((bf16[128,2048]{1,0:T(8,128)(2,1)S(1)}, bf16[128,2048]{1,0:T(8,128)(2,1)S(1)}, u32[]{:S(2)}, u32[]{:S(2)}) %collective-permute-start.81) | collective-permute-done | bytes 524320 | tf_op jit(solution)/shard_map/scatter_g_attn_in_3/ppermute | solution.py:274
  497.9 21.7 %collective-permute-done.68.refs_1_ = bf16[4,128,2048]{2,1,0:T(8,128)(2,1)} collective-permute-done((bf16[4,128,2048]{2,1,0:T(8,128)(2,1)S(1)}, bf16[4,128,2048]{2,1,0:T(8,128)(2,1)}, u32[]{:S(2)}, u32[]{:S(2)}) %collective-permute-start.68) | collective-permute-done | bytes 2097184 | tf_op jit(solution)/shard_map/sum_glu_across/ppermute | solution.py:274
  539.4 9.5 %collective-permute-done.85 = bf16[128,2048]{1,0:T(8,128)(2,1)S(1)} collective-permute-done((bf16[128,2048]{1,0:T(8,128)(2,1)S(1)}, bf16[128,2048]{1,0:T(8,128)(2,1)S(1)}, u32[]{:S(2)}, u32[]{:S(2)}) %collective-permute-start.85) | collective-permute-done | bytes 524320 | tf_op jit(solution)/shard_map/scatter_ffn_branch_2/ppermute | solution.py:274
  549.2 9.7 %collective-permute-done.86 = bf16[512,2048]{1,0:T(8,128)(2,1)S(1)} collective-permute-done((bf16[512,2048]{1,0:T(8,128)(2,1)S(1)}, bf16[512,2048]{1,0:T(8,128)(2,1)S(1)}, u32[]{:S(2)}, u32[]{:S(2)}) %collective-permute-start.86) | collective-permute-done | bytes 2097184 | tf_op jit(solution)/shard_map/sum_down_second/ppermute | solution.py:274
  569.7 8.6 %place_blocks.8 = (f32[256,8192]{1,0:T(8,128)}, f32[256,8192]{1,0:T(8,128)}) custom-call(s32[32]{0:T(128)S(1)} %reshape.232.row_ref, s32[32]{0:T(128)S(1)} %reshape.233.column_ref, bf16[4,128,2048]{2,1,0:T(8,128)(2,1)S(1)} %pad_maximum_fusion.6.refs_0_, bf16[4,128,2048]{2,1,0:T(8,128)(2,1)} %collective-permute-done.68.refs_1_, ...), custom_call_target="tpu_custom_call" | custom-call | flops 1 | bytes 1 | tf_op jit(solution)/shard_map/place_blocks/pallas_call | solution.py:250
  579.3 15.2 %collective-permute-done.89 = bf16[128,2048]{1,0:T(8,128)(2,1)S(1)} collective-permute-done((bf16[128,2048]{1,0:T(8,128)(2,1)S(1)}, bf16[128,2048]{1,0:T(8,128)(2,1)S(1)}, u32[]{:S(2)}, u32[]{:S(2)}) %collective-permute-start.89) | collective-permute-done | bytes 524320 | tf_op jit(solution)/shard_map/scatter_ffn_branch_3/ppermute | solution.py:274
  613.7 7.4 %collective-permute-done.93.refs_1_ = bf16[4,128,384]{2,1,0:T(8,128)(2,1)S(1)} collective-permute-done((bf16[4,128,384]{2,1,0:T(8,128)(2,1)S(1)}, bf16[4,128,384]{2,1,0:T(8,128)(2,1)S(1)}, u32[]{:S(2)}, u32[]{:S(2)}) %collective-permute-start.93) | collective-permute-done | bytes 393248 | tf_op jit(solution)/shard_map/sum_qkv_across/ppermute | solution.py:274
  (575 shorter events, 394.6 us)
Async XLA Ops:
  14.2 45.5 %collective-permute-start.8 = (bf16[128,2048]{1,0:T(8,128)(2,1)}, bf16[128,2048]{1,0:T(8,128)(2,1)}, u32[]{:S(2)}, u32[]{:S(2)}) collective-permute-start(bf16[128,2048]{1,0:T(8,128)(2,1)} %constant_dynamic-slice_fusion.5), channel_id=1, source_target_pairs={{1,5},{3,7},{5,1},{7,3},{9,13},{11,15},{13,9},{15,11},{17,21},{19,... | collective-permute-start | bytes 1572872 | tf_op jit(solution)/shard_map/w_out_across_y/ppermute | solution.py:274
  24.3 39.0 %collective-permute-start.11 = (bf16[128,2048]{1,0:T(8,128)(2,1)}, bf16[128,2048]{1,0:T(8,128)(2,1)}, u32[]{:S(2)}, u32[]{:S(2)}) collective-permute-start(bf16[128,2048]{1,0:T(8,128)(2,1)} %pad_maximum_fusion.11), channel_id=1, source_target_pairs={{0,8},{1,9},{2,10},{3,11},{4,12},{5,13},{6,14},{7,15},{8,16},{9,17... | collective-permute-start | bytes 1572872 | tf_op jit(solution)/shard_map/w_glu_along_z/ppermute | solution.py:274
  30.4 32.9 %collective-permute-start.12 = (bf16[128,2048]{1,0:T(8,128)(2,1)}, bf16[128,2048]{1,0:T(8,128)(2,1)}, u32[]{:S(2)}, u32[]{:S(2)}) collective-permute-start(bf16[128,2048]{1,0:T(8,128)(2,1)} %pad_maximum_fusion.12), channel_id=1, source_target_pairs={{0,16},{1,17},{2,18},{3,19},{4,20},{5,21},{6,22},{7,23},{8,24},{9,... | collective-permute-start | bytes 1572872 | tf_op jit(solution)/shard_map/w_glu_along_z/ppermute | solution.py:274
  77.8 49.9 %collective-permute-start.20 = (bf16[4,128,2048]{2,1,0:T(8,128)(2,1)}, bf16[4,128,2048]{2,1,0:T(8,128)(2,1)}, u32[]{:S(2)}, u32[]{:S(2)}) collective-permute-start(bf16[4,128,2048]{2,1,0:T(8,128)(2,1)} %pad_maximum_fusion.3.refs_0_), channel_id=1, source_target_pairs={{0,5},{1,4},{2,7},{3,6},{4,1},{5,0},{6,3},{7,2},{8,13},{9,12},{10,... | collective-permute-start | bytes 6291464 | tf_op jit(solution)/shard_map/w_glu_across/ppermute | solution.py:274
  81.7 46.6 %collective-permute-start.19 = (bf16[4,128,2048]{2,1,0:T(8,128)(2,1)}, bf16[4,128,2048]{2,1,0:T(8,128)(2,1)}, u32[]{:S(2)}, u32[]{:S(2)}) collective-permute-start(bf16[4,128,2048]{2,1,0:T(8,128)(2,1)} %pad_maximum_fusion.3.refs_0_), channel_id=1, source_target_pairs={{0,2},{1,3},{2,0},{3,1},{4,6},{5,7},{6,4},{7,5},{8,10},{9,11},{10,... | collective-permute-start | bytes 6291464 | tf_op jit(solution)/shard_map/w_glu_across/ppermute | solution.py:274
  150.5 28.5 %collective-permute-start.10 = (bf16[128,2048]{1,0:T(8,128)(2,1)}, bf16[128,2048]{1,0:T(8,128)(2,1)}, u32[]{:S(2)}, u32[]{:S(2)}) collective-permute-start(bf16[128,2048]{1,0:T(8,128)(2,1)} %get-tuple-element.110), channel_id=1, source_target_pairs={{0,1},{1,0},{2,3},{3,2},{4,5},{5,4},{6,7},{7,6},{8,9},{9,8},{10,11... | collective-permute-start | bytes 1572872 | tf_op jit(solution)/shard_map/scatter_attn_branch_3/ppermute | solution.py:274
  151.0 31.7 %collective-permute-start.16 = (bf16[512,2048]{1,0:T(8,128)(2,1)}, bf16[512,2048]{1,0:T(8,128)(2,1)}, u32[]{:S(2)}, u32[]{:S(2)}) collective-permute-start(bf16[512,2048]{1,0:T(8,128)(2,1)} %collective-permute-done.14), channel_id=1, source_target_pairs={{1,3},{3,1},{5,7},{7,5},{9,11},{11,9},{13,15},{15,13},{17,19},{19,... | collective-permute-start | bytes 6291464 | tf_op jit(solution)/shard_map/w_down_across_x/ppermute | solution.py:274
  168.2 33.2 %collective-permute-start.39 = (bf16[128,2048]{1,0:T(8,128)(2,1)}, bf16[128,2048]{1,0:T(8,128)(2,1)S(1)}, u32[]{:S(2)}, u32[]{:S(2)}) collective-permute-start(bf16[128,2048]{1,0:T(8,128)(2,1)} %param.27), channel_id=1, source_target_pairs={{0,1},{1,0},{2,3},{3,2},{4,5},{5,4},{6,7},{7,6},{8,9},{9,8},{10,11... | collective-permute-start | bytes 1572872 | tf_op jit(solution)/shard_map/gather_d_out_0/ppermute | solution.py:274
  207.2 103.3 %collective-permute-start.50 = (bf16[128,2048]{1,0:T(8,128)(2,1)}, bf16[128,2048]{1,0:T(8,128)(2,1)S(1)}, u32[]{:S(2)}, u32[]{:S(2)}) collective-permute-start(bf16[128,2048]{1,0:T(8,128)(2,1)} %slice.223), channel_id=1, source_target_pairs={{0,1},{1,0},{2,3},{3,2},{4,5},{5,4},{6,7},{7,6},{8,9},{9,8},{10,11... | collective-permute-start | bytes 1572872 | tf_op jit(solution)/shard_map/scatter_g_ffn_in_3/ppermute | solution.py:274
  308.9 46.0 %collective-permute-start.58 = (bf16[4,2,128,1024]{3,2,0,1:T(8,128)(2,1)S(1)}, bf16[4,2,128,1024]{3,2,0,1:T(8,128)(2,1)S(1)}, u32[]{:S(2)}, u32[]{:S(2)}) collective-permute-start(bf16[4,2,128,1024]{3,2,0,1:T(8,128)(2,1)S(1)} %copy_bitcast_fusion), channel_id=1, source_target_pairs={{0,2},{1,3},{2,0},{3,1},{4,6},{5,7},{6,4},{7,5},{8,10},{9,11},{10,... | collective-permute-start | bytes 6291464 | tf_op jit(solution)/shard_map/sum_up_first/ppermute | solution.py:274
  310.5 47.0 %collective-permute-start.49 = (bf16[4,2,128,1024]{3,2,0,1:T(8,128)(2,1)S(1)}, bf16[4,2,128,1024]{3,2,0,1:T(8,128)(2,1)S(1)}, u32[]{:S(2)}, u32[]{:S(2)}) collective-permute-start(bf16[4,2,128,1024]{3,2,0,1:T(8,128)(2,1)S(1)} %copy_bitcast_fusion.1), channel_id=1, source_target_pairs={{0,5},{1,4},{2,7},{3,6},{4,1},{5,0},{6,3},{7,2},{8,13},{9,12},{10,... | collective-permute-start | bytes 6291464 | tf_op jit(solution)/shard_map/sum_gate_first/ppermute | solution.py:274
  346.0 29.9 %collective-permute-start.75 = (bf16[128,2048]{1,0:T(8,128)(2,1)S(1)}, bf16[128,2048]{1,0:T(8,128)(2,1)S(1)}, u32[]{:S(2)}, u32[]{:S(2)}) collective-permute-start(bf16[128,2048]{1,0:T(8,128)(2,1)S(1)} %get-tuple-element.138), channel_id=1, source_target_pairs={{0,1},{1,0},{2,3},{3,2},{4,5},{5,4},{6,7},{7,6},{8,9},{9,8},{10,11... | collective-permute-start | bytes 1572872 | tf_op jit(solution)/shard_map/scatter_g_attn_in_0/ppermute | solution.py:274
  375.3 74.5 %collective-permute-start.74 = (bf16[128,2048]{1,0:T(8,128)(2,1)S(1)}, bf16[128,2048]{1,0:T(8,128)(2,1)}, u32[]{:S(2)}, u32[]{:S(2)}) collective-permute-start(bf16[128,2048]{1,0:T(8,128)(2,1)S(1)} %get-tuple-element.143), channel_id=1, source_target_pairs={{0,1},{1,0},{2,3},{3,2},{4,5},{5,4},{6,7},{7,6},{8,9},{9,8},{10,11... | collective-permute-start | bytes 1572872 | tf_op jit(solution)/shard_map/scatter_g_attn_in_1/ppermute | solution.py:274
  394.8 83.6 %collective-permute-start.78 = (bf16[2,512,2048]{2,1,0:T(8,128)(2,1)S(1)}, bf16[2,512,2048]{2,1,0:T(8,128)(2,1)S(1)}, u32[]{:S(2)}, u32[]{:S(2)}) collective-permute-start(bf16[2,512,2048]{2,1,0:T(8,128)(2,1)S(1)} %bitcast.190), channel_id=1, source_target_pairs={{1,4},{3,6},{5,0},{7,2},{9,12},{11,14},{13,8},{15,10},{17,20},{19,... | collective-permute-start | bytes 12582920 | tf_op jit(solution)/shard_map/sum_down_first/ppermute | solution.py:274
  400.5 35.9 %collective-permute-start.62 = (bf16[128,2048]{1,0:T(8,128)(2,1)}, bf16[128,2048]{1,0:T(8,128)(2,1)}, u32[]{:S(2)}, u32[]{:S(2)}) collective-permute-start(bf16[128,2048]{1,0:T(8,128)(2,1)} %pad_maximum_fusion.15), channel_id=1, source_target_pairs={{0,16},{1,17},{2,18},{3,19},{4,20},{5,21},{6,22},{7,23},{8,24},{9,... | collective-permute-start | bytes 1572872 | tf_op jit(solution)/shard_map/sum_glu_along_z_2/ppermute | solution.py:274
  410.9 52.5 %collective-permute-start.79 = (bf16[4,2,128,384]{3,2,0,1:T(8,128)(2,1)S(1)}, bf16[4,2,128,384]{3,2,0,1:T(8,128)(2,1)S(1)}, u32[]{:S(2)}, u32[]{:S(2)}) collective-permute-start(bf16[4,2,128,384]{3,2,0,1:T(8,128)(2,1)S(1)} %copy_bitcast_fusion.2), channel_id=1, source_target_pairs={{0,5},{1,4},{2,7},{3,6},{4,1},{5,0},{6,3},{7,2},{8,13},{9,12},{10,... | collective-permute-start | bytes 2359304 | tf_op jit(solution)/shard_map/sum_qkv_first/ppermute | solution.py:274
  413.8 33.2 %collective-permute-start.63 = (bf16[128,2048]{1,0:T(8,128)(2,1)S(1)}, bf16[128,2048]{1,0:T(8,128)(2,1)S(1)}, u32[]{:S(2)}, u32[]{:S(2)}) collective-permute-start(bf16[128,2048]{1,0:T(8,128)(2,1)S(1)} %pad_maximum_fusion.16), channel_id=1, source_target_pairs={{0,24},{1,25},{2,26},{3,27},{4,28},{5,29},{6,30},{7,31},{8,0},{9,1... | collective-permute-start | bytes 1572872 | tf_op jit(solution)/shard_map/sum_glu_along_z_3/ppermute | solution.py:274
  473.0 46.7 %collective-permute-start.68 = (bf16[4,128,2048]{2,1,0:T(8,128)(2,1)S(1)}, bf16[4,128,2048]{2,1,0:T(8,128)(2,1)}, u32[]{:S(2)}, u32[]{:S(2)}) collective-permute-start(bf16[4,128,2048]{2,1,0:T(8,128)(2,1)S(1)} %pad_maximum_fusion.6.refs_0_), channel_id=1, source_target_pairs={{0,2},{1,3},{2,0},{3,1},{4,6},{5,7},{6,4},{7,5},{8,10},{9,11},{10,... | collective-permute-start | bytes 6291464 | tf_op jit(solution)/shard_map/sum_glu_across/ppermute | solution.py:274
  480.6 46.8 %collective-permute-start.66 = (bf16[128,2048]{1,0:T(8,128)(2,1)S(1)}, bf16[128,2048]{1,0:T(8,128)(2,1)S(1)}, u32[]{:S(2)}, u32[]{:S(2)}) collective-permute-start(bf16[128,2048]{1,0:T(8,128)(2,1)S(1)} %slice.231), channel_id=1, source_target_pairs={{0,1},{1,0},{2,3},{3,2},{4,5},{5,4},{6,7},{7,6},{8,9},{9,8},{10,11... | collective-permute-start | bytes 1572872 | tf_op jit(solution)/shard_map/scatter_ffn_branch_1/ppermute | solution.py:274
  527.4 31.5 %collective-permute-start.86 = (bf16[512,2048]{1,0:T(8,128)(2,1)S(1)}, bf16[512,2048]{1,0:T(8,128)(2,1)S(1)}, u32[]{:S(2)}, u32[]{:S(2)}) collective-permute-start(bf16[512,2048]{1,0:T(8,128)(2,1)S(1)} %fusion.12), channel_id=1, source_target_pairs={{0,2},{2,0},{4,6},{6,4},{8,10},{10,8},{12,14},{14,12},{16,18},{18,... | collective-permute-start | bytes 6291464 | tf_op jit(solution)/shard_map/sum_down_second/ppermute | solution.py:274
  538.9 30.7 %collective-permute-start.87 = (bf16[4,128,2048]{2,1,0:T(8,128)(2,1)S(1)}, bf16[4,128,2048]{2,1,0:T(8,128)(2,1)}, u32[]{:S(2)}, u32[]{:S(2)}) collective-permute-start(bf16[4,128,2048]{2,1,0:T(8,128)(2,1)S(1)} %pad_maximum_fusion.6.refs_0_), channel_id=1, source_target_pairs={{0,1},{1,0},{2,3},{3,2},{4,5},{5,4},{6,7},{7,6},{8,9},{9,8},{10,11... | collective-permute-start | bytes 6291464 | tf_op jit(solution)/shard_map/sum_glu_core/ppermute | solution.py:274
  538.9 30.7 %collective-permute-start.88 = (bf16[4,128,2048]{2,1,0:T(8,128)(2,1)}, bf16[4,128,2048]{2,1,0:T(8,128)(2,1)}, u32[]{:S(2)}, u32[]{:S(2)}) collective-permute-start(bf16[4,128,2048]{2,1,0:T(8,128)(2,1)} %collective-permute-done.68.refs_1_), channel_id=1, source_target_pairs={{0,1},{1,0},{2,3},{3,2},{4,5},{5,4},{6,7},{7,6},{8,9},{9,8},{10,11... | collective-permute-start | bytes 6291464 | tf_op jit(solution)/shard_map/sum_glu_core/ppermute | solution.py:274
  561.6 34.8 %collective-permute-start.98 = (bf16[512,2048]{1,0:T(8,128)(2,1)}, bf16[512,2048]{1,0:T(8,128)(2,1)}, u32[]{:S(2)}, u32[]{:S(2)}) collective-permute-start(bf16[512,2048]{1,0:T(8,128)(2,1)} %fusion.8), channel_id=1, source_target_pairs={{0,2},{2,0},{4,6},{6,4},{8,10},{10,8},{12,14},{14,12},{16,18},{18,... | collective-permute-start | bytes 6291464 | tf_op jit(solution)/shard_map/sum_down_third/ppermute | solution.py:274
  601.1 50.0 %collective-permute-start.99 = (bf16[2,512,2048]{2,1,0:T(8,128)(2,1)}, bf16[2,512,2048]{2,1,0:T(8,128)(2,1)}, u32[]{:S(2)}, u32[]{:S(2)}) collective-permute-start(bf16[2,512,2048]{2,1,0:T(8,128)(2,1)} %pad_maximum_fusion.2), channel_id=1, source_target_pairs={{0,1},{2,3},{4,5},{6,7},{8,9},{10,11},{12,13},{14,15},{16,17},{18,... | collective-permute-start | bytes 12582920 | tf_op jit(solution)/shard_map/sum_down_last/ppermute | solution.py:274
  (175 other events, 3164.4 us)

commit v5 on v4

--- a/solution.py
+++ b/solution.py
@@ -702,7 +702,7 @@
             for item in (down_sum, qkv_sum, out_sum):
                 item.first(sent)
         if step == 2:
-            sent = after(sent, down_sum.payload, qkv_sum.payload, out_sum.payload)
+            sent = after(sent, down_sum.payload, qkv_sum.payload, out_sum.payload, glu_across)
         return sent
 
     g_attn_in = scatter_group(partial, "g_attn_in", beside_back)
@@ -712,30 +712,32 @@
     for s in range(depth):
         part = matmul(after(glu_kept[s][2], glu_same), w_down_here).astype(BF)
         down_partial.append((part[:block_rows], part[block_rows:]))
-    ffn_ties = {0: (glu_across, d_tokens)}
-    glu_placed = []
+    glu_placed = columns_placed(glu_same, glu_across, [columns_here, columns_here], "glu")
+
+    arrived = []
 
     def beside_branch(step, sent):
+        arrived.append(sent)
         if step == 0:
-            glu_placed.extend(columns_placed(glu_same, glu_across, [columns_here, columns_here], "glu"))
+            return after(sent, d_tokens)
         if step == 1:
-            qkv_sum.second(sent)
-            out_sum.second(sent)
-            ffn_ties[1] = (qkv_sum.payload, out_sum.payload)
+            down_sum.second(d_tokens)
+            return after(sent, down_sum.payload)
         if step == 2:
-            down_sum.second(sent)
-            ffn_ties[2] = (down_sum.payload, *glu_placed)
-        return after(sent, *ffn_ties.get(step, ()))
+            qkv_sum.second(arrived[1])
+            out_sum.second(arrived[1])
+            return after(sent, qkv_sum.payload, out_sum.payload)
+        return sent
 
     ffn_branch = scatter_group(down_partial, "ffn_branch", beside_branch)
-    block = middle + ffn_branch
+    block = middle + after(ffn_branch, *glu_placed)
     grad_gate, grad_up = glu_placed
     qkv_slots = along_z([qkv_sum.payload], "qkv")
-    qkv_same = jnp.stack(qkv_slots)
+    qkv_same = jnp.stack(after((*qkv_slots,), arrived[2]))
     qkv_across = across_x(qkv_same, "qkv")
     grad_query, grad_kv = columns_placed(qkv_same, qkv_across, [q_cols, 2 * kv_cols], "qkv")
-    down_sum.third(ffn_branch)
-    out_sum.third(ffn_branch)
+    down_sum.third()
+    out_sum.third()
     grad_down, grad_out = down_sum.last(), out_sum.last()
     grad_kv = grad_kv.reshape(grad_kv.shape[0], -1, share, 2 * kv_cols).sum(axis=2)
     grad_key = grad_kv[:, :, :kv_cols].reshape(grad_kv.shape[0], -1)

time: 669 us -> 655 us (0.979)
  waiting for transfers between devices: 294 us -> 260 us
  starting transfers between devices: 113 us -> 131 us
  matrix products: 69.4 us -> 60.6 us
  local copies, waits for them, and re-layouts: 46.7 us -> 54.4 us
    ppermute x105, waiting for transfers between devices: 294 us -> 260 us  [move(): return lax.ppermute(values, ('fsdp', 'rep'), pairs)]
    ppermute x105, starting transfers between devices: 113 us -> 131 us  [move(): return lax.ppermute(values, ('fsdp', 'rep'), pairs)]
    unnamed x207 -> x253, local copies, waits for them, and re-layouts: 17.3 us -> 22.7 us
  transfers between devices with their start and end apart: 105 -> 105, of which waited for: 43 -> 43; matrix products, arithmetic and copies ran while one was open for 24% -> 24% of each run, Pallas kernels for 10% -> 11%
where the time goes in v5:
time: 655 us; the launch traced here: 645 us
  waiting for transfers between devices  260 us (40%)
  starting transfers between devices  131 us (20%)
  Pallas kernels  73.8 us (11%)
  other arithmetic  61.3 us (9%)
  matrix products  60.6 us (9%)
  local copies, waits for them, and re-layouts  54.4 us (8%)
    ppermute x105, waiting for transfers between devices, move(): return lax.ppermute(values, ('fsdp', 'rep'), pairs)  260 us
    ppermute x105, starting transfers between devices, move(): return lax.ppermute(values, ('fsdp', 'rep'), pairs)  131 us
    pallas_call x8, Pallas kernels, slot_call(): pl.pallas_call(kernel, grid=(1,), in_specs=specs, out_specs=[single(shape...  45.4 us
    pallas_call x6, Pallas kernels, place_blocks(): pl.pallas_call(functools.partial(place_kernel, moves, len(sources), len(s...  28.4 us
    dot_general x8, matrix products, right_tmul(): lax.dot_general(left, right, (((1,), (1,)), ((), ())), preferred_element_...  22.9 us
    unnamed x253, local copies, waits for them, and re-layouts  22.7 us
    dot_general x5, matrix products, left_tmul(): lax.dot_general(left, right, (((0,), (0,)), ((), ())), preferred_element_...  20.8 us
    dot_general x8, matrix products, matmul(): return jnp.dot(left, right, preferred_element_type=F32)  17 us
  transfers between devices with their start and end apart: 105, of which 43 were waited for; matrix products, arithmetic and copies ran while one was open for 24% of the time, Pallas kernels for 11%

profile of v5, /device:TPU:0, one launch (start us, length us, event | category | flops | bytes accessed | tf_op | source)
XLA Modules:
  0.0 645.4 jit_solution(2697517730941296448)
XLA Ops:
  38.0 7.4 %collective-permute-done.7.refs_3_ = bf16[4,144,384]{2,1,0:T(8,128)(2,1)S(1)} collective-permute-done((bf16[4,144,384]{2,1,0:T(8,128)(2,1)S(1)}, bf16[4,144,384]{2,1,0:T(8,128)(2,1)S(1)}, u32[]{:S(2)}, u32[]{:S(2)}) %collective-permute-start.7) | collective-permute-done | bytes 442400 | tf_op jit(solution)/shard_map/w_qkv_across_both/ppermute | solution.py:274
  66.7 11.6 %collective-permute-start.15 = (bf16[128,2048]{1,0:T(8,128)(2,1)S(1)}, bf16[128,2048]{1,0:T(8,128)(2,1)}, u32[]{:S(2)}, u32[]{:S(2)}) collective-permute-start(bf16[128,2048]{1,0:T(8,128)(2,1)S(1)} %copy-done.4), channel_id=1, source_target_pairs={{0,8},{1,9},{2,10},{3,11},{4,12},{5,13},{6,14},{7,15},{8,16},{9,17... | collective-permute-start | bytes 1572872 | tf_op jit(solution)/shard_map/gather_tokens_1/ppermute | solution.py:274
  81.8 8.2 %collective-permute-done.15.refs_0_ = bf16[128,2048]{1,0:T(8,128)(2,1)} collective-permute-done((bf16[128,2048]{1,0:T(8,128)(2,1)S(1)}, bf16[128,2048]{1,0:T(8,128)(2,1)}, u32[]{:S(2)}, u32[]{:S(2)}) %collective-permute-start.15) | collective-permute-done | bytes 524320 | tf_op jit(solution)/shard_map/gather_tokens_1/ppermute | solution.py:274
  114.1 10.3 %collective-permute-done.18.refs_0_ = bf16[128,2048]{1,0:T(8,128)(2,1)S(1)} collective-permute-done((bf16[128,2048]{1,0:T(8,128)(2,1)S(1)}, bf16[128,2048]{1,0:T(8,128)(2,1)S(1)}, u32[]{:S(2)}, u32[]{:S(2)}) %collective-permute-start.18) | collective-permute-done | bytes 524320 | tf_op jit(solution)/shard_map/gather_tokens_3/ppermute | solution.py:274
  128.1 7.1 %collective-permute-done.27 = bf16[128,2048]{1,0:T(8,128)(2,1)S(1)} collective-permute-done((bf16[128,2048]{1,0:T(8,128)(2,1)S(1)}, bf16[128,2048]{1,0:T(8,128)(2,1)S(1)}, u32[]{:S(2)}, u32[]{:S(2)}) %collective-permute-start.27) | collective-permute-done | bytes 524320 | tf_op jit(solution)/shard_map/scatter_attn_branch_1/ppermute | solution.py:274
  154.7 14.1 %collective-permute-done.31.refs_4_ = bf16[2,128,2048]{2,1,0:T(8,128)(2,1)} collective-permute-done((bf16[2,128,2048]{2,1,0:T(8,128)(2,1)}, bf16[2,128,2048]{2,1,0:T(8,128)(2,1)}, u32[]{:S(2)}, u32[]{:S(2)}) %collective-permute-start.31) | collective-permute-done | bytes 1048608 | tf_op jit(solution)/shard_map/w_glu_across_both/ppermute | solution.py:274
  172.3 7.2 %place_blocks.7 = bf16[2048,2048]{1,0:T(8,128)(2,1)} custom-call(s32[16]{0:T(128)S(1)} %copy-done.24, s32[16]{0:T(128)S(1)} %copy-done.26, bf16[4,128,2048]{2,1,0:T(8,128)(2,1)} %pad_maximum_fusion.3.refs_0_, bf16[4,128,2048]{2,1,0:T(8,128)(2,1)} %collective-permute-done.19.refs_1_, bf16[4,128,2048]{2,1,0:T(8,128)(2,1)} %collective-permute-done.20.refs_2_, ...), custom_call_target="tpu_custom_call" | custom-call | flops 1 | bytes 1 | tf_op jit(solution)/shard_map/place_blocks/pallas_call | solution.py:250
  186.0 13.1 %collective-permute-done.33 = bf16[128,2048]{1,0:T(8,128)(2,1)S(1)} collective-permute-done((bf16[128,2048]{1,0:T(8,128)(2,1)S(1)}, bf16[128,2048]{1,0:T(8,128)(2,1)S(1)}, u32[]{:S(2)}, u32[]{:S(2)}) %collective-permute-start.33) | collective-permute-done | bytes 524320 | tf_op jit(solution)/shard_map/gather_ffn_in_1/ppermute | solution.py:274
  218.7 10.3 %collective-permute-done.37 = bf16[128,2048]{1,0:T(8,128)(2,1)S(1)} collective-permute-done((bf16[128,2048]{1,0:T(8,128)(2,1)S(1)}, bf16[128,2048]{1,0:T(8,128)(2,1)S(1)}, u32[]{:S(2)}, u32[]{:S(2)}) %collective-permute-start.37) | collective-permute-done | bytes 524320 | tf_op jit(solution)/shard_map/gather_ffn_in_3/ppermute | solution.py:274
  234.3 8.0 %collective-permute-done.40 = bf16[128,2048]{1,0:T(8,128)(2,1)S(1)} collective-permute-done((bf16[128,2048]{1,0:T(8,128)(2,1)S(1)}, bf16[128,2048]{1,0:T(8,128)(2,1)S(1)}, u32[]{:S(2)}, u32[]{:S(2)}) %collective-permute-start.40) | collective-permute-done | bytes 524320 | tf_op jit(solution)/shard_map/gather_d_out_1/ppermute | solution.py:274
  246.9 7.9 %collective-permute-done.42 = bf16[128,2048]{1,0:T(8,128)(2,1)S(1)} collective-permute-done((bf16[128,2048]{1,0:T(8,128)(2,1)S(1)}, bf16[128,2048]{1,0:T(8,128)(2,1)S(1)}, u32[]{:S(2)}, u32[]{:S(2)}) %collective-permute-start.42) | collective-permute-done | bytes 524320 | tf_op jit(solution)/shard_map/gather_d_out_2/ppermute | solution.py:274
  308.9 12.5 %collective-permute-done.53 = bf16[128,2048]{1,0:T(8,128)(2,1)S(1)} collective-permute-done((bf16[128,2048]{1,0:T(8,128)(2,1)S(1)}, bf16[128,2048]{1,0:T(8,128)(2,1)S(1)}, u32[]{:S(2)}, u32[]{:S(2)}) %collective-permute-start.53) | collective-permute-done | bytes 524320 | tf_op jit(solution)/shard_map/scatter_g_ffn_in_3/ppermute | solution.py:274
  326.3 11.0 %collective-permute-done.54.refs_0_ = bf16[128,2048]{1,0:T(8,128)(2,1)} collective-permute-done((bf16[128,2048]{1,0:T(8,128)(2,1)}, bf16[128,2048]{1,0:T(8,128)(2,1)}, u32[]{:S(2)}, u32[]{:S(2)}) %collective-permute-start.54) | collective-permute-done | bytes 524320 | tf_op jit(solution)/shard_map/gather_g_attn_1/ppermute | solution.py:274
  340.1 7.1 %attention_back.4 = (bf16[256,2048]{1,0:T(8,128)(2,1)S(1)}, bf16[256,384]{1,0:T(8,128)(2,1)S(1)}, bf16[128,2048]{1,0:T(8,128)(2,1)S(1)}, bf16[128,2048]{1,0:T(8,128)(2,1)S(1)}, f32[2,64]{1,0:T(2,128)S(1)}) custom-call(bf16[128,2048]{1,0:T(8,128)(2,1)} %collective-permute-done.54.refs_0_, bf16[128,2048]{1,0:T(8,128)(2,1)S(1)} %collective-permute-done.55.refs_1_, ...), custom_call_target="tpu_custom_call" | custom-call | flops 1 | bytes 1 | tf_op jit(solution)/shard_map/attention_back/pallas_call | solution.py:159
  358.0 7.0 %attention_back.6 = (bf16[256,2048]{1,0:T(8,128)(2,1)S(1)}, bf16[256,384]{1,0:T(8,128)(2,1)S(1)}, bf16[128,2048]{1,0:T(8,128)(2,1)S(1)}, bf16[128,2048]{1,0:T(8,128)(2,1)S(1)}, f32[2,64]{1,0:T(2,128)S(1)}) custom-call(bf16[128,2048]{1,0:T(8,128)(2,1)} %fusion.127.refs_0_, bf16[128,2048]{1,0:T(8,128)(2,1)S(1)} %collective-permute-done.68.refs_1_, ...), custom_call_target="tpu_custom_call" | custom-call | flops 1 | bytes 1 | tf_op jit(solution)/shard_map/attention_back/pallas_call | solution.py:159
  366.2 7.1 %collective-permute-done.49 = bf16[4,2,128,1024]{3,2,0,1:T(8,128)(2,1)S(1)} collective-permute-done((bf16[4,2,128,1024]{3,2,0,1:T(8,128)(2,1)}, bf16[4,2,128,1024]{3,2,0,1:T(8,128)(2,1)S(1)}, u32[]{:S(2)}, u32[]{:S(2)}) %collective-permute-start.49) | collective-permute-done | bytes 2097184 | tf_op jit(solution)/shard_map/sum_gate_first/ppermute | solution.py:274
  375.3 6.8 %attention_back.5 = (bf16[256,2048]{1,0:T(8,128)(2,1)S(1)}, bf16[256,384]{1,0:T(8,128)(2,1)S(1)}, bf16[128,2048]{1,0:T(8,128)(2,1)S(1)}, bf16[128,2048]{1,0:T(8,128)(2,1)}, f32[2,64]{1,0:T(2,128)S(1)}) custom-call(bf16[128,2048]{1,0:T(8,128)(2,1)S(1)} %collective-permute-done.57.refs_0_, bf16[128,2048]{1,0:T(8,128)(2,1)S(1)} %collective-permute-done.59.refs_1_, ...), custom_call_target="tpu_custom_call" | custom-call | flops 1 | bytes 1 | tf_op jit(solution)/shard_map/attention_back/pallas_call | solution.py:159
  382.6 12.2 %collective-permute-done.60 = bf16[4,128,1024]{2,1,0:T(8,128)(2,1)S(1)} collective-permute-done((bf16[4,128,1024]{2,1,0:T(8,128)(2,1)S(1)}, bf16[4,128,1024]{2,1,0:T(8,128)(2,1)S(1)}, u32[]{:S(2)}, u32[]{:S(2)}) %collective-permute-start.60) | collective-permute-done | bytes 1048608 | tf_op jit(solution)/shard_map/sum_up_second/ppermute | solution.py:274
  426.3 19.0 %collective-permute-done.62 = bf16[128,2048]{1,0:T(8,128)(2,1)S(1)} collective-permute-done((bf16[128,2048]{1,0:T(8,128)(2,1)S(1)}, bf16[128,2048]{1,0:T(8,128)(2,1)S(1)}, u32[]{:S(2)}, u32[]{:S(2)}) %collective-permute-start.62) | collective-permute-done | bytes 524320 | tf_op jit(solution)/shard_map/sum_glu_along_z_2/ppermute | solution.py:274
  484.9 12.0 %collective-permute-done.80.refs_1_ = bf16[4,128,2048]{2,1,0:T(8,128)(2,1)} collective-permute-done((bf16[4,128,2048]{2,1,0:T(8,128)(2,1)S(1)}, bf16[4,128,2048]{2,1,0:T(8,128)(2,1)}, u32[]{:S(2)}, u32[]{:S(2)}) %collective-permute-start.80) | collective-permute-done | bytes 2097184 | tf_op jit(solution)/shard_map/sum_glu_across/ppermute | solution.py:274
  502.4 17.5 %collective-permute-start.67 = (bf16[128,2048]{1,0:T(8,128)(2,1)S(1)}, bf16[128,2048]{1,0:T(8,128)(2,1)S(1)}, u32[]{:S(2)}, u32[]{:S(2)}) collective-permute-start(bf16[128,2048]{1,0:T(8,128)(2,1)S(1)} %slice.233), channel_id=1, source_target_pairs={{0,1},{1,0},{2,3},{3,2},{4,5},{5,4},{6,7},{7,6},{8,9},{9,8},{10,11... | collective-permute-start | bytes 1572872 | tf_op jit(solution)/shard_map/scatter_ffn_branch_0/ppermute | solution.py:274
  540.3 10.9 %collective-permute-done.82 = bf16[128,2048]{1,0:T(8,128)(2,1)S(1)} collective-permute-done((bf16[128,2048]{1,0:T(8,128)(2,1)S(1)}, bf16[128,2048]{1,0:T(8,128)(2,1)S(1)}, u32[]{:S(2)}, u32[]{:S(2)}) %collective-permute-start.82) | collective-permute-done | bytes 524320 | tf_op jit(solution)/shard_map/scatter_ffn_branch_1/ppermute | solution.py:274
  552.0 7.3 %collective-permute-done.98 = bf16[512,2048]{1,0:T(8,128)(2,1)S(1)} collective-permute-done((bf16[512,2048]{1,0:T(8,128)(2,1)S(1)}, bf16[512,2048]{1,0:T(8,128)(2,1)S(1)}, u32[]{:S(2)}, u32[]{:S(2)}) %collective-permute-start.98) | collective-permute-done | bytes 2097184 | tf_op jit(solution)/shard_map/sum_down_third/ppermute | solution.py:274
  585.9 7.9 %place_blocks.8 = (f32[256,8192]{1,0:T(8,128)}, f32[256,8192]{1,0:T(8,128)}) custom-call(s32[32]{0:T(128)S(1)} %reshape.232.row_ref, s32[32]{0:T(128)S(1)} %reshape.233.column_ref, bf16[4,128,2048]{2,1,0:T(8,128)(2,1)S(1)} %pad_maximum_fusion.6.refs_0_, bf16[4,128,2048]{2,1,0:T(8,128)(2,1)} %collective-permute-done.80.refs_1_, ...), custom_call_target="tpu_custom_call" | custom-call | flops 1 | bytes 1 | tf_op jit(solution)/shard_map/place_blocks/pallas_call | solution.py:250
  (621 shorter events, 398.3 us)
Async XLA Ops:
  14.2 45.3 %collective-permute-start.8 = (bf16[128,2048]{1,0:T(8,128)(2,1)}, bf16[128,2048]{1,0:T(8,128)(2,1)}, u32[]{:S(2)}, u32[]{:S(2)}) collective-permute-start(bf16[128,2048]{1,0:T(8,128)(2,1)} %constant_dynamic-slice_fusion.4), channel_id=1, source_target_pairs={{1,5},{3,7},{5,1},{7,3},{9,13},{11,15},{13,9},{15,11},{17,21},{19,... | collective-permute-start | bytes 1572872 | tf_op jit(solution)/shard_map/w_out_across_y/ppermute | solution.py:274
  24.9 38.9 %collective-permute-start.11 = (bf16[128,2048]{1,0:T(8,128)(2,1)}, bf16[128,2048]{1,0:T(8,128)(2,1)}, u32[]{:S(2)}, u32[]{:S(2)}) collective-permute-start(bf16[128,2048]{1,0:T(8,128)(2,1)} %pad_maximum_fusion.11), channel_id=1, source_target_pairs={{0,8},{1,9},{2,10},{3,11},{4,12},{5,13},{6,14},{7,15},{8,16},{9,17... | collective-permute-start | bytes 1572872 | tf_op jit(solution)/shard_map/w_glu_along_z/ppermute | solution.py:274
  30.4 33.3 %collective-permute-start.12 = (bf16[128,2048]{1,0:T(8,128)(2,1)}, bf16[128,2048]{1,0:T(8,128)(2,1)}, u32[]{:S(2)}, u32[]{:S(2)}) collective-permute-start(bf16[128,2048]{1,0:T(8,128)(2,1)} %pad_maximum_fusion.12), channel_id=1, source_target_pairs={{0,16},{1,17},{2,18},{3,19},{4,20},{5,21},{6,22},{7,23},{8,24},{9,... | collective-permute-start | bytes 1572872 | tf_op jit(solution)/shard_map/w_glu_along_z/ppermute | solution.py:274
  78.3 48.7 %collective-permute-start.20 = (bf16[4,128,2048]{2,1,0:T(8,128)(2,1)}, bf16[4,128,2048]{2,1,0:T(8,128)(2,1)}, u32[]{:S(2)}, u32[]{:S(2)}) collective-permute-start(bf16[4,128,2048]{2,1,0:T(8,128)(2,1)} %pad_maximum_fusion.3.refs_0_), channel_id=1, source_target_pairs={{0,5},{1,4},{2,7},{3,6},{4,1},{5,0},{6,3},{7,2},{8,13},{9,12},{10,... | collective-permute-start | bytes 6291464 | tf_op jit(solution)/shard_map/w_glu_across/ppermute | solution.py:274
  81.3 46.8 %collective-permute-start.19 = (bf16[4,128,2048]{2,1,0:T(8,128)(2,1)}, bf16[4,128,2048]{2,1,0:T(8,128)(2,1)}, u32[]{:S(2)}, u32[]{:S(2)}) collective-permute-start(bf16[4,128,2048]{2,1,0:T(8,128)(2,1)} %pad_maximum_fusion.3.refs_0_), channel_id=1, source_target_pairs={{0,2},{1,3},{2,0},{3,1},{4,6},{5,7},{6,4},{7,5},{8,10},{9,11},{10,... | collective-permute-start | bytes 6291464 | tf_op jit(solution)/shard_map/w_glu_across/ppermute | solution.py:274
  168.8 33.2 %collective-permute-start.39 = (bf16[128,2048]{1,0:T(8,128)(2,1)}, bf16[128,2048]{1,0:T(8,128)(2,1)S(1)}, u32[]{:S(2)}, u32[]{:S(2)}) collective-permute-start(bf16[128,2048]{1,0:T(8,128)(2,1)} %param.27), channel_id=1, source_target_pairs={{0,1},{1,0},{2,3},{3,2},{4,5},{5,4},{6,7},{7,6},{8,9},{9,8},{10,11... | collective-permute-start | bytes 1572872 | tf_op jit(solution)/shard_map/gather_d_out_0/ppermute | solution.py:274
  207.7 101.3 %collective-permute-start.50 = (bf16[128,2048]{1,0:T(8,128)(2,1)S(1)}, bf16[128,2048]{1,0:T(8,128)(2,1)S(1)}, u32[]{:S(2)}, u32[]{:S(2)}) collective-permute-start(bf16[128,2048]{1,0:T(8,128)(2,1)S(1)} %slice.223), channel_id=1, source_target_pairs={{0,1},{1,0},{2,3},{3,2},{4,5},{5,4},{6,7},{7,6},{8,9},{9,8},{10,11... | collective-permute-start | bytes 1572872 | tf_op jit(solution)/shard_map/scatter_g_ffn_in_3/ppermute | solution.py:274
  307.4 46.4 %collective-permute-start.58 = (bf16[4,2,128,1024]{3,2,0,1:T(8,128)(2,1)}, bf16[4,2,128,1024]{3,2,0,1:T(8,128)(2,1)}, u32[]{:S(2)}, u32[]{:S(2)}) collective-permute-start(bf16[4,2,128,1024]{3,2,0,1:T(8,128)(2,1)} %copy_bitcast_fusion), channel_id=1, source_target_pairs={{0,2},{1,3},{2,0},{3,1},{4,6},{5,7},{6,4},{7,5},{8,10},{9,11},{10,... | collective-permute-start | bytes 6291464 | tf_op jit(solution)/shard_map/sum_up_first/ppermute | solution.py:274
  325.1 48.2 %collective-permute-start.49 = (bf16[4,2,128,1024]{3,2,0,1:T(8,128)(2,1)}, bf16[4,2,128,1024]{3,2,0,1:T(8,128)(2,1)S(1)}, u32[]{:S(2)}, u32[]{:S(2)}) collective-permute-start(bf16[4,2,128,1024]{3,2,0,1:T(8,128)(2,1)} %copy_bitcast_fusion.1), channel_id=1, source_target_pairs={{0,5},{1,4},{2,7},{3,6},{4,1},{5,0},{6,3},{7,2},{8,13},{9,12},{10,... | collective-permute-start | bytes 6291464 | tf_op jit(solution)/shard_map/sum_gate_first/ppermute | solution.py:274
  355.4 39.4 %collective-permute-start.60 = (bf16[4,128,1024]{2,1,0:T(8,128)(2,1)S(1)}, bf16[4,128,1024]{2,1,0:T(8,128)(2,1)S(1)}, u32[]{:S(2)}, u32[]{:S(2)}) collective-permute-start(bf16[4,128,1024]{2,1,0:T(8,128)(2,1)S(1)} %fusion.15), channel_id=1, source_target_pairs={{0,5},{1,4},{2,7},{3,6},{4,1},{5,0},{6,3},{7,2},{8,13},{9,12},{10,... | collective-permute-start | bytes 3145736 | tf_op jit(solution)/shard_map/sum_up_second/ppermute | solution.py:274
  365.9 38.6 %collective-permute-start.74 = (bf16[128,2048]{1,0:T(8,128)(2,1)S(1)}, bf16[128,2048]{1,0:T(8,128)(2,1)S(1)}, u32[]{:S(2)}, u32[]{:S(2)}) collective-permute-start(bf16[128,2048]{1,0:T(8,128)(2,1)S(1)} %get-tuple-element.141), channel_id=1, source_target_pairs={{0,1},{1,0},{2,3},{3,2},{4,5},{5,4},{6,7},{7,6},{8,9},{9,8},{10,11... | collective-permute-start | bytes 1572872 | tf_op jit(solution)/shard_map/scatter_g_attn_in_0/ppermute | solution.py:274
  382.1 71.8 %collective-permute-start.73 = (bf16[128,2048]{1,0:T(8,128)(2,1)}, bf16[128,2048]{1,0:T(8,128)(2,1)}, u32[]{:S(2)}, u32[]{:S(2)}) collective-permute-start(bf16[128,2048]{1,0:T(8,128)(2,1)} %get-tuple-element.146), channel_id=1, source_target_pairs={{0,1},{1,0},{2,3},{3,2},{4,5},{5,4},{6,7},{7,6},{8,9},{9,8},{10,11... | collective-permute-start | bytes 1572872 | tf_op jit(solution)/shard_map/scatter_g_attn_in_1/ppermute | solution.py:274
  403.2 69.4 %collective-permute-start.77 = (bf16[2,512,2048]{2,1,0:T(8,128)(2,1)}, bf16[2,512,2048]{2,1,0:T(8,128)(2,1)}, u32[]{:S(2)}, u32[]{:S(2)}) collective-permute-start(bf16[2,512,2048]{2,1,0:T(8,128)(2,1)} %bitcast.44), channel_id=1, source_target_pairs={{1,4},{3,6},{5,0},{7,2},{9,12},{11,14},{13,8},{15,10},{17,20},{19,... | collective-permute-start | bytes 12582920 | tf_op jit(solution)/shard_map/sum_down_first/ppermute | solution.py:274
  406.4 38.9 %collective-permute-start.62 = (bf16[128,2048]{1,0:T(8,128)(2,1)S(1)}, bf16[128,2048]{1,0:T(8,128)(2,1)S(1)}, u32[]{:S(2)}, u32[]{:S(2)}) collective-permute-start(bf16[128,2048]{1,0:T(8,128)(2,1)S(1)} %pad_maximum_fusion.15), channel_id=1, source_target_pairs={{0,16},{1,17},{2,18},{3,19},{4,20},{5,21},{6,22},{7,23},{8,24},{9,... | collective-permute-start | bytes 1572872 | tf_op jit(solution)/shard_map/sum_glu_along_z_2/ppermute | solution.py:274
  424.9 44.1 %collective-permute-start.79 = (bf16[2,128,2048]{2,1,0:T(8,128)(2,1)}, bf16[2,128,2048]{2,1,0:T(8,128)(2,1)}, u32[]{:S(2)}, u32[]{:S(2)}) collective-permute-start(bf16[2,128,2048]{2,1,0:T(8,128)(2,1)} %bitcast.50), channel_id=1, source_target_pairs={{1,4},{3,6},{5,0},{7,2},{9,12},{11,14},{13,8},{15,10},{17,20},{19,... | collective-permute-start | bytes 3145736 | tf_op jit(solution)/shard_map/sum_out_first/ppermute | solution.py:274
  451.8 45.0 %collective-permute-start.80 = (bf16[4,128,2048]{2,1,0:T(8,128)(2,1)S(1)}, bf16[4,128,2048]{2,1,0:T(8,128)(2,1)}, u32[]{:S(2)}, u32[]{:S(2)}) collective-permute-start(bf16[4,128,2048]{2,1,0:T(8,128)(2,1)S(1)} %pad_maximum_fusion.6.refs_0_), channel_id=1, source_target_pairs={{0,2},{1,3},{2,0},{3,1},{4,6},{5,7},{6,4},{7,5},{8,10},{9,11},{10,... | collective-permute-start | bytes 6291464 | tf_op jit(solution)/shard_map/sum_glu_across/ppermute | solution.py:274
  475.7 50.8 %collective-permute-start.83 = (bf16[512,2048]{1,0:T(8,128)(2,1)S(1)}, bf16[512,2048]{1,0:T(8,128)(2,1)S(1)}, u32[]{:S(2)}, u32[]{:S(2)}) collective-permute-start(bf16[512,2048]{1,0:T(8,128)(2,1)S(1)} %fusion.12), channel_id=1, source_target_pairs={{0,2},{2,0},{4,6},{6,4},{8,10},{10,8},{12,14},{14,12},{16,18},{18,... | collective-permute-start | bytes 6291464 | tf_op jit(solution)/shard_map/sum_down_second/ppermute | solution.py:274
  496.9 54.5 %collective-permute-start.85 = (bf16[4,128,384]{2,1,0:T(8,128)(2,1)S(1)}, bf16[4,128,384]{2,1,0:T(8,128)(2,1)S(1)}, u32[]{:S(2)}, u32[]{:S(2)}) collective-permute-start(bf16[4,128,384]{2,1,0:T(8,128)(2,1)S(1)} %fusion.98), channel_id=1, source_target_pairs={{0,2},{1,3},{2,0},{3,1},{4,6},{5,7},{6,4},{7,5},{8,10},{9,11},{10,... | collective-permute-start | bytes 1179656 | tf_op jit(solution)/shard_map/sum_qkv_second/ppermute | solution.py:274
  498.3 67.4 %collective-permute-start.86 = (bf16[128,2048]{1,0:T(8,128)(2,1)S(1)}, bf16[128,2048]{1,0:T(8,128)(2,1)S(1)}, u32[]{:S(2)}, u32[]{:S(2)}) collective-permute-start(bf16[128,2048]{1,0:T(8,128)(2,1)S(1)} %fusion.99), channel_id=1, source_target_pairs={{0,2},{2,0},{4,6},{6,4},{8,10},{10,8},{12,14},{14,12},{16,18},{18,... | collective-permute-start | bytes 1572872 | tf_op jit(solution)/shard_map/sum_out_second/ppermute | solution.py:274
  502.4 32.5 %collective-permute-start.67 = (bf16[128,2048]{1,0:T(8,128)(2,1)S(1)}, bf16[128,2048]{1,0:T(8,128)(2,1)S(1)}, u32[]{:S(2)}, u32[]{:S(2)}) collective-permute-start(bf16[128,2048]{1,0:T(8,128)(2,1)S(1)} %slice.233), channel_id=1, source_target_pairs={{0,1},{1,0},{2,3},{3,2},{4,5},{5,4},{6,7},{7,6},{8,9},{9,8},{10,11... | collective-permute-start | bytes 1572872 | tf_op jit(solution)/shard_map/scatter_ffn_branch_0/ppermute | solution.py:274
  540.0 43.5 %collective-permute-start.88 = (bf16[4,128,2048]{2,1,0:T(8,128)(2,1)S(1)}, bf16[4,128,2048]{2,1,0:T(8,128)(2,1)S(1)}, u32[]{:S(2)}, u32[]{:S(2)}) collective-permute-start(bf16[4,128,2048]{2,1,0:T(8,128)(2,1)S(1)} %pad_maximum_fusion.6.refs_0_), channel_id=1, source_target_pairs={{0,1},{1,0},{2,3},{3,2},{4,5},{5,4},{6,7},{7,6},{8,9},{9,8},{10,11... | collective-permute-start | bytes 6291464 | tf_op jit(solution)/shard_map/sum_glu_core/ppermute | solution.py:274
  551.5 34.4 %collective-permute-start.89 = (bf16[4,128,2048]{2,1,0:T(8,128)(2,1)}, bf16[4,128,2048]{2,1,0:T(8,128)(2,1)S(1)}, u32[]{:S(2)}, u32[]{:S(2)}) collective-permute-start(bf16[4,128,2048]{2,1,0:T(8,128)(2,1)} %collective-permute-done.80.refs_1_), channel_id=1, source_target_pairs={{0,1},{1,0},{2,3},{3,2},{4,5},{5,4},{6,7},{7,6},{8,9},{9,8},{10,11... | collective-permute-start | bytes 6291464 | tf_op jit(solution)/shard_map/sum_glu_core/ppermute | solution.py:274
  562.1 71.6 %collective-permute-start.99 = (bf16[2,512,2048]{2,1,0:T(8,128)(2,1)}, bf16[2,512,2048]{2,1,0:T(8,128)(2,1)}, u32[]{:S(2)}, u32[]{:S(2)}) collective-permute-start(bf16[2,512,2048]{2,1,0:T(8,128)(2,1)} %pad_maximum_fusion.2), channel_id=1, source_target_pairs={{0,1},{2,3},{4,5},{6,7},{8,9},{10,11},{12,13},{14,15},{16,17},{18,... | collective-permute-start | bytes 12582920 | tf_op jit(solution)/shard_map/sum_down_last/ppermute | solution.py:274
  583.6 33.8 %collective-permute-start.97 = (bf16[2,128,2048]{2,1,0:T(8,128)(2,1)}, bf16[2,128,2048]{2,1,0:T(8,128)(2,1)}, u32[]{:S(2)}, u32[]{:S(2)}) collective-permute-start(bf16[2,128,2048]{2,1,0:T(8,128)(2,1)} %pad_maximum_fusion.9), channel_id=1, source_target_pairs={{0,1},{2,3},{4,5},{6,7},{8,9},{10,11},{12,13},{14,15},{16,17},{18,... | collective-permute-start | bytes 3145736 | tf_op jit(solution)/shard_map/sum_out_last/ppermute | solution.py:274
  (198 other events, 2997.5 us)

commit v6 on v5

--- a/solution.py
+++ b/solution.py
@@ -335,11 +335,12 @@
     return total
 
 
-def total_sum(values):
-    for bit in range(2):
-        values = values + move(values, lambda f, r: (f, r ^ (1 << bit)))
-    for bit in range((lax.axis_size("fsdp") - 1).bit_length()):
-        values = values + move(values, lambda f, r: (f ^ (1 << bit), r))
+def total_sum(values, beside):
+    steps = [lambda f, r, bit=bit: (f, r ^ (1 << bit)) for bit in range(2)]
+    ranks = lax.axis_size("fsdp")
+    steps += [lambda f, r, bit=bit: (f ^ (1 << bit), r) for bit in range((ranks - 1).bit_length())]
+    for index, step in enumerate(steps):
+        values = values + after(move(values, step), *beside.get(index, ()))
     return values
 
 
@@ -730,14 +731,14 @@
         return sent
 
     ffn_branch = scatter_group(down_partial, "ffn_branch", beside_branch)
-    block = middle + after(ffn_branch, *glu_placed)
     grad_gate, grad_up = glu_placed
     qkv_slots = along_z([qkv_sum.payload], "qkv")
-    qkv_same = jnp.stack(after((*qkv_slots,), arrived[2]))
+    qkv_same = jnp.stack(after((*qkv_slots,), arrived[-1]))
+    block = middle + after(ffn_branch, *glu_placed, qkv_same)
     qkv_across = across_x(qkv_same, "qkv")
     grad_query, grad_kv = columns_placed(qkv_same, qkv_across, [q_cols, 2 * kv_cols], "qkv")
-    down_sum.third()
-    out_sum.third()
+    down_sum.third(arrived[2])
+    out_sum.third(arrived[-1])
     grad_down, grad_out = down_sum.last(), out_sum.last()
     grad_kv = grad_kv.reshape(grad_kv.shape[0], -1, share, 2 * kv_cols).sum(axis=2)
     grad_key = grad_kv[:, :, :kv_cols].reshape(grad_kv.shape[0], -1)
@@ -747,7 +748,7 @@
     )
     small = jnp.concatenate([attn_gain_grad, ffn_gain_grad, head_gains[0], head_gains[1], squares])
     with jax.named_scope("total_sum"):
-        small = total_sum(small)
+        small = total_sum(small, {0: (grad_down,), 1: (grad_out,), 3: (grad_query,)})
     gain_rows = gain_attn.shape[0]
     attn_gain_sum = lax.dynamic_slice(small, (rank * gain_rows,), (gain_rows,))
     ffn_gain_sum = lax.dynamic_slice(small, (width + rank * gain_rows,), (gain_rows,))

time: 655 us -> 648 us (0.989)
  waiting for transfers between devices: 260 us -> 281 us
  starting transfers between devices: 131 us -> 114 us
    ppermute x105, waiting for transfers between devices: 260 us -> 281 us  [move(): return lax.ppermute(values, ('fsdp', 'rep'), pairs)]
    ppermute x105, starting transfers between devices: 131 us -> 114 us  [move(): return lax.ppermute(values, ('fsdp', 'rep'), pairs)]
    unnamed x253 -> x213, local copies, waits for them, and re-layouts: 22.7 us -> 20.8 us
  transfers between devices with their start and end apart: 105 -> 105, of which waited for: 43 -> 46; matrix products, arithmetic and copies ran while one was open for 24% -> 24% of each run, Pallas kernels for 11% -> 11%
where the time goes in v6:
time: 648 us; the launch traced here: 640 us
  waiting for transfers between devices  281 us (43%)
  starting transfers between devices  114 us (18%)
  Pallas kernels  71.2 us (11%)
  matrix products  62.6 us (10%)
  other arithmetic  56.6 us (9%)
  local copies, waits for them, and re-layouts  51.2 us (8%)
    ppermute x105, waiting for transfers between devices, move(): return lax.ppermute(values, ('fsdp', 'rep'), pairs)  281 us
    ppermute x105, starting transfers between devices, move(): return lax.ppermute(values, ('fsdp', 'rep'), pairs)  114 us
    pallas_call x8, Pallas kernels, slot_call(): pl.pallas_call(kernel, grid=(1,), in_specs=specs, out_specs=[single(shape...  42.2 us
    pallas_call x6, Pallas kernels, place_blocks(): pl.pallas_call(functools.partial(place_kernel, moves, len(sources), len(s...  29.1 us
    dot_general x8, matrix products, right_tmul(): lax.dot_general(left, right, (((1,), (1,)), ((), ())), preferred_element_...  22.8 us
    unnamed x213, local copies, waits for them, and re-layouts  20.8 us
    dot_general x5, matrix products, left_tmul(): lax.dot_general(left, right, (((0,), (0,)), ((), ())), preferred_element_...  20.5 us
    dot_general x8, matrix products, matmul(): return jnp.dot(left, right, preferred_element_type=F32)  19.3 us
  transfers between devices with their start and end apart: 105, of which 46 were waited for; matrix products, arithmetic and copies ran while one was open for 24% of the time, Pallas kernels for 11%

profile of v6, /device:TPU:0, one launch (start us, length us, event | category | flops | bytes accessed | tf_op | source)
XLA Modules:
  0.0 640.1 jit_solution(8322665602491878478)
XLA Ops:
  37.9 7.4 %collective-permute-done.7.refs_3_ = bf16[4,144,384]{2,1,0:T(8,128)(2,1)S(1)} collective-permute-done((bf16[4,144,384]{2,1,0:T(8,128)(2,1)S(1)}, bf16[4,144,384]{2,1,0:T(8,128)(2,1)S(1)}, u32[]{:S(2)}, u32[]{:S(2)}) %collective-permute-start.7) | collective-permute-done | bytes 442400 | tf_op jit(solution)/shard_map/w_qkv_across_both/ppermute | solution.py:274
  66.2 11.5 %collective-permute-start.15 = (bf16[128,2048]{1,0:T(8,128)(2,1)S(1)}, bf16[128,2048]{1,0:T(8,128)(2,1)}, u32[]{:S(2)}, u32[]{:S(2)}) collective-permute-start(bf16[128,2048]{1,0:T(8,128)(2,1)S(1)} %copy-done.3), channel_id=1, source_target_pairs={{0,8},{1,9},{2,10},{3,11},{4,12},{5,13},{6,14},{7,15},{8,16},{9,17... | collective-permute-start | bytes 1572872 | tf_op jit(solution)/shard_map/gather_tokens_1/ppermute | solution.py:274
  114.5 9.4 %collective-permute-done.18.refs_0_ = bf16[128,2048]{1,0:T(8,128)(2,1)S(1)} collective-permute-done((bf16[128,2048]{1,0:T(8,128)(2,1)S(1)}, bf16[128,2048]{1,0:T(8,128)(2,1)S(1)}, u32[]{:S(2)}, u32[]{:S(2)}) %collective-permute-start.18) | collective-permute-done | bytes 524320 | tf_op jit(solution)/shard_map/gather_tokens_3/ppermute | solution.py:274
  154.1 14.1 %collective-permute-done.31.refs_4_ = bf16[2,128,2048]{2,1,0:T(8,128)(2,1)} collective-permute-done((bf16[2,128,2048]{2,1,0:T(8,128)(2,1)}, bf16[2,128,2048]{2,1,0:T(8,128)(2,1)}, u32[]{:S(2)}, u32[]{:S(2)}) %collective-permute-start.31) | collective-permute-done | bytes 1048608 | tf_op jit(solution)/shard_map/w_glu_across_both/ppermute | solution.py:274
  171.8 7.2 %place_blocks.7 = bf16[2048,2048]{1,0:T(8,128)(2,1)} custom-call(s32[16]{0:T(128)S(1)} %copy-done.21, s32[16]{0:T(128)S(1)} %copy-done.23, bf16[4,128,2048]{2,1,0:T(8,128)(2,1)} %pad_maximum_fusion.3.refs_0_, bf16[4,128,2048]{2,1,0:T(8,128)(2,1)} %collective-permute-done.19.refs_1_, bf16[4,128,2048]{2,1,0:T(8,128)(2,1)} %collective-permute-done.20.refs_2_, ...), custom_call_target="tpu_custom_call" | custom-call | flops 1 | bytes 1 | tf_op jit(solution)/shard_map/place_blocks/pallas_call | solution.py:250
  186.4 13.2 %collective-permute-done.33 = bf16[128,2048]{1,0:T(8,128)(2,1)S(1)} collective-permute-done((bf16[128,2048]{1,0:T(8,128)(2,1)S(1)}, bf16[128,2048]{1,0:T(8,128)(2,1)S(1)}, u32[]{:S(2)}, u32[]{:S(2)}) %collective-permute-start.33) | collective-permute-done | bytes 524320 | tf_op jit(solution)/shard_map/gather_ffn_in_1/ppermute | solution.py:274
  218.9 10.3 %collective-permute-done.37 = bf16[128,2048]{1,0:T(8,128)(2,1)S(1)} collective-permute-done((bf16[128,2048]{1,0:T(8,128)(2,1)S(1)}, bf16[128,2048]{1,0:T(8,128)(2,1)S(1)}, u32[]{:S(2)}, u32[]{:S(2)}) %collective-permute-start.37) | collective-permute-done | bytes 524320 | tf_op jit(solution)/shard_map/gather_ffn_in_3/ppermute | solution.py:274
  234.5 8.1 %collective-permute-done.40 = bf16[128,2048]{1,0:T(8,128)(2,1)S(1)} collective-permute-done((bf16[128,2048]{1,0:T(8,128)(2,1)S(1)}, bf16[128,2048]{1,0:T(8,128)(2,1)S(1)}, u32[]{:S(2)}, u32[]{:S(2)}) %collective-permute-start.40) | collective-permute-done | bytes 524320 | tf_op jit(solution)/shard_map/gather_d_out_1/ppermute | solution.py:274
  247.2 7.9 %collective-permute-done.42 = bf16[128,2048]{1,0:T(8,128)(2,1)S(1)} collective-permute-done((bf16[128,2048]{1,0:T(8,128)(2,1)S(1)}, bf16[128,2048]{1,0:T(8,128)(2,1)S(1)}, u32[]{:S(2)}, u32[]{:S(2)}) %collective-permute-start.42) | collective-permute-done | bytes 524320 | tf_op jit(solution)/shard_map/gather_d_out_2/ppermute | solution.py:274
  283.7 6.7 %collective-permute-done.48 = bf16[128,2048]{1,0:T(8,128)(2,1)S(1)} collective-permute-done((bf16[128,2048]{1,0:T(8,128)(2,1)S(1)}, bf16[128,2048]{1,0:T(8,128)(2,1)S(1)}, u32[]{:S(2)}, u32[]{:S(2)}) %collective-permute-start.48) | collective-permute-done | bytes 524320 | tf_op jit(solution)/shard_map/scatter_g_ffn_in_1/ppermute | solution.py:274
  310.8 11.5 %collective-permute-done.53 = bf16[128,2048]{1,0:T(8,128)(2,1)} collective-permute-done((bf16[128,2048]{1,0:T(8,128)(2,1)}, bf16[128,2048]{1,0:T(8,128)(2,1)}, u32[]{:S(2)}, u32[]{:S(2)}) %collective-permute-start.53) | collective-permute-done | bytes 524320 | tf_op jit(solution)/shard_map/scatter_g_ffn_in_3/ppermute | solution.py:274
  327.2 13.8 %collective-permute-done.54.refs_0_ = bf16[128,2048]{1,0:T(8,128)(2,1)S(1)} collective-permute-done((bf16[128,2048]{1,0:T(8,128)(2,1)S(1)}, bf16[128,2048]{1,0:T(8,128)(2,1)S(1)}, u32[]{:S(2)}, u32[]{:S(2)}) %collective-permute-start.54) | collective-permute-done | bytes 524320 | tf_op jit(solution)/shard_map/gather_g_attn_1/ppermute | solution.py:274
  349.9 6.6 %collective-permute-done.58 = bf16[4,2,128,1024]{3,2,0,1:T(8,128)(2,1)S(1)} collective-permute-done((bf16[4,2,128,1024]{3,2,0,1:T(8,128)(2,1)}, bf16[4,2,128,1024]{3,2,0,1:T(8,128)(2,1)S(1)}, u32[]{:S(2)}, u32[]{:S(2)}) %collective-permute-start.58) | collective-permute-done | bytes 2097184 | tf_op jit(solution)/shard_map/sum_up_first/ppermute | solution.py:274
  374.1 7.3 %collective-permute-done.60 = bf16[4,128,1024]{2,1,0:T(8,128)(2,1)S(1)} collective-permute-done((bf16[4,128,1024]{2,1,0:T(8,128)(2,1)S(1)}, bf16[4,128,1024]{2,1,0:T(8,128)(2,1)S(1)}, u32[]{:S(2)}, u32[]{:S(2)}) %collective-permute-start.60) | collective-permute-done | bytes 1048608 | tf_op jit(solution)/shard_map/sum_up_second/ppermute | solution.py:274
  385.1 7.0 %convolution_convert_fusion = bf16[1024,2048]{1,0:T(8,128)(2,1)S(1)} fusion(bf16[1024,1024]{1,0:T(8,128)(2,1)S(1)} %pad_maximum_fusion.7, bf16[1024,2048]{1,0:T(8,128)(2,1)} %constant_dynamic-update-slice_fusion.8), kind=kOutput, calls=%fused_computation.15 | convolution fusion | flops 4297064448 | bytes 10485760 | tf_op jit(solution)/shard_map/dot_general | solution.py:27
  413.9 19.6 %collective-permute-done.62 = bf16[128,2048]{1,0:T(8,128)(2,1)S(1)} collective-permute-done((bf16[128,2048]{1,0:T(8,128)(2,1)S(1)}, bf16[128,2048]{1,0:T(8,128)(2,1)S(1)}, u32[]{:S(2)}, u32[]{:S(2)}) %collective-permute-start.62) | collective-permute-done | bytes 524320 | tf_op jit(solution)/shard_map/sum_glu_along_z_2/ppermute | solution.py:274
  433.5 10.3 %collective-permute-start.75 = (bf16[128,2048]{1,0:T(8,128)(2,1)S(1)}, bf16[128,2048]{1,0:T(8,128)(2,1)S(1)}, u32[]{:S(2)}, u32[]{:S(2)}) collective-permute-start(bf16[128,2048]{1,0:T(8,128)(2,1)S(1)} %add_convert_fusion.6), channel_id=1, source_target_pairs={{0,8},{1,9},{2,10},{3,11},{4,12},{5,13},{6,14},{7,15},{8,16},{9,17... | collective-permute-start | bytes 1572872 | tf_op jit(solution)/shard_map/scatter_g_attn_in_1/ppermute | solution.py:274
  446.6 11.8 %collective-permute-done.75 = bf16[128,2048]{1,0:T(8,128)(2,1)S(1)} collective-permute-done((bf16[128,2048]{1,0:T(8,128)(2,1)S(1)}, bf16[128,2048]{1,0:T(8,128)(2,1)S(1)}, u32[]{:S(2)}, u32[]{:S(2)}) %collective-permute-start.75) | collective-permute-done | bytes 524320 | tf_op jit(solution)/shard_map/scatter_g_attn_in_1/ppermute | solution.py:274
  459.5 10.8 %collective-permute-done.78 = bf16[4,2,128,384]{3,2,0,1:T(8,128)(2,1)S(1)} collective-permute-done((bf16[4,2,128,384]{3,2,0,1:T(8,128)(2,1)S(1)}, bf16[4,2,128,384]{3,2,0,1:T(8,128)(2,1)S(1)}, u32[]{:S(2)}, u32[]{:S(2)}) %collective-permute-start.78) | collective-permute-done | bytes 786464 | tf_op jit(solution)/shard_map/sum_qkv_first/ppermute | solution.py:274
  496.3 11.9 %collective-permute-done.81 = bf16[128,2048]{1,0:T(8,128)(2,1)S(1)} collective-permute-done((bf16[128,2048]{1,0:T(8,128)(2,1)S(1)}, bf16[128,2048]{1,0:T(8,128)(2,1)S(1)}, u32[]{:S(2)}, u32[]{:S(2)}) %collective-permute-start.81) | collective-permute-done | bytes 524320 | tf_op jit(solution)/shard_map/scatter_g_attn_in_3/ppermute | solution.py:274
  520.5 11.0 %collective-permute-done.82 = bf16[128,2048]{1,0:T(8,128)(2,1)S(1)} collective-permute-done((bf16[128,2048]{1,0:T(8,128)(2,1)S(1)}, bf16[128,2048]{1,0:T(8,128)(2,1)S(1)}, u32[]{:S(2)}, u32[]{:S(2)}) %collective-permute-start.82) | collective-permute-done | bytes 524320 | tf_op jit(solution)/shard_map/scatter_ffn_branch_1/ppermute | solution.py:274
  534.1 8.8 %collective-permute-done.84 = bf16[128,2048]{1,0:T(8,128)(2,1)S(1)} collective-permute-done((bf16[128,2048]{1,0:T(8,128)(2,1)S(1)}, bf16[128,2048]{1,0:T(8,128)(2,1)S(1)}, u32[]{:S(2)}, u32[]{:S(2)}) %collective-permute-start.84) | collective-permute-done | bytes 524320 | tf_op jit(solution)/shard_map/scatter_ffn_branch_2/ppermute | solution.py:274
  573.2 7.4 %collective-permute-done.96 = bf16[128,2048]{1,0:T(8,128)(2,1)} collective-permute-done((bf16[128,2048]{1,0:T(8,128)(2,1)S(1)}, bf16[128,2048]{1,0:T(8,128)(2,1)}, u32[]{:S(2)}, u32[]{:S(2)}) %collective-permute-start.96) | collective-permute-done | bytes 524320 | tf_op jit(solution)/shard_map/sum_out_third/ppermute | solution.py:274
  598.5 8.6 %place_blocks.8 = (f32[256,8192]{1,0:T(8,128)}, f32[256,8192]{1,0:T(8,128)}) custom-call(s32[32]{0:T(128)S(1)} %reshape.232.row_ref, s32[32]{0:T(128)S(1)} %reshape.233.column_ref, bf16[4,128,2048]{2,1,0:T(8,128)(2,1)S(1)} %pad_maximum_fusion.6.refs_0_, bf16[4,128,2048]{2,1,0:T(8,128)(2,1)} %collective-permute-done.80.refs_1_, ...), custom_call_target="tpu_custom_call" | custom-call | flops 1 | bytes 1 | tf_op jit(solution)/shard_map/place_blocks/pallas_call | solution.py:250
  (581 shorter events, 394.7 us)
Async XLA Ops:
  14.2 45.5 %collective-permute-start.8 = (bf16[128,2048]{1,0:T(8,128)(2,1)}, bf16[128,2048]{1,0:T(8,128)(2,1)}, u32[]{:S(2)}, u32[]{:S(2)}) collective-permute-start(bf16[128,2048]{1,0:T(8,128)(2,1)} %constant_dynamic-slice_fusion.4), channel_id=1, source_target_pairs={{1,5},{3,7},{5,1},{7,3},{9,13},{11,15},{13,9},{15,11},{17,21},{19,... | collective-permute-start | bytes 1572872 | tf_op jit(solution)/shard_map/w_out_across_y/ppermute | solution.py:274
  24.3 38.9 %collective-permute-start.11 = (bf16[128,2048]{1,0:T(8,128)(2,1)}, bf16[128,2048]{1,0:T(8,128)(2,1)}, u32[]{:S(2)}, u32[]{:S(2)}) collective-permute-start(bf16[128,2048]{1,0:T(8,128)(2,1)} %pad_maximum_fusion.11), channel_id=1, source_target_pairs={{0,8},{1,9},{2,10},{3,11},{4,12},{5,13},{6,14},{7,15},{8,16},{9,17... | collective-permute-start | bytes 1572872 | tf_op jit(solution)/shard_map/w_glu_along_z/ppermute | solution.py:274
  30.4 32.8 %collective-permute-start.12 = (bf16[128,2048]{1,0:T(8,128)(2,1)}, bf16[128,2048]{1,0:T(8,128)(2,1)}, u32[]{:S(2)}, u32[]{:S(2)}) collective-permute-start(bf16[128,2048]{1,0:T(8,128)(2,1)} %pad_maximum_fusion.12), channel_id=1, source_target_pairs={{0,16},{1,17},{2,18},{3,19},{4,20},{5,21},{6,22},{7,23},{8,24},{9,... | collective-permute-start | bytes 1572872 | tf_op jit(solution)/shard_map/w_glu_along_z/ppermute | solution.py:274
  35.3 27.9 %collective-permute-start.13 = (bf16[128,2048]{1,0:T(8,128)(2,1)}, bf16[128,2048]{1,0:T(8,128)(2,1)}, u32[]{:S(2)}, u32[]{:S(2)}) collective-permute-start(bf16[128,2048]{1,0:T(8,128)(2,1)} %pad_maximum_fusion.13), channel_id=1, source_target_pairs={{0,24},{1,25},{2,26},{3,27},{4,28},{5,29},{6,30},{7,31},{8,0},{9,1... | collective-permute-start | bytes 1572872 | tf_op jit(solution)/shard_map/w_glu_along_z/ppermute | solution.py:274
  77.8 49.9 %collective-permute-start.20 = (bf16[4,128,2048]{2,1,0:T(8,128)(2,1)}, bf16[4,128,2048]{2,1,0:T(8,128)(2,1)}, u32[]{:S(2)}, u32[]{:S(2)}) collective-permute-start(bf16[4,128,2048]{2,1,0:T(8,128)(2,1)} %pad_maximum_fusion.3.refs_0_), channel_id=1, source_target_pairs={{0,5},{1,4},{2,7},{3,6},{4,1},{5,0},{6,3},{7,2},{8,13},{9,12},{10,... | collective-permute-start | bytes 6291464 | tf_op jit(solution)/shard_map/w_glu_across/ppermute | solution.py:274
  81.7 46.6 %collective-permute-start.19 = (bf16[4,128,2048]{2,1,0:T(8,128)(2,1)}, bf16[4,128,2048]{2,1,0:T(8,128)(2,1)}, u32[]{:S(2)}, u32[]{:S(2)}) collective-permute-start(bf16[4,128,2048]{2,1,0:T(8,128)(2,1)} %pad_maximum_fusion.3.refs_0_), channel_id=1, source_target_pairs={{0,2},{1,3},{2,0},{3,1},{4,6},{5,7},{6,4},{7,5},{8,10},{9,11},{10,... | collective-permute-start | bytes 6291464 | tf_op jit(solution)/shard_map/w_glu_across/ppermute | solution.py:274
  150.4 28.5 %collective-permute-start.10 = (bf16[128,2048]{1,0:T(8,128)(2,1)}, bf16[128,2048]{1,0:T(8,128)(2,1)}, u32[]{:S(2)}, u32[]{:S(2)}) collective-permute-start(bf16[128,2048]{1,0:T(8,128)(2,1)} %get-tuple-element.118), channel_id=1, source_target_pairs={{0,1},{1,0},{2,3},{3,2},{4,5},{5,4},{6,7},{7,6},{8,9},{9,8},{10,11... | collective-permute-start | bytes 1572872 | tf_op jit(solution)/shard_map/scatter_attn_branch_3/ppermute | solution.py:274
  151.0 32.8 %collective-permute-start.16 = (bf16[512,2048]{1,0:T(8,128)(2,1)}, bf16[512,2048]{1,0:T(8,128)(2,1)}, u32[]{:S(2)}, u32[]{:S(2)}) collective-permute-start(bf16[512,2048]{1,0:T(8,128)(2,1)} %collective-permute-done.14), channel_id=1, source_target_pairs={{1,3},{3,1},{5,7},{7,5},{9,11},{11,9},{13,15},{15,13},{17,19},{19,... | collective-permute-start | bytes 6291464 | tf_op jit(solution)/shard_map/w_down_across_x/ppermute | solution.py:274
  168.2 33.9 %collective-permute-start.39 = (bf16[128,2048]{1,0:T(8,128)(2,1)}, bf16[128,2048]{1,0:T(8,128)(2,1)S(1)}, u32[]{:S(2)}, u32[]{:S(2)}) collective-permute-start(bf16[128,2048]{1,0:T(8,128)(2,1)} %param.27), channel_id=1, source_target_pairs={{0,1},{1,0},{2,3},{3,2},{4,5},{5,4},{6,7},{7,6},{8,9},{9,8},{10,11... | collective-permute-start | bytes 1572872 | tf_op jit(solution)/shard_map/gather_d_out_0/ppermute | solution.py:274
  207.9 102.9 %collective-permute-start.50 = (bf16[128,2048]{1,0:T(8,128)(2,1)}, bf16[128,2048]{1,0:T(8,128)(2,1)}, u32[]{:S(2)}, u32[]{:S(2)}) collective-permute-start(bf16[128,2048]{1,0:T(8,128)(2,1)} %slice.223), channel_id=1, source_target_pairs={{0,1},{1,0},{2,3},{3,2},{4,5},{5,4},{6,7},{7,6},{8,9},{9,8},{10,11... | collective-permute-start | bytes 1572872 | tf_op jit(solution)/shard_map/scatter_g_ffn_in_3/ppermute | solution.py:274
  309.4 47.2 %collective-permute-start.58 = (bf16[4,2,128,1024]{3,2,0,1:T(8,128)(2,1)}, bf16[4,2,128,1024]{3,2,0,1:T(8,128)(2,1)S(1)}, u32[]{:S(2)}, u32[]{:S(2)}) collective-permute-start(bf16[4,2,128,1024]{3,2,0,1:T(8,128)(2,1)} %copy_bitcast_fusion), channel_id=1, source_target_pairs={{0,2},{1,3},{2,0},{3,1},{4,6},{5,7},{6,4},{7,5},{8,10},{9,11},{10,... | collective-permute-start | bytes 6291464 | tf_op jit(solution)/shard_map/sum_up_first/ppermute | solution.py:274
  310.8 47.4 %collective-permute-start.49 = (bf16[4,2,128,1024]{3,2,0,1:T(8,128)(2,1)}, bf16[4,2,128,1024]{3,2,0,1:T(8,128)(2,1)S(1)}, u32[]{:S(2)}, u32[]{:S(2)}) collective-permute-start(bf16[4,2,128,1024]{3,2,0,1:T(8,128)(2,1)} %copy_bitcast_fusion.1), channel_id=1, source_target_pairs={{0,5},{1,4},{2,7},{3,6},{4,1},{5,0},{6,3},{7,2},{8,13},{9,12},{10,... | collective-permute-start | bytes 6291464 | tf_op jit(solution)/shard_map/sum_gate_first/ppermute | solution.py:274
  373.4 71.4 %collective-permute-start.73 = (bf16[128,2048]{1,0:T(8,128)(2,1)S(1)}, bf16[128,2048]{1,0:T(8,128)(2,1)S(1)}, u32[]{:S(2)}, u32[]{:S(2)}) collective-permute-start(bf16[128,2048]{1,0:T(8,128)(2,1)S(1)} %get-tuple-element.151), channel_id=1, source_target_pairs={{0,1},{1,0},{2,3},{3,2},{4,5},{5,4},{6,7},{7,6},{8,9},{9,8},{10,11... | collective-permute-start | bytes 1572872 | tf_op jit(solution)/shard_map/scatter_g_attn_in_1/ppermute | solution.py:274
  392.1 82.6 %collective-permute-start.77 = (bf16[2,512,2048]{2,1,0:T(8,128)(2,1)S(1)}, bf16[2,512,2048]{2,1,0:T(8,128)(2,1)S(1)}, u32[]{:S(2)}, u32[]{:S(2)}) collective-permute-start(bf16[2,512,2048]{2,1,0:T(8,128)(2,1)S(1)} %bitcast.197), channel_id=1, source_target_pairs={{1,4},{3,6},{5,0},{7,2},{9,12},{11,14},{13,8},{15,10},{17,20},{19,... | collective-permute-start | bytes 12582920 | tf_op jit(solution)/shard_map/sum_down_first/ppermute | solution.py:274
  398.0 35.5 %collective-permute-start.62 = (bf16[128,2048]{1,0:T(8,128)(2,1)S(1)}, bf16[128,2048]{1,0:T(8,128)(2,1)S(1)}, u32[]{:S(2)}, u32[]{:S(2)}) collective-permute-start(bf16[128,2048]{1,0:T(8,128)(2,1)S(1)} %pad_maximum_fusion.15), channel_id=1, source_target_pairs={{0,16},{1,17},{2,18},{3,19},{4,20},{5,21},{6,22},{7,23},{8,24},{9,... | collective-permute-start | bytes 1572872 | tf_op jit(solution)/shard_map/sum_glu_along_z_2/ppermute | solution.py:274
  409.6 34.2 %collective-permute-start.63 = (bf16[128,2048]{1,0:T(8,128)(2,1)S(1)}, bf16[128,2048]{1,0:T(8,128)(2,1)S(1)}, u32[]{:S(2)}, u32[]{:S(2)}) collective-permute-start(bf16[128,2048]{1,0:T(8,128)(2,1)S(1)} %pad_maximum_fusion.16), channel_id=1, source_target_pairs={{0,24},{1,25},{2,26},{3,27},{4,28},{5,29},{6,30},{7,31},{8,0},{9,1... | collective-permute-start | bytes 1572872 | tf_op jit(solution)/shard_map/sum_glu_along_z_3/ppermute | solution.py:274
  412.6 57.7 %collective-permute-start.79 = (bf16[2,128,2048]{2,1,0:T(8,128)(2,1)S(1)}, bf16[2,128,2048]{2,1,0:T(8,128)(2,1)S(1)}, u32[]{:S(2)}, u32[]{:S(2)}) collective-permute-start(bf16[2,128,2048]{2,1,0:T(8,128)(2,1)S(1)} %bitcast.207), channel_id=1, source_target_pairs={{1,4},{3,6},{5,0},{7,2},{9,12},{11,14},{13,8},{15,10},{17,20},{19,... | collective-permute-start | bytes 3145736 | tf_op jit(solution)/shard_map/sum_out_first/ppermute | solution.py:274
  444.1 48.0 %collective-permute-start.80 = (bf16[4,128,2048]{2,1,0:T(8,128)(2,1)S(1)}, bf16[4,128,2048]{2,1,0:T(8,128)(2,1)}, u32[]{:S(2)}, u32[]{:S(2)}) collective-permute-start(bf16[4,128,2048]{2,1,0:T(8,128)(2,1)S(1)} %pad_maximum_fusion.6.refs_0_), channel_id=1, source_target_pairs={{0,2},{1,3},{2,0},{3,1},{4,6},{5,7},{6,4},{7,5},{8,10},{9,11},{10,... | collective-permute-start | bytes 6291464 | tf_op jit(solution)/shard_map/sum_glu_across/ppermute | solution.py:274
  458.4 38.0 %collective-permute-start.69 = (bf16[128,2048]{1,0:T(8,128)(2,1)S(1)}, bf16[128,2048]{1,0:T(8,128)(2,1)S(1)}, u32[]{:S(2)}, u32[]{:S(2)}) collective-permute-start(bf16[128,2048]{1,0:T(8,128)(2,1)S(1)} %get-tuple-element.161), channel_id=1, source_target_pairs={{0,1},{1,0},{2,3},{3,2},{4,5},{5,4},{6,7},{7,6},{8,9},{9,8},{10,11... | collective-permute-start | bytes 1572872 | tf_op jit(solution)/shard_map/scatter_g_attn_in_3/ppermute | solution.py:274
  475.5 39.6 %collective-permute-start.83 = (bf16[512,2048]{1,0:T(8,128)(2,1)S(1)}, bf16[512,2048]{1,0:T(8,128)(2,1)S(1)}, u32[]{:S(2)}, u32[]{:S(2)}) collective-permute-start(bf16[512,2048]{1,0:T(8,128)(2,1)S(1)} %fusion.12), channel_id=1, source_target_pairs={{0,2},{2,0},{4,6},{6,4},{8,10},{10,8},{12,14},{14,12},{16,18},{18,... | collective-permute-start | bytes 6291464 | tf_op jit(solution)/shard_map/sum_down_second/ppermute | solution.py:274
  516.4 28.7 %collective-permute-start.98 = (bf16[512,2048]{1,0:T(8,128)(2,1)S(1)}, bf16[512,2048]{1,0:T(8,128)(2,1)S(1)}, u32[]{:S(2)}, u32[]{:S(2)}) collective-permute-start(bf16[512,2048]{1,0:T(8,128)(2,1)S(1)} %fusion.8), channel_id=1, source_target_pairs={{0,2},{2,0},{4,6},{6,4},{8,10},{10,8},{12,14},{14,12},{16,18},{18,... | collective-permute-start | bytes 6291464 | tf_op jit(solution)/shard_map/sum_down_third/ppermute | solution.py:274
  547.8 65.5 %collective-permute-start.99 = (bf16[2,512,2048]{2,1,0:T(8,128)(2,1)}, bf16[2,512,2048]{2,1,0:T(8,128)(2,1)}, u32[]{:S(2)}, u32[]{:S(2)}) collective-permute-start(bf16[2,512,2048]{2,1,0:T(8,128)(2,1)} %pad_maximum_fusion.2), channel_id=1, source_target_pairs={{0,1},{2,3},{4,5},{6,7},{8,9},{10,11},{12,13},{14,15},{16,17},{18,... | collective-permute-start | bytes 12582920 | tf_op jit(solution)/shard_map/sum_down_last/ppermute | solution.py:274
  555.5 43.0 %collective-permute-start.88 = (bf16[4,128,2048]{2,1,0:T(8,128)(2,1)S(1)}, bf16[4,128,2048]{2,1,0:T(8,128)(2,1)}, u32[]{:S(2)}, u32[]{:S(2)}) collective-permute-start(bf16[4,128,2048]{2,1,0:T(8,128)(2,1)S(1)} %pad_maximum_fusion.6.refs_0_), channel_id=1, source_target_pairs={{0,1},{1,0},{2,3},{3,2},{4,5},{5,4},{6,7},{7,6},{8,9},{9,8},{10,11... | collective-permute-start | bytes 6291464 | tf_op jit(solution)/shard_map/sum_glu_core/ppermute | solution.py:274
  559.7 38.8 %collective-permute-start.89 = (bf16[4,128,2048]{2,1,0:T(8,128)(2,1)}, bf16[4,128,2048]{2,1,0:T(8,128)(2,1)}, u32[]{:S(2)}, u32[]{:S(2)}) collective-permute-start(bf16[4,128,2048]{2,1,0:T(8,128)(2,1)} %collective-permute-done.80.refs_1_), channel_id=1, source_target_pairs={{0,1},{1,0},{2,3},{3,2},{4,5},{5,4},{6,7},{7,6},{8,9},{9,8},{10,11... | collective-permute-start | bytes 6291464 | tf_op jit(solution)/shard_map/sum_glu_core/ppermute | solution.py:274
  (178 other events, 2530.7 us)

commit v7 on v6

--- a/solution.py
+++ b/solution.py
@@ -738,7 +738,7 @@
     qkv_across = across_x(qkv_same, "qkv")
     grad_query, grad_kv = columns_placed(qkv_same, qkv_across, [q_cols, 2 * kv_cols], "qkv")
     down_sum.third(arrived[2])
-    out_sum.third(arrived[-1])
+    out_sum.third(arrived[2])
     grad_down, grad_out = down_sum.last(), out_sum.last()
     grad_kv = grad_kv.reshape(grad_kv.shape[0], -1, share, 2 * kv_cols).sum(axis=2)
     grad_key = grad_kv[:, :, :kv_cols].reshape(grad_kv.shape[0], -1)

time: 648 us -> 640 us (0.988)
    unnamed x213 -> x223, local copies, waits for them, and re-layouts: 20.8 us -> 20.9 us
  transfers between devices with their start and end apart: 105 -> 105, of which waited for: 46 -> 45; matrix products, arithmetic and copies ran while one was open for 24% -> 23% of each run, Pallas kernels for 11% -> 11%
where the time goes in v7:
time: 640 us; the launch traced here: 633 us
  waiting for transfers between devices  276 us (43%)
  starting transfers between devices  116 us (18%)
  Pallas kernels  71.3 us (11%)
  matrix products  62.8 us (10%)
  other arithmetic  53.2 us (8%)
  local copies, waits for them, and re-layouts  50.6 us (8%)
    ppermute x105, waiting for transfers between devices, move(): return lax.ppermute(values, ('fsdp', 'rep'), pairs)  276 us
    ppermute x105, starting transfers between devices, move(): return lax.ppermute(values, ('fsdp', 'rep'), pairs)  116 us
    pallas_call x8, Pallas kernels, slot_call(): pl.pallas_call(kernel, grid=(1,), in_specs=specs, out_specs=[single(shape...  42.2 us
    pallas_call x6, Pallas kernels, place_blocks(): pl.pallas_call(functools.partial(place_kernel, moves, len(sources), len(s...  29.1 us
    dot_general x8, matrix products, right_tmul(): lax.dot_general(left, right, (((1,), (1,)), ((), ())), preferred_element_...  22.8 us
    unnamed x223, local copies, waits for them, and re-layouts  20.9 us
    dot_general x5, matrix products, left_tmul(): lax.dot_general(left, right, (((0,), (0,)), ((), ())), preferred_element_...  20.5 us
    dot_general x8, matrix products, matmul(): return jnp.dot(left, right, preferred_element_type=F32)  19.4 us
  transfers between devices with their start and end apart: 105, of which 45 were waited for; matrix products, arithmetic and copies ran while one was open for 23% of the time, Pallas kernels for 11%

profile of v7, /device:TPU:0, one launch (start us, length us, event | category | flops | bytes accessed | tf_op | source)
XLA Modules:
  0.0 632.6 jit_solution(8901358711552605488)
XLA Ops:
  37.9 7.5 %collective-permute-done.7.refs_3_ = bf16[4,144,384]{2,1,0:T(8,128)(2,1)S(1)} collective-permute-done((bf16[4,144,384]{2,1,0:T(8,128)(2,1)S(1)}, bf16[4,144,384]{2,1,0:T(8,128)(2,1)S(1)}, u32[]{:S(2)}, u32[]{:S(2)}) %collective-permute-start.7) | collective-permute-done | bytes 442400 | tf_op jit(solution)/shard_map/w_qkv_across_both/ppermute | solution.py:274
  66.2 11.5 %collective-permute-start.15 = (bf16[128,2048]{1,0:T(8,128)(2,1)S(1)}, bf16[128,2048]{1,0:T(8,128)(2,1)}, u32[]{:S(2)}, u32[]{:S(2)}) collective-permute-start(bf16[128,2048]{1,0:T(8,128)(2,1)S(1)} %copy-done.3), channel_id=1, source_target_pairs={{0,8},{1,9},{2,10},{3,11},{4,12},{5,13},{6,14},{7,15},{8,16},{9,17... | collective-permute-start | bytes 1572872 | tf_op jit(solution)/shard_map/gather_tokens_1/ppermute | solution.py:274
  82.2 6.6 %collective-permute-done.15.refs_0_ = bf16[128,2048]{1,0:T(8,128)(2,1)} collective-permute-done((bf16[128,2048]{1,0:T(8,128)(2,1)S(1)}, bf16[128,2048]{1,0:T(8,128)(2,1)}, u32[]{:S(2)}, u32[]{:S(2)}) %collective-permute-start.15) | collective-permute-done | bytes 524320 | tf_op jit(solution)/shard_map/gather_tokens_1/ppermute | solution.py:274
  114.5 9.4 %collective-permute-done.18.refs_0_ = bf16[128,2048]{1,0:T(8,128)(2,1)S(1)} collective-permute-done((bf16[128,2048]{1,0:T(8,128)(2,1)S(1)}, bf16[128,2048]{1,0:T(8,128)(2,1)S(1)}, u32[]{:S(2)}, u32[]{:S(2)}) %collective-permute-start.18) | collective-permute-done | bytes 524320 | tf_op jit(solution)/shard_map/gather_tokens_3/ppermute | solution.py:274
  154.1 14.1 %collective-permute-done.31.refs_4_ = bf16[2,128,2048]{2,1,0:T(8,128)(2,1)} collective-permute-done((bf16[2,128,2048]{2,1,0:T(8,128)(2,1)}, bf16[2,128,2048]{2,1,0:T(8,128)(2,1)}, u32[]{:S(2)}, u32[]{:S(2)}) %collective-permute-start.31) | collective-permute-done | bytes 1048608 | tf_op jit(solution)/shard_map/w_glu_across_both/ppermute | solution.py:274
  171.8 7.2 %place_blocks.7 = bf16[2048,2048]{1,0:T(8,128)(2,1)} custom-call(s32[16]{0:T(128)S(1)} %copy-done.21, s32[16]{0:T(128)S(1)} %copy-done.23, bf16[4,128,2048]{2,1,0:T(8,128)(2,1)} %pad_maximum_fusion.3.refs_0_, bf16[4,128,2048]{2,1,0:T(8,128)(2,1)} %collective-permute-done.19.refs_1_, bf16[4,128,2048]{2,1,0:T(8,128)(2,1)} %collective-permute-done.20.refs_2_, ...), custom_call_target="tpu_custom_call" | custom-call | flops 1 | bytes 1 | tf_op jit(solution)/shard_map/place_blocks/pallas_call | solution.py:250
  186.3 13.2 %collective-permute-done.33 = bf16[128,2048]{1,0:T(8,128)(2,1)S(1)} collective-permute-done((bf16[128,2048]{1,0:T(8,128)(2,1)S(1)}, bf16[128,2048]{1,0:T(8,128)(2,1)S(1)}, u32[]{:S(2)}, u32[]{:S(2)}) %collective-permute-start.33) | collective-permute-done | bytes 524320 | tf_op jit(solution)/shard_map/gather_ffn_in_1/ppermute | solution.py:274
  218.9 10.3 %collective-permute-done.37 = bf16[128,2048]{1,0:T(8,128)(2,1)S(1)} collective-permute-done((bf16[128,2048]{1,0:T(8,128)(2,1)S(1)}, bf16[128,2048]{1,0:T(8,128)(2,1)S(1)}, u32[]{:S(2)}, u32[]{:S(2)}) %collective-permute-start.37) | collective-permute-done | bytes 524320 | tf_op jit(solution)/shard_map/gather_ffn_in_3/ppermute | solution.py:274
  234.5 8.1 %collective-permute-done.40 = bf16[128,2048]{1,0:T(8,128)(2,1)S(1)} collective-permute-done((bf16[128,2048]{1,0:T(8,128)(2,1)S(1)}, bf16[128,2048]{1,0:T(8,128)(2,1)S(1)}, u32[]{:S(2)}, u32[]{:S(2)}) %collective-permute-start.40) | collective-permute-done | bytes 524320 | tf_op jit(solution)/shard_map/gather_d_out_1/ppermute | solution.py:274
  247.1 7.9 %collective-permute-done.42 = bf16[128,2048]{1,0:T(8,128)(2,1)S(1)} collective-permute-done((bf16[128,2048]{1,0:T(8,128)(2,1)S(1)}, bf16[128,2048]{1,0:T(8,128)(2,1)S(1)}, u32[]{:S(2)}, u32[]{:S(2)}) %collective-permute-start.42) | collective-permute-done | bytes 524320 | tf_op jit(solution)/shard_map/gather_d_out_2/ppermute | solution.py:274
  283.7 6.7 %collective-permute-done.48 = bf16[128,2048]{1,0:T(8,128)(2,1)S(1)} collective-permute-done((bf16[128,2048]{1,0:T(8,128)(2,1)S(1)}, bf16[128,2048]{1,0:T(8,128)(2,1)S(1)}, u32[]{:S(2)}, u32[]{:S(2)}) %collective-permute-start.48) | collective-permute-done | bytes 524320 | tf_op jit(solution)/shard_map/scatter_g_ffn_in_1/ppermute | solution.py:274
  310.8 11.5 %collective-permute-done.53 = bf16[128,2048]{1,0:T(8,128)(2,1)} collective-permute-done((bf16[128,2048]{1,0:T(8,128)(2,1)}, bf16[128,2048]{1,0:T(8,128)(2,1)}, u32[]{:S(2)}, u32[]{:S(2)}) %collective-permute-start.53) | collective-permute-done | bytes 524320 | tf_op jit(solution)/shard_map/scatter_g_ffn_in_3/ppermute | solution.py:274
  327.2 13.8 %collective-permute-done.54.refs_0_ = bf16[128,2048]{1,0:T(8,128)(2,1)S(1)} collective-permute-done((bf16[128,2048]{1,0:T(8,128)(2,1)S(1)}, bf16[128,2048]{1,0:T(8,128)(2,1)S(1)}, u32[]{:S(2)}, u32[]{:S(2)}) %collective-permute-start.54) | collective-permute-done | bytes 524320 | tf_op jit(solution)/shard_map/gather_g_attn_1/ppermute | solution.py:274
  374.1 7.3 %collective-permute-done.60 = bf16[4,128,1024]{2,1,0:T(8,128)(2,1)S(1)} collective-permute-done((bf16[4,128,1024]{2,1,0:T(8,128)(2,1)S(1)}, bf16[4,128,1024]{2,1,0:T(8,128)(2,1)S(1)}, u32[]{:S(2)}, u32[]{:S(2)}) %collective-permute-start.60) | collective-permute-done | bytes 1048608 | tf_op jit(solution)/shard_map/sum_up_second/ppermute | solution.py:274
  385.1 7.0 %convolution_convert_fusion = bf16[1024,2048]{1,0:T(8,128)(2,1)S(1)} fusion(bf16[1024,1024]{1,0:T(8,128)(2,1)S(1)} %pad_maximum_fusion.7, bf16[1024,2048]{1,0:T(8,128)(2,1)} %constant_dynamic-update-slice_fusion.8), kind=kOutput, calls=%fused_computation.15 | convolution fusion | flops 4297064448 | bytes 10485760 | tf_op jit(solution)/shard_map/dot_general | solution.py:27
  413.8 19.7 %collective-permute-done.62 = bf16[128,2048]{1,0:T(8,128)(2,1)S(1)} collective-permute-done((bf16[128,2048]{1,0:T(8,128)(2,1)S(1)}, bf16[128,2048]{1,0:T(8,128)(2,1)S(1)}, u32[]{:S(2)}, u32[]{:S(2)}) %collective-permute-start.62) | collective-permute-done | bytes 524320 | tf_op jit(solution)/shard_map/sum_glu_along_z_2/ppermute | solution.py:274
  433.5 10.3 %collective-permute-start.75 = (bf16[128,2048]{1,0:T(8,128)(2,1)S(1)}, bf16[128,2048]{1,0:T(8,128)(2,1)S(1)}, u32[]{:S(2)}, u32[]{:S(2)}) collective-permute-start(bf16[128,2048]{1,0:T(8,128)(2,1)S(1)} %add_convert_fusion.6), channel_id=1, source_target_pairs={{0,8},{1,9},{2,10},{3,11},{4,12},{5,13},{6,14},{7,15},{8,16},{9,17... | collective-permute-start | bytes 1572872 | tf_op jit(solution)/shard_map/scatter_g_attn_in_1/ppermute | solution.py:274
  446.6 11.8 %collective-permute-done.75 = bf16[128,2048]{1,0:T(8,128)(2,1)S(1)} collective-permute-done((bf16[128,2048]{1,0:T(8,128)(2,1)S(1)}, bf16[128,2048]{1,0:T(8,128)(2,1)S(1)}, u32[]{:S(2)}, u32[]{:S(2)}) %collective-permute-start.75) | collective-permute-done | bytes 524320 | tf_op jit(solution)/shard_map/scatter_g_attn_in_1/ppermute | solution.py:274
  459.4 10.8 %collective-permute-done.78 = bf16[4,2,128,384]{3,2,0,1:T(8,128)(2,1)S(1)} collective-permute-done((bf16[4,2,128,384]{3,2,0,1:T(8,128)(2,1)S(1)}, bf16[4,2,128,384]{3,2,0,1:T(8,128)(2,1)S(1)}, u32[]{:S(2)}, u32[]{:S(2)}) %collective-permute-start.78) | collective-permute-done | bytes 786464 | tf_op jit(solution)/shard_map/sum_qkv_first/ppermute | solution.py:274
  496.3 11.9 %collective-permute-done.81 = bf16[128,2048]{1,0:T(8,128)(2,1)S(1)} collective-permute-done((bf16[128,2048]{1,0:T(8,128)(2,1)S(1)}, bf16[128,2048]{1,0:T(8,128)(2,1)S(1)}, u32[]{:S(2)}, u32[]{:S(2)}) %collective-permute-start.81) | collective-permute-done | bytes 524320 | tf_op jit(solution)/shard_map/scatter_g_attn_in_3/ppermute | solution.py:274
  520.5 11.0 %collective-permute-done.82 = bf16[128,2048]{1,0:T(8,128)(2,1)S(1)} collective-permute-done((bf16[128,2048]{1,0:T(8,128)(2,1)S(1)}, bf16[128,2048]{1,0:T(8,128)(2,1)S(1)}, u32[]{:S(2)}, u32[]{:S(2)}) %collective-permute-start.82) | collective-permute-done | bytes 524320 | tf_op jit(solution)/shard_map/scatter_ffn_branch_1/ppermute | solution.py:274
  534.0 8.7 %collective-permute-done.84 = bf16[128,2048]{1,0:T(8,128)(2,1)S(1)} collective-permute-done((bf16[128,2048]{1,0:T(8,128)(2,1)S(1)}, bf16[128,2048]{1,0:T(8,128)(2,1)S(1)}, u32[]{:S(2)}, u32[]{:S(2)}) %collective-permute-start.84) | collective-permute-done | bytes 524320 | tf_op jit(solution)/shard_map/scatter_ffn_branch_2/ppermute | solution.py:274
  555.4 6.8 %collective-permute-done.85 = bf16[4,128,384]{2,1,0:T(8,128)(2,1)} collective-permute-done((bf16[4,128,384]{2,1,0:T(8,128)(2,1)S(1)}, bf16[4,128,384]{2,1,0:T(8,128)(2,1)}, u32[]{:S(2)}, u32[]{:S(2)}) %collective-permute-start.85) | collective-permute-done | bytes 393248 | tf_op jit(solution)/shard_map/sum_qkv_second/ppermute | solution.py:274
  583.2 8.6 %place_blocks.8 = (f32[256,8192]{1,0:T(8,128)}, f32[256,8192]{1,0:T(8,128)}) custom-call(s32[32]{0:T(128)S(1)} %reshape.232.row_ref, s32[32]{0:T(128)S(1)} %reshape.233.column_ref, bf16[4,128,2048]{2,1,0:T(8,128)(2,1)S(1)} %pad_maximum_fusion.6.refs_0_, bf16[4,128,2048]{2,1,0:T(8,128)(2,1)} %collective-permute-done.80.refs_1_, ...), custom_call_target="tpu_custom_call" | custom-call | flops 1 | bytes 1 | tf_op jit(solution)/shard_map/place_blocks/pallas_call | solution.py:250
  (591 shorter events, 387.6 us)
Async XLA Ops:
  14.2 45.5 %collective-permute-start.8 = (bf16[128,2048]{1,0:T(8,128)(2,1)}, bf16[128,2048]{1,0:T(8,128)(2,1)}, u32[]{:S(2)}, u32[]{:S(2)}) collective-permute-start(bf16[128,2048]{1,0:T(8,128)(2,1)} %constant_dynamic-slice_fusion.4), channel_id=1, source_target_pairs={{1,5},{3,7},{5,1},{7,3},{9,13},{11,15},{13,9},{15,11},{17,21},{19,... | collective-permute-start | bytes 1572872 | tf_op jit(solution)/shard_map/w_out_across_y/ppermute | solution.py:274
  24.3 38.9 %collective-permute-start.11 = (bf16[128,2048]{1,0:T(8,128)(2,1)}, bf16[128,2048]{1,0:T(8,128)(2,1)}, u32[]{:S(2)}, u32[]{:S(2)}) collective-permute-start(bf16[128,2048]{1,0:T(8,128)(2,1)} %pad_maximum_fusion.11), channel_id=1, source_target_pairs={{0,8},{1,9},{2,10},{3,11},{4,12},{5,13},{6,14},{7,15},{8,16},{9,17... | collective-permute-start | bytes 1572872 | tf_op jit(solution)/shard_map/w_glu_along_z/ppermute | solution.py:274
  30.4 32.8 %collective-permute-start.12 = (bf16[128,2048]{1,0:T(8,128)(2,1)}, bf16[128,2048]{1,0:T(8,128)(2,1)}, u32[]{:S(2)}, u32[]{:S(2)}) collective-permute-start(bf16[128,2048]{1,0:T(8,128)(2,1)} %pad_maximum_fusion.12), channel_id=1, source_target_pairs={{0,16},{1,17},{2,18},{3,19},{4,20},{5,21},{6,22},{7,23},{8,24},{9,... | collective-permute-start | bytes 1572872 | tf_op jit(solution)/shard_map/w_glu_along_z/ppermute | solution.py:274
  35.3 27.9 %collective-permute-start.13 = (bf16[128,2048]{1,0:T(8,128)(2,1)}, bf16[128,2048]{1,0:T(8,128)(2,1)}, u32[]{:S(2)}, u32[]{:S(2)}) collective-permute-start(bf16[128,2048]{1,0:T(8,128)(2,1)} %pad_maximum_fusion.13), channel_id=1, source_target_pairs={{0,24},{1,25},{2,26},{3,27},{4,28},{5,29},{6,30},{7,31},{8,0},{9,1... | collective-permute-start | bytes 1572872 | tf_op jit(solution)/shard_map/w_glu_along_z/ppermute | solution.py:274
  77.8 49.9 %collective-permute-start.20 = (bf16[4,128,2048]{2,1,0:T(8,128)(2,1)}, bf16[4,128,2048]{2,1,0:T(8,128)(2,1)}, u32[]{:S(2)}, u32[]{:S(2)}) collective-permute-start(bf16[4,128,2048]{2,1,0:T(8,128)(2,1)} %pad_maximum_fusion.3.refs_0_), channel_id=1, source_target_pairs={{0,5},{1,4},{2,7},{3,6},{4,1},{5,0},{6,3},{7,2},{8,13},{9,12},{10,... | collective-permute-start | bytes 6291464 | tf_op jit(solution)/shard_map/w_glu_across/ppermute | solution.py:274
  81.7 46.6 %collective-permute-start.19 = (bf16[4,128,2048]{2,1,0:T(8,128)(2,1)}, bf16[4,128,2048]{2,1,0:T(8,128)(2,1)}, u32[]{:S(2)}, u32[]{:S(2)}) collective-permute-start(bf16[4,128,2048]{2,1,0:T(8,128)(2,1)} %pad_maximum_fusion.3.refs_0_), channel_id=1, source_target_pairs={{0,2},{1,3},{2,0},{3,1},{4,6},{5,7},{6,4},{7,5},{8,10},{9,11},{10,... | collective-permute-start | bytes 6291464 | tf_op jit(solution)/shard_map/w_glu_across/ppermute | solution.py:274
  150.4 28.5 %collective-permute-start.10 = (bf16[128,2048]{1,0:T(8,128)(2,1)}, bf16[128,2048]{1,0:T(8,128)(2,1)}, u32[]{:S(2)}, u32[]{:S(2)}) collective-permute-start(bf16[128,2048]{1,0:T(8,128)(2,1)} %get-tuple-element.118), channel_id=1, source_target_pairs={{0,1},{1,0},{2,3},{3,2},{4,5},{5,4},{6,7},{7,6},{8,9},{9,8},{10,11... | collective-permute-start | bytes 1572872 | tf_op jit(solution)/shard_map/scatter_attn_branch_3/ppermute | solution.py:274
  151.0 32.7 %collective-permute-start.16 = (bf16[512,2048]{1,0:T(8,128)(2,1)}, bf16[512,2048]{1,0:T(8,128)(2,1)}, u32[]{:S(2)}, u32[]{:S(2)}) collective-permute-start(bf16[512,2048]{1,0:T(8,128)(2,1)} %collective-permute-done.14), channel_id=1, source_target_pairs={{1,3},{3,1},{5,7},{7,5},{9,11},{11,9},{13,15},{15,13},{17,19},{19,... | collective-permute-start | bytes 6291464 | tf_op jit(solution)/shard_map/w_down_across_x/ppermute | solution.py:274
  168.2 33.9 %collective-permute-start.39 = (bf16[128,2048]{1,0:T(8,128)(2,1)}, bf16[128,2048]{1,0:T(8,128)(2,1)S(1)}, u32[]{:S(2)}, u32[]{:S(2)}) collective-permute-start(bf16[128,2048]{1,0:T(8,128)(2,1)} %param.27), channel_id=1, source_target_pairs={{0,1},{1,0},{2,3},{3,2},{4,5},{5,4},{6,7},{7,6},{8,9},{9,8},{10,11... | collective-permute-start | bytes 1572872 | tf_op jit(solution)/shard_map/gather_d_out_0/ppermute | solution.py:274
  207.9 102.9 %collective-permute-start.50 = (bf16[128,2048]{1,0:T(8,128)(2,1)}, bf16[128,2048]{1,0:T(8,128)(2,1)}, u32[]{:S(2)}, u32[]{:S(2)}) collective-permute-start(bf16[128,2048]{1,0:T(8,128)(2,1)} %slice.223), channel_id=1, source_target_pairs={{0,1},{1,0},{2,3},{3,2},{4,5},{5,4},{6,7},{7,6},{8,9},{9,8},{10,11... | collective-permute-start | bytes 1572872 | tf_op jit(solution)/shard_map/scatter_g_ffn_in_3/ppermute | solution.py:274
  309.4 47.2 %collective-permute-start.58 = (bf16[4,2,128,1024]{3,2,0,1:T(8,128)(2,1)}, bf16[4,2,128,1024]{3,2,0,1:T(8,128)(2,1)S(1)}, u32[]{:S(2)}, u32[]{:S(2)}) collective-permute-start(bf16[4,2,128,1024]{3,2,0,1:T(8,128)(2,1)} %copy_bitcast_fusion), channel_id=1, source_target_pairs={{0,2},{1,3},{2,0},{3,1},{4,6},{5,7},{6,4},{7,5},{8,10},{9,11},{10,... | collective-permute-start | bytes 6291464 | tf_op jit(solution)/shard_map/sum_up_first/ppermute | solution.py:274
  310.8 47.4 %collective-permute-start.49 = (bf16[4,2,128,1024]{3,2,0,1:T(8,128)(2,1)}, bf16[4,2,128,1024]{3,2,0,1:T(8,128)(2,1)S(1)}, u32[]{:S(2)}, u32[]{:S(2)}) collective-permute-start(bf16[4,2,128,1024]{3,2,0,1:T(8,128)(2,1)} %copy_bitcast_fusion.1), channel_id=1, source_target_pairs={{0,5},{1,4},{2,7},{3,6},{4,1},{5,0},{6,3},{7,2},{8,13},{9,12},{10,... | collective-permute-start | bytes 6291464 | tf_op jit(solution)/shard_map/sum_gate_first/ppermute | solution.py:274
  373.4 71.3 %collective-permute-start.73 = (bf16[128,2048]{1,0:T(8,128)(2,1)S(1)}, bf16[128,2048]{1,0:T(8,128)(2,1)S(1)}, u32[]{:S(2)}, u32[]{:S(2)}) collective-permute-start(bf16[128,2048]{1,0:T(8,128)(2,1)S(1)} %get-tuple-element.151), channel_id=1, source_target_pairs={{0,1},{1,0},{2,3},{3,2},{4,5},{5,4},{6,7},{7,6},{8,9},{9,8},{10,11... | collective-permute-start | bytes 1572872 | tf_op jit(solution)/shard_map/scatter_g_attn_in_1/ppermute | solution.py:274
  392.1 82.6 %collective-permute-start.77 = (bf16[2,512,2048]{2,1,0:T(8,128)(2,1)S(1)}, bf16[2,512,2048]{2,1,0:T(8,128)(2,1)S(1)}, u32[]{:S(2)}, u32[]{:S(2)}) collective-permute-start(bf16[2,512,2048]{2,1,0:T(8,128)(2,1)S(1)} %bitcast.197), channel_id=1, source_target_pairs={{1,4},{3,6},{5,0},{7,2},{9,12},{11,14},{13,8},{15,10},{17,20},{19,... | collective-permute-start | bytes 12582920 | tf_op jit(solution)/shard_map/sum_down_first/ppermute | solution.py:274
  398.0 35.5 %collective-permute-start.62 = (bf16[128,2048]{1,0:T(8,128)(2,1)S(1)}, bf16[128,2048]{1,0:T(8,128)(2,1)S(1)}, u32[]{:S(2)}, u32[]{:S(2)}) collective-permute-start(bf16[128,2048]{1,0:T(8,128)(2,1)S(1)} %pad_maximum_fusion.15), channel_id=1, source_target_pairs={{0,16},{1,17},{2,18},{3,19},{4,20},{5,21},{6,22},{7,23},{8,24},{9,... | collective-permute-start | bytes 1572872 | tf_op jit(solution)/shard_map/sum_glu_along_z_2/ppermute | solution.py:274
  409.6 34.2 %collective-permute-start.63 = (bf16[128,2048]{1,0:T(8,128)(2,1)S(1)}, bf16[128,2048]{1,0:T(8,128)(2,1)S(1)}, u32[]{:S(2)}, u32[]{:S(2)}) collective-permute-start(bf16[128,2048]{1,0:T(8,128)(2,1)S(1)} %pad_maximum_fusion.16), channel_id=1, source_target_pairs={{0,24},{1,25},{2,26},{3,27},{4,28},{5,29},{6,30},{7,31},{8,0},{9,1... | collective-permute-start | bytes 1572872 | tf_op jit(solution)/shard_map/sum_glu_along_z_3/ppermute | solution.py:274
  412.5 57.7 %collective-permute-start.79 = (bf16[2,128,2048]{2,1,0:T(8,128)(2,1)S(1)}, bf16[2,128,2048]{2,1,0:T(8,128)(2,1)S(1)}, u32[]{:S(2)}, u32[]{:S(2)}) collective-permute-start(bf16[2,128,2048]{2,1,0:T(8,128)(2,1)S(1)} %bitcast.209), channel_id=1, source_target_pairs={{1,4},{3,6},{5,0},{7,2},{9,12},{11,14},{13,8},{15,10},{17,20},{19,... | collective-permute-start | bytes 3145736 | tf_op jit(solution)/shard_map/sum_out_first/ppermute | solution.py:274
  444.0 48.0 %collective-permute-start.80 = (bf16[4,128,2048]{2,1,0:T(8,128)(2,1)S(1)}, bf16[4,128,2048]{2,1,0:T(8,128)(2,1)}, u32[]{:S(2)}, u32[]{:S(2)}) collective-permute-start(bf16[4,128,2048]{2,1,0:T(8,128)(2,1)S(1)} %pad_maximum_fusion.6.refs_0_), channel_id=1, source_target_pairs={{0,2},{1,3},{2,0},{3,1},{4,6},{5,7},{6,4},{7,5},{8,10},{9,11},{10,... | collective-permute-start | bytes 6291464 | tf_op jit(solution)/shard_map/sum_glu_across/ppermute | solution.py:274
  458.3 38.0 %collective-permute-start.69 = (bf16[128,2048]{1,0:T(8,128)(2,1)S(1)}, bf16[128,2048]{1,0:T(8,128)(2,1)S(1)}, u32[]{:S(2)}, u32[]{:S(2)}) collective-permute-start(bf16[128,2048]{1,0:T(8,128)(2,1)S(1)} %get-tuple-element.161), channel_id=1, source_target_pairs={{0,1},{1,0},{2,3},{3,2},{4,5},{5,4},{6,7},{7,6},{8,9},{9,8},{10,11... | collective-permute-start | bytes 1572872 | tf_op jit(solution)/shard_map/scatter_g_attn_in_3/ppermute | solution.py:274
  475.5 39.6 %collective-permute-start.83 = (bf16[512,2048]{1,0:T(8,128)(2,1)S(1)}, bf16[512,2048]{1,0:T(8,128)(2,1)S(1)}, u32[]{:S(2)}, u32[]{:S(2)}) collective-permute-start(bf16[512,2048]{1,0:T(8,128)(2,1)S(1)} %fusion.12), channel_id=1, source_target_pairs={{0,2},{2,0},{4,6},{6,4},{8,10},{10,8},{12,14},{14,12},{16,18},{18,... | collective-permute-start | bytes 6291464 | tf_op jit(solution)/shard_map/sum_down_second/ppermute | solution.py:274
  516.3 27.9 %collective-permute-start.98 = (bf16[512,2048]{1,0:T(8,128)(2,1)S(1)}, bf16[512,2048]{1,0:T(8,128)(2,1)S(1)}, u32[]{:S(2)}, u32[]{:S(2)}) collective-permute-start(bf16[512,2048]{1,0:T(8,128)(2,1)S(1)} %fusion.8), channel_id=1, source_target_pairs={{0,2},{2,0},{4,6},{6,4},{8,10},{10,8},{12,14},{14,12},{16,18},{18,... | collective-permute-start | bytes 6291464 | tf_op jit(solution)/shard_map/sum_down_third/ppermute | solution.py:274
  547.0 59.8 %collective-permute-start.99 = (bf16[2,512,2048]{2,1,0:T(8,128)(2,1)}, bf16[2,512,2048]{2,1,0:T(8,128)(2,1)}, u32[]{:S(2)}, u32[]{:S(2)}) collective-permute-start(bf16[2,512,2048]{2,1,0:T(8,128)(2,1)} %pad_maximum_fusion.2), channel_id=1, source_target_pairs={{0,1},{2,3},{4,5},{6,7},{8,9},{10,11},{12,13},{14,15},{16,17},{18,... | collective-permute-start | bytes 12582920 | tf_op jit(solution)/shard_map/sum_down_last/ppermute | solution.py:274
  550.3 31.0 %collective-permute-start.88 = (bf16[4,128,2048]{2,1,0:T(8,128)(2,1)S(1)}, bf16[4,128,2048]{2,1,0:T(8,128)(2,1)}, u32[]{:S(2)}, u32[]{:S(2)}) collective-permute-start(bf16[4,128,2048]{2,1,0:T(8,128)(2,1)S(1)} %pad_maximum_fusion.6.refs_0_), channel_id=1, source_target_pairs={{0,1},{1,0},{2,3},{3,2},{4,5},{5,4},{6,7},{7,6},{8,9},{9,8},{10,11... | collective-permute-start | bytes 6291464 | tf_op jit(solution)/shard_map/sum_glu_core/ppermute | solution.py:274
  550.3 32.2 %collective-permute-start.89 = (bf16[4,128,2048]{2,1,0:T(8,128)(2,1)}, bf16[4,128,2048]{2,1,0:T(8,128)(2,1)}, u32[]{:S(2)}, u32[]{:S(2)}) collective-permute-start(bf16[4,128,2048]{2,1,0:T(8,128)(2,1)} %collective-permute-done.80.refs_1_), channel_id=1, source_target_pairs={{0,1},{1,0},{2,3},{3,2},{4,5},{5,4},{6,7},{7,6},{8,9},{9,8},{10,11... | collective-permute-start | bytes 6291464 | tf_op jit(solution)/shard_map/sum_glu_core/ppermute | solution.py:274
  (183 other events, 2616.5 us)
